TPU v7x, 32 devices: a whole 2x2x4 slice. The times are simulated.
32 devices in a mesh: az: 16 (over z, y, x), grp: 2 (over core).
Axes of the slice: x: 2, y: 2, z: 4, core: 2. Of those that a mesh axis runs over, the one named last changes fastest.
Arguments:
- features: bfloat16 [256, 64, 128], P(None, 'az', 'grp'), may hold values from -6 to 6
- cotangent: bfloat16 [256, 64, 128], P(None, 'az', 'grp'), may hold values from -6 to 6
- w_first: bfloat16 [256, 6912], P('grp'), may hold values from -0.078125 to 0.078125
- w_second: bfloat16 [256, 6912], P('grp'), may hold values from -0.078125 to 0.078125
Outputs:
- flow_out: bfloat16 [256, 64, 128], P(None, 'az', 'grp')
- grad_first: float32 [256, 6912], P('grp')
- grad_second: float32 [256, 6912], P('grp')
All inputs are finite; a program needn't handle non-finite values.
Results may differ from a plain program's by a relative error of at most 0.01.
Values may be sent and summed in bfloat16 or wider, within the bound.
No kernel may reach another device: no remote copies, remote signals or barrier semaphores. Data moves between devices by JAX's collectives and lax.ppermute only.
A program may use at most 128 MiB of HBM per device.

v0:
```python
import math

import jax
import jax.numpy as jnp
from jax import lax
from jax.sharding import PartitionSpec as P

RAD_DEV = 8
AXIAL = 8


def with_halo(cells, sides, width, closed):
    for axis, dim in sides:
        count = lax.axis_size(axis)
        ends = count if closed else count - 1
        head = lax.slice_in_dim(cells, 0, width, axis=dim)
        tail = lax.slice_in_dim(cells, cells.shape[dim] - width, cells.shape[dim], axis=dim)
        cells = jnp.concatenate(
            [
                lax.ppermute(tail, axis, [(i, (i + 1) % count) for i in range(ends)]),
                cells,
                lax.ppermute(head, axis, [((i + 1) % count, i) for i in range(ends)]),
            ],
            axis=dim,
        )
    return cells


def silu_slope(values):
    sigma = jax.nn.sigmoid(values)
    return sigma * (1.0 + values * (1.0 - sigma))


def patches(padded, flipped):
    channels, span_az, span_rad, span_ax = padded.shape
    inner_az = span_az - 2
    inner_rad = span_rad - 2
    inner_ax = span_ax - 2
    stacked = []
    for along_az in range(3):
        for along_rad in range(3):
            for along_ax in range(3):
                if flipped:
                    first_az, first_rad, first_ax = (2 - along_az, 2 - along_rad, 2 - along_ax)
                else:
                    first_az, first_rad, first_ax = (along_az, along_rad, along_ax)
                stacked.append(
                    padded[
                        :,
                        first_az : first_az + inner_az,
                        first_rad : first_rad + inner_rad,
                        first_ax : first_ax + inner_ax,
                    ]
                )
    return jnp.stack(stacked, axis=0).reshape(27 * channels, inner_az * inner_rad * inner_ax)


def az_rim(field):
    return with_halo(field, (("az", 1),), 1, True)


def radial_rim(field):
    return with_halo(field, (("grp", 2),), 1, False)


def axial_pad(field):
    return jnp.pad(field, ((0, 0), (0, 0), (0, 0), (1, 1)))


def flip_weight(weight):
    rows_here = weight.shape[0]
    channels = weight.shape[1] // 27
    return (
        weight.reshape(rows_here, 27, channels).transpose(2, 1, 0).reshape(channels, 27 * rows_here)
    )


def contract_cells(left, right):
    return lax.dot_general(
        left, right, (((1,), (1,)), ((), ())), preferred_element_type=jnp.float32
    )


def rows_forward(weight, columns):
    return jnp.dot(
        lax.all_gather(weight, "grp", axis=0, tiled=True),
        columns,
        preferred_element_type=jnp.float32,
    )


def group_grad(source, columns):
    return lax.psum_scatter(
        contract_cells(source, columns).astype(jnp.bfloat16), "grp", scatter_dimension=0, tiled=True
    ).astype(jnp.float32)


def local(features, cotangent, w_first, w_second):
    channels, az_cells, flat_cells = features.shape
    groups = lax.axis_size("grp")
    cell_count = az_cells * RAD_DEV * AXIAL
    factor = 1.0 / math.sqrt(az_cells * lax.axis_size("az") * RAD_DEV * groups * AXIAL)
    field_in = features.reshape(channels, az_cells, RAD_DEV, AXIAL)
    field_cot = cotangent.reshape(channels, az_cells, RAD_DEV, AXIAL)
    input_columns = patches(axial_pad(radial_rim(az_rim(field_in))), False)
    pre_first = rows_forward(w_first, input_columns).reshape(channels, az_cells, flat_cells)
    hidden = jax.nn.silu(pre_first).astype(jnp.bfloat16)
    hidden_columns = patches(
        axial_pad(radial_rim(az_rim(hidden.reshape(channels, az_cells, RAD_DEV, AXIAL)))), False
    )
    second = rows_forward(w_second, hidden_columns).reshape(channels, az_cells, flat_cells)
    flow_out = (features.astype(jnp.float32) + second).astype(jnp.bfloat16)
    cot_columns = patches(axial_pad(radial_rim(az_rim(field_cot))), True).reshape(
        27, channels, cell_count
    )
    weight_piece = lax.all_gather(w_second, "grp", axis=0, tiled=True)
    piece_rows = weight_piece.shape[0]
    turned = flip_weight(weight_piece)
    picked = cot_columns.reshape(27 * piece_rows, cell_count)
    back_grad = jnp.dot(turned, picked, preferred_element_type=jnp.float32)
    slope = (back_grad * silu_slope(pre_first.reshape(channels, cell_count))).astype(jnp.bfloat16)
    grad_second = group_grad(cotangent.reshape(channels, cell_count), hidden_columns)
    grad_first = group_grad(slope, input_columns)
    grad_first, grad_second = lax.psum((grad_first, grad_second), "az")
    return (flow_out, grad_first * factor, grad_second * factor)


def solution(mesh):
    in_specs = (P(None, "az", "grp"), P(None, "az", "grp"), P("grp", None), P("grp", None))
    out_specs = (P(None, "az", "grp"), P("grp", None), P("grp", None))
    return jax.shard_map(local, mesh=mesh, in_specs=in_specs, out_specs=out_specs, check_vma=False)
```

profile of v0, /device:TPU:10, one launch (start us, length us, event | category | flops | bytes accessed | tf_op | source)
XLA Modules:
  0.0 407.9 jit_solution(12982529073874746874)
XLA Ops:
  7.2 0.0 copy-start.2
  7.2 0.0 copy-start
  7.2 0.0 all-gather.5.cloned.1.call-start
  7.2 3.9 copy.92
  11.1 0.0 all-gather.5.cloned.1.call-update
  11.1 0.0 all-gather.3.cloned.1.call-start
  11.2 0.0 copy-done.2
  11.2 0.6 collective-permute-start.1
  11.8 2.4 collective-permute-start
  14.2 0.0 copy-done
  14.2 0.1 collective-permute-start.9
  14.3 2.9 collective-permute-start.8
  17.2 0.0 all-gather.3.cloned.1.call-update
  17.2 0.0 reduce-scatter.3.cloned.1.call-start
  17.3 0.0 collective-permute-done.1
  17.3 0.0 collective-permute-done
  17.3 1.3 collective-permute-start.3
  18.6 3.0 collective-permute-start.2
  21.6 0.0 collective-permute-done.9
  21.6 0.0 collective-permute-done.8
  21.7 1.3 collective-permute-start.11
  23.0 3.0 collective-permute-start.10
  26.0 0.0 collective-permute-done.3
  26.0 0.0 collective-permute-done.2
  26.0 0.3 fusion.13
  27.2 2.0 copy.97
  29.2 0.0 collective-permute-done.11
  29.2 0.0 collective-permute-done.10
  29.2 0.3 select_maximum_fusion
  30.3 0.2 copy.99
  30.5 0.0 all-gather.5.cloned.1.call-done
  30.6 5.8 %copy.94 = bf16[256,27,256]{0,2,1:T(8,128)(2,1)} copy(bf16[256,27,256]{2,0,1:T(8,128)(2,1)} %bitcast.408) | data formatting | bytes 7077888 | tf_op jit(solution)/shard_map/transpose | solution.py:74
  36.4 4.0 all-gather.3.cloned.1.call-done
  40.3 4.9 %fusion.37 = f32[256,256]{1,0:T(8,128)} fusion(bf16[6912,256]{0,1:T(8,128)(2,1)} %bitcast.389, bf16[256,6912]{1,0:T(8,128)(2,1)} %all-gather.3.cloned.1.call-done), kind=kOutput, calls=%fused_computation.227 | convolution fusion | flops 905969664 | bytes 7340032 | tf_op jit(solution)/shard_map/dot_general | solution.py:85
  45.2 8.9 %convolution_convert_fusion.1 = bf16[256,6912]{1,0:T(8,128)(2,1)} fusion(bf16[6912,256]{0,1:T(8,128)(2,1)} %bitcast.390, bf16[6912,256]{0,1:T(8,128)(2,1)S(1)} %bitcast.386, bf16[256,6912]{0,1:T(8,128)(2,1)} %bitcast.391, f32[256,256]{1,0:T(8,128)} %fusion.37), kind=kOutput, calls=%fused_computation.1 | convolution fusion | flops 1814298624 | bytes 14417920 | tf_op jit(solution)/shard_map/dot_general | solution.py:79
  54.2 0.0 copy-start.4
  54.2 0.0 reduce-scatter.3.cloned.1.call-update
  54.2 0.0 reduce-scatter.5.cloned.1.call-start
  54.2 0.9 copy-done.4
  55.1 0.1 multiply_convert_fusion.1
  55.2 0.6 collective-permute-start.5
  55.8 2.4 collective-permute-start.4
  58.2 1.9 collective-permute-done.5
  60.1 0.3 collective-permute-done.4
  60.4 1.3 collective-permute-start.7
  61.7 3.0 collective-permute-start.6
  64.8 0.0 collective-permute-done.7
  64.8 0.8 collective-permute-done.6
  65.6 0.3 select_maximum_fusion.4
  66.3 0.1 constant_dynamic-update-slice_fusion.40
  66.8 0.0 copy-start.1
  66.8 0.2 copy.98
  67.0 0.7 copy-done.1
  67.7 2.9 fusion
  70.6 0.0 reduce-scatter.5.cloned.1.call-update
  70.7 0.0 copy-start.3
  70.7 3.1 fusion.38
  73.8 0.0 copy-done.3
  73.8 0.7 add_convert_fusion
  74.5 0.0 reduce-scatter.3.cloned.1.call-done
  74.5 13.3 %reduce-scatter.5.cloned.1.call-done = bf16[128,6912]{1,0:T(8,128)(2,1)} async-done(((bf16[256,6912]{1,0:T(8,128)(2,1)}), bf16[128,6912]{1,0:T(8,128)(2,1)}) %reduce-scatter.5.cloned.1.call-update) | async-done | bytes 1769488 | tf_op jit(solution)/shard_map/reduce_scatter | solution.py:93
  87.8 308.0 %all-reduce.5 = (f32[128,6912]{1,0:T(8,128)S(1)}, f32[128,6912]{1,0:T(8,128)}) all-reduce(bf16[128,6912]{1,0:T(8,128)(2,1)} %reduce-scatter.3.cloned.1.call-done, bf16[128,6912]{1,0:T(8,128)(2,1)} %reduce-scatter.5.cloned.1.call-done), channel_id=1, replica_groups=mesh['az'=16,'grp'=2] {'az'}, use_global_device_ids=true, to_apply=%region_1.2 | all-reduce | flops 1769472 | bytes 10616832 | tf_op jit(solution)/shard_map/psum | solution.py:124
  395.8 5.6 %broadcast_multiply_fusion = (f32[128,6912]{1,0:T(8,128)}, f32[128,6912]{1,0:T(8,128)}) fusion(f32[128,6912]{1,0:T(8,128)} %get-tuple-element.4, f32[128,6912]{1,0:T(8,128)S(1)} %get-tuple-element.3), kind=kLoop, calls=%fused_computation.3 | loop fusion | flops 1769472 | bytes 14155776 | tf_op jit(solution)/shard_map/mul | solution.py:125
  (89 shorter events, 1.9 us)
Async XLA Ops:
  7.2 4.0 copy-start.2
  7.2 7.0 %copy-start = (bf16[256,4,64]{0,2,1:T(8,128)(2,1)S(1)}, bf16[256,4,64]{0,2,1:T(8,128)(2,1)}, u32[]{:S(2)}) copy-start(bf16[256,4,64]{0,2,1:T(8,128)(2,1)} %param.5) | copy-start | bytes 393220
  7.2 23.4 %all-gather.5.cloned.1.call-start = ((), (), s32[]{:S(2)}) async-start(), calls=%async_computation.3 | async-start | bytes 5308416 | tf_op jit(solution)/shard_map/all_gather | solution.py:86
  11.1 29.2 %all-gather.3.cloned.1.call-start = ((), (), s32[]{:S(2)}) async-start(), calls=%async_computation.2 | async-start | bytes 5308416 | tf_op jit(solution)/shard_map/all_gather | solution.py:86
  11.2 6.0 %collective-permute-start.1 = (bf16[256,1,8,8]{0,3,2,1:T(8,128)(2,1)S(1)}, bf16[256,1,8,8]{0,3,2,1:T(8,128)(2,1)S(1)}, u32[]{:S(2)}, u32[]{:S(2)}) collective-permute-start(bf16[256,1,8,8]{0,3,2,1:T(8,128)(2,1)S(1)} %get-tuple-element.22), channel_id=1, source_target_pairs={{2,0},{4,2},{6,4},{8,6},{10,8},{12,10},{14,12},{16,14},{18,16},{20... | collective-permute-start | bytes 98312 | tf_op jit(solution)/shard_map/ppermute | solution.py:22
  11.8 5.5 %collective-permute-start = (bf16[256,1,8,8]{0,3,2,1:T(8,128)(2,1)S(1)}, bf16[256,1,8,8]{0,3,2,1:T(8,128)(2,1)S(1)}, u32[]{:S(2)}, u32[]{:S(2)}) collective-permute-start(bf16[256,1,8,8]{0,3,2,1:T(8,128)(2,1)S(1)} %get-tuple-element.21), channel_id=1, source_target_pairs={{0,2},{2,4},{4,6},{6,8},{8,10},{10,12},{12,14},{14,16},{16,18},{18... | collective-permute-start | bytes 98312 | tf_op jit(solution)/shard_map/ppermute | solution.py:20
  14.2 7.4 %collective-permute-start.9 = (bf16[256,1,8,8]{0,3,2,1:T(8,128)(2,1)S(1)}, bf16[256,1,8,8]{0,3,2,1:T(8,128)(2,1)S(1)}, u32[]{:S(2)}, u32[]{:S(2)}) collective-permute-start(bf16[256,1,8,8]{0,3,2,1:T(8,128)(2,1)S(1)} %get-tuple-element.18), channel_id=1, source_target_pairs={{2,0},{4,2},{6,4},{8,6},{10,8},{12,10},{14,12},{16,14},{18,16},{20... | collective-permute-start | bytes 98312 | tf_op jit(solution)/shard_map/ppermute | solution.py:22
  14.3 7.4 %collective-permute-start.8 = (bf16[256,1,8,8]{0,3,2,1:T(8,128)(2,1)S(1)}, bf16[256,1,8,8]{0,3,2,1:T(8,128)(2,1)S(1)}, u32[]{:S(2)}, u32[]{:S(2)}) collective-permute-start(bf16[256,1,8,8]{0,3,2,1:T(8,128)(2,1)S(1)} %get-tuple-element.17), channel_id=1, source_target_pairs={{0,2},{2,4},{4,6},{6,8},{8,10},{10,12},{12,14},{14,16},{16,18},{18... | collective-permute-start | bytes 98312 | tf_op jit(solution)/shard_map/ppermute | solution.py:20
  17.2 57.3 %reduce-scatter.3.cloned.1.call-start = ((), (), s32[]{:S(2)}) async-start(), calls=%async_computation.4 | async-start | bytes 5308416 | tf_op jit(solution)/shard_map/reduce_scatter | solution.py:93
  17.3 8.7 %collective-permute-start.3 = (bf16[256,6,1,8]{0,3,2,1:T(8,128)(2,1)S(1)}, bf16[256,6,1,8]{0,3,2,1:T(8,128)(2,1)S(1)}, u32[]{:S(2)}, u32[]{:S(2)}) collective-permute-start(bf16[256,6,1,8]{0,3,2,1:T(8,128)(2,1)S(1)} %get-tuple-element.16), channel_id=1, source_target_pairs={{1,0},{3,2},{5,4},{7,6},{9,8},{11,10},{13,12},{15,14},{17,16},{19,... | collective-permute-start | bytes 73736 | tf_op jit(solution)/shard_map/ppermute | solution.py:22
  18.6 7.4 %collective-permute-start.2 = (bf16[256,6,1,8]{0,3,2,1:T(8,128)(2,1)S(1)}, bf16[256,6,1,8]{0,3,2,1:T(8,128)(2,1)S(1)}, u32[]{:S(2)}, u32[]{:S(2)}) collective-permute-start(bf16[256,6,1,8]{0,3,2,1:T(8,128)(2,1)S(1)} %get-tuple-element.15), channel_id=1, source_target_pairs={{0,1},{2,3},{4,5},{6,7},{8,9},{10,11},{12,13},{14,15},{16,17},{18,... | collective-permute-start | bytes 73736 | tf_op jit(solution)/shard_map/ppermute | solution.py:20
  21.7 7.5 %collective-permute-start.11 = (bf16[256,6,1,8]{0,3,2,1:T(8,128)(2,1)S(1)}, bf16[256,6,1,8]{0,3,2,1:T(8,128)(2,1)S(1)}, u32[]{:S(2)}, u32[]{:S(2)}) collective-permute-start(bf16[256,6,1,8]{0,3,2,1:T(8,128)(2,1)S(1)} %get-tuple-element.8), channel_id=1, source_target_pairs={{1,0},{3,2},{5,4},{7,6},{9,8},{11,10},{13,12},{15,14},{17,16},{19,... | collective-permute-start | bytes 73736 | tf_op jit(solution)/shard_map/ppermute | solution.py:22
  23.0 6.2 %collective-permute-start.10 = (bf16[256,6,1,8]{0,3,2,1:T(8,128)(2,1)S(1)}, bf16[256,6,1,8]{0,3,2,1:T(8,128)(2,1)S(1)}, u32[]{:S(2)}, u32[]{:S(2)}) collective-permute-start(bf16[256,6,1,8]{0,3,2,1:T(8,128)(2,1)S(1)} %get-tuple-element.7), channel_id=1, source_target_pairs={{0,1},{2,3},{4,5},{6,7},{8,9},{10,11},{12,13},{14,15},{16,17},{18,... | collective-permute-start | bytes 73736 | tf_op jit(solution)/shard_map/ppermute | solution.py:20
  54.2 0.9 copy-start.4
  54.2 33.6 %reduce-scatter.5.cloned.1.call-start = ((), (), s32[]{:S(2)}) async-start(), calls=%async_computation.5 | async-start | bytes 5308416 | tf_op jit(solution)/shard_map/reduce_scatter | solution.py:93
  55.2 4.9 %collective-permute-start.5 = (bf16[256,1,8,8]{0,3,2,1:T(8,128)(2,1)S(1)}, bf16[256,1,8,8]{0,3,2,1:T(8,128)(2,1)S(1)}, u32[]{:S(2)}, u32[]{:S(2)}) collective-permute-start(bf16[256,1,8,8]{0,3,2,1:T(8,128)(2,1)S(1)} %get-tuple-element.20), channel_id=1, source_target_pairs={{2,0},{4,2},{6,4},{8,6},{10,8},{12,10},{14,12},{16,14},{18,16},{20... | collective-permute-start | bytes 98312 | tf_op jit(solution)/shard_map/ppermute | solution.py:22
  55.8 4.6 %collective-permute-start.4 = (bf16[256,1,8,8]{0,3,2,1:T(8,128)(2,1)S(1)}, bf16[256,1,8,8]{0,3,2,1:T(8,128)(2,1)S(1)}, u32[]{:S(2)}, u32[]{:S(2)}) collective-permute-start(bf16[256,1,8,8]{0,3,2,1:T(8,128)(2,1)S(1)} %get-tuple-element.19), channel_id=1, source_target_pairs={{0,2},{2,4},{4,6},{6,8},{8,10},{10,12},{12,14},{14,16},{16,18},{18... | collective-permute-start | bytes 98312 | tf_op jit(solution)/shard_map/ppermute | solution.py:20
  60.4 4.3 %collective-permute-start.7 = (bf16[256,6,1,8]{0,3,2,1:T(8,128)(2,1)S(1)}, bf16[256,6,1,8]{0,3,2,1:T(8,128)(2,1)S(1)}, u32[]{:S(2)}, u32[]{:S(2)}) collective-permute-start(bf16[256,6,1,8]{0,3,2,1:T(8,128)(2,1)S(1)} %get-tuple-element.12), channel_id=1, source_target_pairs={{1,0},{3,2},{5,4},{7,6},{9,8},{11,10},{13,12},{15,14},{17,16},{19,... | collective-permute-start | bytes 73736 | tf_op jit(solution)/shard_map/ppermute | solution.py:22
  61.7 3.9 collective-permute-start.6
  66.8 0.9 copy-start.1
  70.7 3.1 copy-start.3
Sparse Core Ops, SparseCore 0:
  11.3 13.6 all-gather.4
  26.5 13.8 all-gather.2
  54.3 14.2 reduce-scatter.2
  71.4 16.3 reduce-scatter.4
where the time goes:
time: 408 us
  blocking collectives  308 us (75%)
  starting transfers between devices  22 us (5%)
  waiting for transfers between devices  20.4 us (5%)
  matrix products  19.9 us (5%)
  local copies, waits for them, and re-layouts  15.4 us (4%)
  between operations  14.7 us (4%)
  other arithmetic  7.46 us (2%)
    psum x1, blocking collectives, local(): grad_first, grad_second = lax.psum((grad_first, grad_second), 'az')  308 us
    ppermute x6, starting transfers between devices, with_halo(): lax.ppermute(tail, axis, [(i, (i + 1) % count) for i in range(ends)])  16.8 us
    reduce_scatter x2, waiting for transfers between devices, group_grad(): lax.psum_scatter(contract_cells(source, columns).astype(jnp.bfloat16), 'g...  13.3 us
    dot_general x2, matrix products, contract_cells(): lax.dot_general(left, right, (((1,), (1,)), ((), ())), preferred_element_...  11.9 us
    unnamed x85, local copies, waits for them, and re-layouts  9.53 us
  transfers between devices with their start and end apart: 16, of which 5 were waited for; matrix products, arithmetic and copies ran while one was open for 4% of the time, Pallas kernels for 0%

commit v1 on v0

v1 whole, which is shorter than its diff:
```python
import functools
import math

import jax
import jax.numpy as jnp
from jax import lax
from jax.experimental import pallas as pl
from jax.experimental.pallas import tpu as pltpu
from jax.sharding import PartitionSpec as P

AXIAL = 8
NRZ = 128
HALF = 64
LANES = 128
CH = 256
LAYERS = 4
TAPS = 27
BLOCK = 16
FIRST_TAPS = 14
ROWS = TAPS * BLOCK
FIRST = FIRST_TAPS * BLOCK
LAST = ROWS - FIRST
VMEM_LIMIT = 40 * 1024 * 1024
BF16 = jnp.bfloat16
F32 = jnp.float32


def params():
    return pltpu.CompilerParams(vmem_limit_bytes=VMEM_LIMIT)


def vmem():
    return pl.BlockSpec(memory_space=pltpu.VMEM)


def anywhere():
    return pl.BlockSpec(memory_space=pl.ANY)


def smem():
    return pl.BlockSpec(memory_space=pltpu.SMEM)


def shape(dims, kind=BF16):
    return jax.ShapeDtypeStruct(dims, kind)


def cost(flops, moved):
    return pl.CostEstimate(flops=flops, bytes_accessed=moved, transcendentals=0)


def az_extents(count):
    side = 1
    while (2 * side) ** 3 <= count:
        side *= 2
    if count % (side * side):
        side = 1
    return {"z": count // (side * side), "y": side, "x": side}


def az_places(count):
    extents = az_extents(count)
    places = []
    for index in range(count):
        rest, x = divmod(index, extents["x"])
        z, y = divmod(rest, extents["y"])
        places.append({"z": z, "y": y, "x": x})
    return extents, places


def shifted(value, along, by):
    extents, places = az_places(lax.axis_size("az"))
    pairs = []
    for index, place in enumerate(places):
        goal = dict(place)
        goal[along] = (place[along] + by) % extents[along]
        pairs.append((index, (goal["z"] * extents["y"] + goal["y"]) * extents["x"] + goal["x"]))
    return lax.ppermute(value, "az", pairs)


def my_place():
    extents, _ = az_places(lax.axis_size("az"))
    me = lax.axis_index("az")
    x = me % extents["x"]
    y = (me // extents["x"]) % extents["y"]
    z = me // (extents["x"] * extents["y"])
    return {"z": z, "y": y, "x": x}


def neighbour(value, az_by, grp_by):
    count = lax.axis_size("az")
    groups = lax.axis_size("grp")
    pairs = []
    for a in range(count):
        for g in range(groups):
            goal = ((a + az_by) % count) * groups + (g + grp_by) % groups
            pairs.append((a * groups + g, goal))
    return lax.ppermute(value, ("az", "grp"), pairs)


def tap_slice(ref, tap):
    return ref[:, tap * CH : (tap + 1) * CH]


def roll_rows(value, by):
    count = value.shape[0]
    rolled = pltpu.roll(value, by % count, axis=0)
    z = lax.broadcasted_iota(jnp.int32, value.shape, 0) % AXIAL
    edge = 0 if by == 1 else AXIAL - 1
    return jnp.where(z == edge, 0.0, rolled)


def shift_radius(value, by):
    layers, _, lanes = value.shape
    empty = jnp.zeros((layers, AXIAL, lanes), value.dtype)
    if by == 1:
        return jnp.concatenate([empty, value[:, : NRZ - AXIAL]], axis=1)
    return jnp.concatenate([value[:, AXIAL:], empty], axis=1)


def conv_rows(x_ref, w_ref, layers, first):
    count = layers * NRZ
    lhs = jnp.concatenate(
        [x_ref[(first + p) * NRZ : (first + p) * NRZ + count, :] for p in range(3)], axis=1
    )
    total = None
    for s in range(3):
        rhs = jnp.concatenate(
            [
                jnp.concatenate(
                    [tap_slice(w_ref, (p * 3 + q) * 3 + s) for p in range(3)], axis=1
                )
                for q in range(3)
            ],
            axis=0,
        )
        part = lax.dot_general(lhs, rhs, (((1,), (1,)), ((), ())), preferred_element_type=F32)
        part = part.reshape(layers, NRZ, 3 * LANES)
        summed = part[:, :, LANES : 2 * LANES]
        summed = summed + shift_radius(part[:, :, :LANES], 1)
        summed = summed + shift_radius(part[:, :, 2 * LANES :], -1)
        summed = summed.reshape(count, LANES)
        if s != 1:
            summed = roll_rows(summed, 1 - s)
        total = summed if total is None else total + summed
    return total


def pick_half(value, own):
    low = value[..., :LANES].astype(F32)
    high = value[..., LANES:].astype(F32)
    return jnp.where(jnp.broadcast_to(own, low.shape) == 0, low, high)


def pack_kernel(f_ref, c_ref, fc_ref, next_ref, last_ref, sems):
    copies = [
        (f_ref, fc_ref.at[:LAYERS]),
        (c_ref, fc_ref.at[LAYERS:]),
        (f_ref.at[LAYERS - 2 :], next_ref.at[:2]),
        (c_ref.at[LAYERS - 1 :], next_ref.at[2:]),
        (f_ref.at[:2], last_ref.at[:2]),
        (c_ref.at[:1], last_ref.at[2:]),
    ]
    copies = [pltpu.make_async_copy(a, b, sems.at[i]) for i, (a, b) in enumerate(copies)]
    for copy in copies:
        copy.start()
    for copy in copies:
        copy.wait()


def pack(f, c):
    return pl.pallas_call(
        pack_kernel,
        out_shape=[
            shape((2 * LAYERS, HALF, CH)),
            shape((3, HALF, CH)),
            shape((3, HALF, CH)),
        ],
        in_specs=[anywhere()] * 2,
        out_specs=[vmem()] * 3,
        scratch_shapes=[pltpu.SemaphoreType.DMA((6,))],
        compiler_params=params(),
        cost_estimate=cost(0, 900000),
    )(f, c)


def load_kernel(w1_ref, w2_ref, after, one_ref, two_ref, sems):
    copies = []
    for which, (source, goal) in enumerate(((w1_ref, one_ref), (w2_ref, two_ref))):
        for part in range(4):
            rows = pl.ds(part * 32, 32)
            copies.append(
                pltpu.make_async_copy(source.at[rows], goal.at[rows], sems.at[which, part])
            )
    for copy in copies:
        copy.start()
    for copy in copies:
        copy.wait()


def load(w_first, w_second, after):
    return pl.pallas_call(
        load_kernel,
        out_shape=[shape(w_first.shape), shape(w_second.shape)],
        in_specs=[anywhere()] * 3,
        out_specs=[vmem()] * 2,
        scratch_shapes=[pltpu.SemaphoreType.DMA((2, 4))],
        compiler_params=params(),
        cost_estimate=cost(0, 7000000),
    )(w_first, w_second, after)


def fields_kernel(
    place_ref, fc_ref, swap_ref, up_same, up_cross, down_same, down_cross,
    w1_ref, w2_ref, x_ref, cot_ref, send_ref, back_ref, slope_ref,
):
    own = place_ref[0]
    mine = pl.multiple_of(own * HALF, HALF)
    other = pl.multiple_of((1 - own) * HALF, HALF)
    for layer in range(2):
        x_ref[pl.ds(layer * NRZ + mine, HALF), :] = up_same[layer]
        x_ref[pl.ds(layer * NRZ + other, HALF), :] = up_cross[layer]
        x_ref[pl.ds((6 + layer) * NRZ + mine, HALF), :] = down_same[layer]
        x_ref[pl.ds((6 + layer) * NRZ + other, HALF), :] = down_cross[layer]
    for layer in range(LAYERS):
        x_ref[pl.ds((2 + layer) * NRZ + mine, HALF), :] = fc_ref[layer]
        x_ref[pl.ds((2 + layer) * NRZ + other, HALF), :] = swap_ref[layer]
        cot_ref[pl.ds((1 + layer) * NRZ + mine, HALF), :] = pick_half(
            fc_ref[LAYERS + layer], own
        ).astype(BF16)
        cot_ref[pl.ds((1 + layer) * NRZ + other, HALF), :] = pick_half(
            swap_ref[LAYERS + layer], own
        ).astype(BF16)
    cot_ref[pl.ds(mine, HALF), :] = pick_half(up_same[2], own).astype(BF16)
    cot_ref[pl.ds(other, HALF), :] = pick_half(up_cross[2], own).astype(BF16)
    cot_ref[pl.ds(5 * NRZ + mine, HALF), :] = pick_half(down_same[2], own).astype(BF16)
    cot_ref[pl.ds(5 * NRZ + other, HALF), :] = pick_half(down_cross[2], own).astype(BF16)

    pre = conv_rows(x_ref, w1_ref, LAYERS + 2, 0)
    sigma = jax.nn.sigmoid(pre)
    send_ref[: (LAYERS + 2) * NRZ, :] = (pre * sigma).astype(BF16)
    inner = pre[NRZ : NRZ * (LAYERS + 1)]
    sigma = sigma[NRZ : NRZ * (LAYERS + 1)]
    slope_ref[...] = sigma * (1.0 + inner * (1.0 - sigma))

    count = LAYERS * NRZ
    lhs = jnp.concatenate(
        [cot_ref[(2 - p) * NRZ : (2 - p) * NRZ + count, :] for p in range(3)], axis=1
    )
    total = None
    for s in range(3):
        summed = None
        for q in range(3):
            rhs = jnp.concatenate(
                [tap_slice(w2_ref, (p * 3 + q) * 3 + s) for p in range(3)], axis=0
            )
            part = jnp.dot(lhs, rhs, preferred_element_type=F32).reshape(LAYERS, NRZ, CH)
            if q != 1:
                part = shift_radius(part, q - 1)
            summed = part if summed is None else summed + part
        summed = summed.reshape(count, CH)
        if s != 1:
            summed = roll_rows(summed, s - 1)
        total = summed if total is None else total + summed
    back_ref[...] = pick_half(total, own)
    send_ref[(LAYERS + 2) * NRZ :, :] = pick_half(total, 1 - own).astype(BF16)


def fields(place, fc, swap, halos, w_first, w_second):
    rows = (LAYERS + 2) * NRZ
    return pl.pallas_call(
        fields_kernel,
        out_shape=[
            shape(((LAYERS + 4) * NRZ, CH)),
            shape((rows, LANES)),
            shape((rows + LAYERS * NRZ, LANES)),
            shape((LAYERS * NRZ, LANES), F32),
            shape((LAYERS * NRZ, LANES), F32),
        ],
        in_specs=[smem()] + [vmem()] * 8,
        out_specs=[vmem()] * 5,
        compiler_params=params(),
        cost_estimate=cost(2300000000, 6000000),
    )(place, fc, swap, *halos, w_first, w_second)


def grad_pieces(place_ref, source, field, factor, turned_ref, outs):
    own_x = place_ref[1]
    own_y = place_ref[2]
    own_z = place_ref[3]
    keep, y_first, y_last, x_first, x_last, d_first, d_last = outs
    lane = lax.broadcasted_iota(jnp.int32, (LANES, NRZ), 1)
    z = lane % AXIAL
    r = lane // AXIAL
    for layer in range(LAYERS):
        turned = source[layer * NRZ : (layer + 1) * NRZ, :].T
        for q in range(3):
            for s in range(3):
                by = AXIAL * (q - 1) + (s - 1)
                moved = pltpu.roll(turned, by % NRZ, axis=1) if by else turned
                if q == 0:
                    moved = jnp.where(r == NRZ // AXIAL - 1, 0.0, moved)
                if q == 2:
                    moved = jnp.where(r == 0, 0.0, moved)
                if s == 0:
                    moved = jnp.where(z == AXIAL - 1, 0.0, moved)
                if s == 2:
                    moved = jnp.where(z == 0, 0.0, moved)
                row = (q * 3 + s) * LANES
                turned_ref[row : row + LANES, layer * NRZ : (layer + 1) * NRZ] = moved.astype(BF16)
    x_zero = jnp.broadcast_to(own_x, (LANES, LANES)) == 0
    y_zero = jnp.broadcast_to(own_y, (HALF, LANES)) == 0
    slots = [lax.rem(index - own_z + 4, 4) for index in range(4)]
    for p in range(3):
        product = jnp.dot(turned_ref[...], field(p), preferred_element_type=F32) * factor
        for within in range(9):
            tap = p * 9 + within
            value = product[within * LANES : (within + 1) * LANES]
            low = value[:, :LANES]
            high = value[:, LANES:]
            halves = (jnp.where(x_zero, low, high), jnp.where(x_zero, high, low))
            for dx in range(2):
                top = halves[dx][:HALF]
                bottom = halves[dx][HALF:]
                parts = (jnp.where(y_zero, top, bottom), jnp.where(y_zero, bottom, top))
                for dy in range(2):
                    if dx == 0 and dy == 0:
                        ref, row = keep, tap * BLOCK
                    else:
                        pair = {(1, 0): (x_first, x_last), (0, 1): (y_first, y_last)}.get(
                            (dx, dy), (d_first, d_last)
                        )
                        if tap < FIRST_TAPS:
                            ref, row = pair[0], tap * BLOCK
                        else:
                            ref, row = pair[1], (tap - FIRST_TAPS) * BLOCK
                    narrow = parts[dy].astype(BF16)
                    for index in range(4):
                        ref[slots[index], row : row + BLOCK, :] = narrow[
                            index * BLOCK : (index + 1) * BLOCK
                        ]


def second_kernel(factor, place_ref, cot_ref, send_ref, got_ref, h_ref, *rest):
    outs, turned_ref = rest[:7], rest[7]
    rows = (LAYERS + 2) * NRZ
    own = place_ref[0]
    mine = send_ref[:rows, :].astype(F32)
    other = got_ref[:rows, :].astype(F32)
    first = jnp.broadcast_to(own, mine.shape) == 0
    h_ref[:, :LANES] = jnp.where(first, mine, other).astype(BF16)
    h_ref[:, LANES:] = jnp.where(first, other, mine).astype(BF16)
    source = cot_ref[NRZ : NRZ * (LAYERS + 1), :].astype(F32)
    field = lambda p: h_ref[p * NRZ : p * NRZ + LAYERS * NRZ, :]
    grad_pieces(place_ref, source, field, factor, turned_ref, outs)


def first_kernel(factor, place_ref, back_ref, got_ref, slope_ref, x_ref, after, *rest):
    outs, turned_ref = rest[:7], rest[7]
    rows = (LAYERS + 2) * NRZ
    source = (back_ref[...] + got_ref[rows:, :].astype(F32)) * slope_ref[...]
    source = source.astype(BF16).astype(F32)
    field = lambda p: x_ref[(p + 1) * NRZ : (p + 1) * NRZ + LAYERS * NRZ, :]
    grad_pieces(place_ref, source, field, factor, turned_ref, outs)


def piece_shapes():
    return [shape((4, ROWS, LANES))] + [shape((4, FIRST, LANES)), shape((4, LAST, LANES))] * 3


def second_grad(place, factor, cot, send, got):
    outs = pl.pallas_call(
        functools.partial(second_kernel, factor),
        out_shape=[shape(((LAYERS + 2) * NRZ, CH))] + piece_shapes(),
        in_specs=[smem()] + [vmem()] * 3,
        out_specs=[vmem()] * 8,
        scratch_shapes=[pltpu.VMEM((9 * LANES, LAYERS * NRZ), BF16)],
        compiler_params=params(),
        cost_estimate=cost(1000000000, 3000000),
    )(place, cot, send, got)
    return outs[0], outs[1:]


def first_grad(place, factor, back, got, slope, x, after):
    return pl.pallas_call(
        functools.partial(first_kernel, factor),
        out_shape=piece_shapes(),
        in_specs=[smem()] + [vmem()] * 4 + [anywhere()],
        out_specs=[vmem()] * 7,
        scratch_shapes=[pltpu.VMEM((9 * LANES, LAYERS * NRZ), BF16)],
        compiler_params=params(),
        cost_estimate=cost(1000000000, 3000000),
    )(place, back, got, slope, x, after)


def flow_kernel(place_ref, x_ref, h_ref, w2_ref, keep_ref, send_ref):
    own = place_ref[0]
    result = conv_rows(h_ref, w2_ref, LAYERS, 0)
    result = result + pick_half(x_ref[2 * NRZ : 2 * NRZ + LAYERS * NRZ, :], own)
    halves = result.reshape(LAYERS, 2, HALF, LANES)
    first = jnp.broadcast_to(own, (LAYERS, HALF, LANES)) == 0
    keep_ref[...] = jnp.where(first, halves[:, 0], halves[:, 1]).astype(BF16)
    send_ref[...] = jnp.where(first, halves[:, 1], halves[:, 0]).astype(BF16)


def flow(place, x, h, w_second):
    return pl.pallas_call(
        flow_kernel,
        out_shape=[shape((LAYERS, HALF, LANES))] * 2,
        in_specs=[smem()] + [vmem()] * 3,
        out_specs=[vmem()] * 2,
        compiler_params=params(),
        cost_estimate=cost(1000000000, 3000000),
    )(place, x, h, w_second)


def join_kernel(place_ref, mine_ref, theirs_ref, out_ref):
    mine = mine_ref[...].astype(F32)
    theirs = theirs_ref[...].astype(F32)
    first = jnp.broadcast_to(place_ref[0], mine.shape) == 0
    out_ref[:, :, :LANES] = jnp.where(first, mine, theirs).astype(BF16)
    out_ref[:, :, LANES:] = jnp.where(first, theirs, mine).astype(BF16)


def join_flow(place, mine, theirs):
    return pl.pallas_call(
        join_kernel,
        out_shape=shape((LAYERS, HALF, CH)),
        in_specs=[smem()] + [vmem()] * 2,
        out_specs=vmem(),
        compiler_params=params(),
        cost_estimate=cost(0, 400000),
    )(place, mine, theirs)


def write_kernel(place_ref, m_ref, mx_ref, my_ref, first_ref, last_ref, out_ref):
    x_zero = jnp.broadcast_to(place_ref[1], (BLOCK, LANES)) == 0
    far = pl.program_id(0)

    def put(tap, near, across):
        low = jnp.where(x_zero, near, across)
        high = jnp.where(x_zero, across, near)
        out_ref[:, tap * CH : tap * CH + LANES] = low
        out_ref[:, tap * CH + LANES : (tap + 1) * CH] = high

    @pl.when(far == 0)
    def _():
        for tap in range(TAPS):
            rows = slice(tap * BLOCK, (tap + 1) * BLOCK)
            put(tap, m_ref[0, rows, :].astype(F32), mx_ref[0, rows, :].astype(F32))

    @pl.when(far == 1)
    def _():
        for tap in range(TAPS):
            rows = slice(tap * BLOCK, (tap + 1) * BLOCK)
            if tap < FIRST_TAPS:
                across = first_ref[0, rows, :]
            else:
                across = last_ref[0, (tap - FIRST_TAPS) * BLOCK : (tap - FIRST_TAPS + 1) * BLOCK, :]
            put(tap, my_ref[0, rows, :].astype(F32), across.astype(F32))


def write_out(place, pieces):
    near = lambda dy, dz, place: (dz * (1 - dy) + 3 * dy, 0, 0)
    far = lambda dy, dz, place: (dz * dy, 0, 0)
    block = lambda dy, dz, place: (
        lax.rem(place[2] + dy, 2) * 4 + lax.rem(place[3] + dz, 4),
        0,
    )
    return pl.pallas_call(
        write_kernel,
        out_shape=shape((LANES, TAPS * CH), F32),
        grid_spec=pltpu.PrefetchScalarGridSpec(
            num_scalar_prefetch=1,
            grid=(2, 4),
            in_specs=[
                pl.BlockSpec((1, ROWS, LANES), near),
                pl.BlockSpec((1, ROWS, LANES), near),
                pl.BlockSpec((1, ROWS, LANES), far),
                pl.BlockSpec((1, FIRST, LANES), far),
                pl.BlockSpec((1, LAST, LANES), far),
            ],
            out_specs=pl.BlockSpec((BLOCK, TAPS * CH), block),
        ),
        compiler_params=params(),
        cost_estimate=cost(0, 6000000),
    )(place, *pieces)


def plus(*terms):
    total = terms[0].astype(F32)
    for term in terms[1:]:
        total = total + term.astype(F32)
    return total.astype(BF16)


def meet_kernel(y_first, got_first, x_last, got_last, after, y_out, x_out):
    y_out[...] = plus(y_first[...], got_first[...])
    x_out[...] = plus(x_last[...], got_last[...])


def meet(y_first, got_first, x_last, got_last, after):
    return pl.pallas_call(
        meet_kernel,
        out_shape=[shape(y_first.shape), shape(x_last.shape)],
        in_specs=[vmem()] * 4 + [anywhere()],
        out_specs=[vmem()] * 2,
        compiler_params=params(),
        cost_estimate=cost(0, 1300000),
    )(y_first, got_first, x_last, got_last, after)


def sum_kernel(keep, x_first, x_last, y_first, y_last, after, *outs):
    for index in range(4):
        for rows, x_part, y_part in (
            (slice(0, FIRST), x_first, y_first),
            (slice(FIRST, ROWS), x_last, y_last),
        ):
            outs[index][rows, :] = plus(keep[index, rows, :], x_part[index], y_part[index])


def sum_quads(keep, x_first, x_last, y_first, y_last, after):
    return pl.pallas_call(
        sum_kernel,
        out_shape=[shape((ROWS, LANES))] * 4,
        in_specs=[vmem()] * 5 + [anywhere()],
        out_specs=[vmem()] * 4,
        compiler_params=params(),
        cost_estimate=cost(0, 1800000),
    )(keep, x_first, x_last, y_first, y_last, after)


def own_kernel(one, two, three, four, after, out):
    out[...] = plus(one[...], two[...], three[...], four[...])


def own_block(rows, after):
    return pl.pallas_call(
        own_kernel,
        out_shape=shape((ROWS, LANES)),
        in_specs=[vmem()] * 4 + [anywhere()],
        out_specs=vmem(),
        compiler_params=params(),
        cost_estimate=cost(0, 600000),
    )(*rows, after)


def stack_kernel(one, two, three, four, after, out):
    for index, ref in enumerate((one, two, three, four)):
        out[index] = ref[...]


def stack_blocks(rows, after):
    return pl.pallas_call(
        stack_kernel,
        out_shape=shape((4, ROWS, LANES)),
        in_specs=[vmem()] * 4 + [anywhere()],
        out_specs=vmem(),
        compiler_params=params(),
        cost_estimate=cost(0, 900000),
    )(*rows, after)


def relay_kernel(x_ref, y_ref, after, first_ref, last_ref):
    first_ref[...] = x_ref[:, :FIRST]
    last_ref[...] = y_ref[:, FIRST:]


def relay(across_x, across_y, after):
    return pl.pallas_call(
        relay_kernel,
        out_shape=[shape((4, FIRST, LANES)), shape((4, LAST, LANES))],
        in_specs=[vmem()] * 2 + [anywhere()],
        out_specs=[vmem()] * 2,
        compiler_params=params(),
        cost_estimate=cost(0, 900000),
    )(across_x, across_y, after)


class QuadSum:
    def diagonal(self, pieces):
        self.keep, self.y_first, self.y_last, self.x_first, self.x_last, d_first, d_last = pieces
        self.got_first = shifted(d_first, "x", 1)
        self.got_last = shifted(d_last, "y", 1)
        self.in_x_first = shifted(self.x_first, "x", 1)
        self.in_y_last = shifted(self.y_last, "y", 1)

    def sides(self, after):
        y_first, x_last = meet(self.y_first, self.got_first, self.x_last, self.got_last, after)
        self.in_y_first = shifted(y_first, "y", 1)
        self.in_x_last = shifted(x_last, "x", 1)
        return x_last

    def along_z(self, after):
        rows = sum_quads(
            self.keep, self.in_x_first, self.in_x_last, self.in_y_first, self.in_y_last, after
        )
        self.rows = [rows[0]] + [shifted(rows[by], "z", by) for by in range(1, 4)]
        return rows[0]

    def back_z(self, after):
        own = own_block(self.rows, after)
        self.blocks = [own] + [shifted(own, "z", -by) for by in range(1, 4)]
        return own

    def back_sides(self, after):
        self.whole = stack_blocks(self.blocks, after)
        self.across_x = shifted(self.whole, "x", 1)
        self.across_y = shifted(self.whole, "y", 1)
        return self.whole

    def back_diagonal(self, after):
        first, last = relay(self.across_x, self.across_y, after)
        self.far_first = shifted(first, "y", 1)
        self.far_last = shifted(last, "x", 1)
        return last

    def result(self):
        return self.whole, self.across_x, self.across_y, self.far_first, self.far_last


def any_reduce_gather(pieces, place):
    extents, _ = az_places(lax.axis_size("az"))
    count = lax.axis_size("az")
    keep, y_first, y_last, x_first, x_last, d_first, d_last = pieces
    join = lambda first, last: jnp.concatenate([first, last], axis=1)
    cut = jnp.stack([keep, join(y_first, y_last), join(x_first, x_last), join(d_first, d_last)])
    order = ("x", "y", "z")
    full = cut.shape
    cut = cut.reshape([extents[name] for name in order] + [-1, LANES])
    for position, name in enumerate(order):
        cut = jnp.roll(cut, -place[name], axis=position)
    for name in order:
        cut = plus(cut[0], *[shifted(cut[by], name, by) for by in range(1, extents[name])])
    for name in order[::-1]:
        mine = cut
        cut = jnp.stack([mine] + [shifted(mine, name, -by) for by in range(1, extents[name])])
    for position, name in enumerate(order):
        cut = jnp.roll(cut, place[name], axis=position)
    cut = cut.reshape(full)
    return cut[0], cut[2], cut[1], cut[3][:, :FIRST], cut[3][:, FIRST:]


def local(features, cotangent, w_first, w_second):
    groups = lax.axis_size("grp")
    cells = lax.axis_size("az") * LAYERS * HALF * groups
    factor = 1.0 / math.sqrt(cells)
    extents, _ = az_places(lax.axis_size("az"))
    quad = extents == {"x": 2, "y": 2, "z": 4}
    spot = my_place()
    own = lax.axis_index("grp")
    zero = jnp.zeros((), jnp.int32)
    place = jnp.stack(
        [own] + [spot[name] if quad else zero for name in ("x", "y", "z")]
    ).astype(jnp.int32)

    f = features.transpose(1, 2, 0)
    c = cotangent.transpose(1, 2, 0)
    fc, to_next, to_last = pack(f, c)
    swap = neighbour(fc, 0, 1)
    up = neighbour(to_next, 1, 0)
    down = neighbour(to_last, -1, 0)
    w_one, w_two = load(w_first, w_second, to_last)
    halos = [up, neighbour(up, 0, 1), down, neighbour(down, 0, 1)]
    x, cot, send, back, slope = fields(place, fc, swap, halos, w_one, w_two)
    got = neighbour(send, 0, 1)
    hidden, second = second_grad(place, factor, cot, send, got)
    mine, theirs = flow(place, x, hidden, w_two)
    theirs = neighbour(theirs, 0, 1)
    if quad:
        one, two = QuadSum(), QuadSum()
        one.diagonal(second)
        step = one.sides(mine)
        two.diagonal(first_grad(place, factor, back, got, slope, x, step))
        flow_out = join_flow(place, mine, theirs)
        step = one.along_z(flow_out)
        step = two.sides(step)
        step = one.back_z(step)
        step = two.along_z(step)
        step = one.back_sides(step)
        step = two.back_z(step)
        step = one.back_diagonal(step)
        step = two.back_sides(step)
        grad_second = write_out(place, one.result())
        two.back_diagonal(grad_second)
        grad_first = write_out(place, two.result())
    else:
        flow_out = join_flow(place, mine, theirs)
        first = first_grad(place, factor, back, got, slope, x, mine)
        grad_second = write_out(place, any_reduce_gather(second, spot))
        grad_first = write_out(place, any_reduce_gather(first, spot))
    return (flow_out.transpose(2, 0, 1), grad_first, grad_second)


def solution(mesh):
    in_specs = (P(None, "az", "grp"), P(None, "az", "grp"), P("grp", None), P("grp", None))
    out_specs = (P(None, "az", "grp"), P("grp", None), P("grp", None))
    return jax.shard_map(local, mesh=mesh, in_specs=in_specs, out_specs=out_specs, check_vma=False)
```

time: 408 us -> 125 us (0.31)
  the two profiles are of different devices: /device:TPU:10 before, /device:TPU:0 now
where the time goes in v1:
time: 125 us
  starting transfers between devices  49.2 us (39%)
  waiting for transfers between devices  45 us (36%)
  Pallas kernels  22.2 us (18%)
  local copies, waits for them, and re-layouts  7.66 us (6%)
    ppermute x32, waiting for transfers between devices, shifted(): return lax.ppermute(value, 'az', pairs)  42.9 us
    ppermute x32, starting transfers between devices, shifted(): return lax.ppermute(value, 'az', pairs)  40.9 us
    ppermute x7, starting transfers between devices, neighbour(): return lax.ppermute(value, ('az', 'grp'), pairs)  8.22 us
    pallas_call x2, Pallas kernels, write_out(): pl.pallas_call(write_kernel, out_shape=shape((LANES, TAPS * CH), F32), gr...  7.9 us
    unnamed x12, local copies, waits for them, and re-layouts  7.66 us
    pallas_call x1, Pallas kernels, fields(): pl.pallas_call(fields_kernel, out_shape=[shape(((LAYERS + 4) * NRZ, CH)),...  3.92 us
  transfers between devices with their start and end apart: 39, of which 18 were waited for; matrix products, arithmetic and copies ran while one was open for 0% of the time, Pallas kernels for 9%

profile of v1, /device:TPU:0, one launch (start us, length us, event | category | flops | bytes accessed | tf_op | source)
XLA Modules:
  0.0 125.0 jit_solution(16290197282421244623)
XLA Ops:
  0.6 0.9 copy-done.4
  1.5 0.9 copy-done.5
  2.4 0.6 shard_map.67
  3.1 0.5 collective-permute-start
  3.6 2.6 %collective-permute-start.1 = (bf16[3,64,256]{2,1,0:T(8,128)(2,1)S(1)}, bf16[3,64,256]{2,1,0:T(8,128)(2,1)S(1)}, u32[]{:S(2)}, u32[]{:S(2)}) collective-permute-start(bf16[3,64,256]{2,1,0:T(8,128)(2,1)S(1)} %get-tuple-element.47), channel_id=1, source_target_pairs={{0,2},{1,3},{2,4},{3,5},{4,6},{5,7},{6,8},{7,9},{8,10},{9,11},{10,... | collective-permute-start | bytes 294920 | tf_op jit(solution)/shard_map/ppermute | solution.py:98
  6.1 4.1 %collective-permute-start.3 = (bf16[3,64,256]{2,1,0:T(8,128)(2,1)S(1)}, bf16[3,64,256]{2,1,0:T(8,128)(2,1)S(1)}, u32[]{:S(2)}, u32[]{:S(2)}) collective-permute-start(bf16[3,64,256]{2,1,0:T(8,128)(2,1)S(1)} %get-tuple-element.48.after), channel_id=1, source_target_pairs={{0,30},{1,31},{2,0},{3,1},{4,2},{5,3},{6,4},{7,5},{8,6},{9,7},{10,... | collective-permute-start | bytes 294920 | tf_op jit(solution)/shard_map/ppermute | solution.py:98
  10.2 1.5 %copy-done.1 = bf16[128,6912]{1,0:T(8,128)(2,1)S(1)} copy-done((bf16[128,6912]{1,0:T(8,128)(2,1)S(1)}, bf16[128,6912]{1,0:T(8,128)(2,1)}, u32[]{:S(2)}) %copy-start.1) | copy-done | bytes 1769496
  11.7 1.5 %copy-done.2 = bf16[128,6912]{1,0:T(8,128)(2,1)S(1)} copy-done((bf16[128,6912]{1,0:T(8,128)(2,1)S(1)}, bf16[128,6912]{1,0:T(8,128)(2,1)}, u32[]{:S(2)}) %copy-start.2) | copy-done | bytes 1769496
  13.2 2.1 %shard_map.68 = (bf16[128,6912]{1,0:T(8,128)(2,1)S(1)}, bf16[128,6912]{1,0:T(8,128)(2,1)S(1)}) custom-call(bf16[128,6912]{1,0:T(8,128)(2,1)S(1)} %copy-done.1, bf16[128,6912]{1,0:T(8,128)(2,1)S(1)} %copy-done.2, bf16[3,64,256]{2,1,0:T(8,128)(2,1)S(1)} %get-tuple-element.48.after), custom_call_target="tpu_custom_call" | custom-call | bytes 7000000 | tf_op jit(solution)/shard_map/pallas_call | solution.py:202
  15.4 0.4 collective-permute-start.4
  15.9 0.7 collective-permute-done.2.up_cross
  16.8 3.9 %shard_map.69 = (bf16[1024,256]{1,0:T(8,128)(2,1)S(1)}, bf16[768,128]{1,0:T(8,128)(2,1)S(1)}, bf16[1280,128]{1,0:T(8,128)(2,1)S(1)}, f32[512,128]{1,0:T(8,128)S(1)}, f32[512,128]{1,0:T(8,128)S(1)}) custom-call(s32[4]{0:T(128)S(1)} %pad_add_fusion.place_ref, bf16[8,64,256]{2,1,0:T(8,128)(2,1)S(1)} %get-tuple-element.46.fc_ref, ...), custom_call_target="tpu_custom_call" | custom-call | flops 2300000000 | bytes 6000000 | tf_op jit(solution)/shard_map/pallas_call | solution.py:271
  20.7 0.4 collective-permute-start.5
  21.1 1.3 %collective-permute-done.5.got_ref = bf16[1280,128]{1,0:T(8,128)(2,1)S(1)} collective-permute-done((bf16[1280,128]{1,0:T(8,128)(2,1)S(1)}, bf16[1280,128]{1,0:T(8,128)(2,1)S(1)}, u32[]{:S(2)}, u32[]{:S(2)}) %collective-permute-start.5) | collective-permute-done | bytes 327712 | tf_op jit(solution)/shard_map/ppermute | solution.py:98
  22.4 1.9 %shard_map.70 = (bf16[768,256]{1,0:T(8,128)(2,1)S(1)}, bf16[4,432,128]{2,1,0:T(8,128)(2,1)S(1)}, bf16[4,224,128]{2,1,0:T(8,128)(2,1)S(1)}, bf16[4,208,128]{2,1,0...) custom-call(s32[4]{0:T(128)S(1)} %pad_add_fusion.place_ref, ...), custom_call_target="tpu_custom_call" | custom-call | flops 1000000000 | bytes 3000000 | tf_op jit(solution)/shard_map/pallas_call | solution.py:372
  24.4 0.3 collective-permute-start.8
  24.7 1.8 %collective-permute-start.15 = (bf16[4,208,128]{2,1,0:T(8,128)(2,1)S(1)}, bf16[4,208,128]{2,1,0:T(8,128)(2,1)S(1)}, u32[]{:S(2)}, u32[]{:S(2)}) collective-permute-start(bf16[4,208,128]{2,1,0:T(8,128)(2,1)S(1)} %get-tuple-element.73), channel_id=1, source_target_pairs={{0,4},{2,6},{4,0},{6,2},{8,12},{10,14},{12,8},{14,10},{16,20},{18,... | collective-permute-start | bytes 638984 | tf_op jit(solution)/shard_map/ppermute | solution.py:78
  26.5 2.0 %shard_map.71 = (bf16[4,64,128]{2,1,0:T(8,128)(2,1)S(1)}, bf16[4,64,128]{2,1,0:T(8,128)(2,1)S(1)}) custom-call(s32[4]{0:T(128)S(1)} %pad_add_fusion.place_ref, bf16[1024,256]{1,0:T(8,128)(2,1)S(1)} %get-tuple-element.51.x_ref, bf16[768,256]{1,0:T(8,128)(2,1)S(1)} %get-tuple-element.54.h_ref, bf16[128,6912]{1,0:T(8,128)(2,1)S(1)} %get-tuple-element.50.w2_ref), custom_call_target="tpu_custom_call" | custom-call | flops 1000000000 | bytes 3000000 | tf_op jit(solution)/shard_map/pallas_call | solution.py:407
  28.5 2.0 %collective-permute-start.12 = (bf16[4,224,128]{2,1,0:T(8,128)(2,1)S(1)}, bf16[4,224,128]{2,1,0:T(8,128)(2,1)S(1)}, u32[]{:S(2)}, u32[]{:S(2)}) collective-permute-start(bf16[4,224,128]{2,1,0:T(8,128)(2,1)S(1)} %get-tuple-element.71), channel_id=1, source_target_pairs={{0,2},{2,0},{4,6},{6,4},{8,10},{10,8},{12,14},{14,12},{16,18},{18,... | collective-permute-start | bytes 688136 | tf_op jit(solution)/shard_map/ppermute | solution.py:78
  30.6 2.0 %collective-permute-done.8.got_last = bf16[4,208,128]{2,1,0:T(8,128)(2,1)S(1)} collective-permute-done((bf16[4,208,128]{2,1,0:T(8,128)(2,1)S(1)}, bf16[4,208,128]{2,1,0:T(8,128)(2,1)S(1)}, u32[]{:S(2)}, u32[]{:S(2)}) %collective-permute-start.8) | collective-permute-done | bytes 213024 | tf_op jit(solution)/shard_map/ppermute | solution.py:78
  32.7 2.0 %collective-permute-start.13 = (bf16[4,208,128]{2,1,0:T(8,128)(2,1)S(1)}, bf16[4,208,128]{2,1,0:T(8,128)(2,1)S(1)}, u32[]{:S(2)}, u32[]{:S(2)}) collective-permute-start(bf16[4,208,128]{2,1,0:T(8,128)(2,1)S(1)} %get-tuple-element.63.after), channel_id=1, source_target_pairs={{0,2},{2,0},{4,6},{6,4},{8,10},{10,8},{12,14},{14,12},{16,18},{18,... | collective-permute-start | bytes 638984 | tf_op jit(solution)/shard_map/ppermute | solution.py:78
  34.7 1.9 %shard_map.74 = (bf16[4,432,128]{2,1,0:T(8,128)(2,1)S(1)}, bf16[4,224,128]{2,1,0:T(8,128)(2,1)S(1)}, bf16[4,208,128]{2,1,0:T(8,128)(2,1)S(1)}, bf16[4,224,128]{2...) custom-call(s32[4]{0:T(128)S(1)} %pad_add_fusion.place_ref, ...), custom_call_target="tpu_custom_call" | custom-call | flops 1000000000 | bytes 3000000 | tf_op jit(solution)/shard_map/pallas_call | solution.py:385
  36.6 2.1 %collective-permute-start.11 = (bf16[4,208,128]{2,1,0:T(8,128)(2,1)S(1)}, bf16[4,208,128]{2,1,0:T(8,128)(2,1)S(1)}, u32[]{:S(2)}, u32[]{:S(2)}) collective-permute-start(bf16[4,208,128]{2,1,0:T(8,128)(2,1)S(1)} %get-tuple-element.69), channel_id=1, source_target_pairs={{0,4},{2,6},{4,0},{6,2},{8,12},{10,14},{12,8},{14,10},{16,20},{18,... | collective-permute-start | bytes 638984 | tf_op jit(solution)/shard_map/ppermute | solution.py:78
  38.7 0.4 collective-permute-start.10
  39.1 1.6 %collective-permute-start.9 = (bf16[4,224,128]{2,1,0:T(8,128)(2,1)S(1)}, bf16[4,224,128]{2,1,0:T(8,128)(2,1)S(1)}, u32[]{:S(2)}, u32[]{:S(2)}) collective-permute-start(bf16[4,224,128]{2,1,0:T(8,128)(2,1)S(1)} %get-tuple-element.65), channel_id=1, source_target_pairs={{0,2},{2,0},{4,6},{6,4},{8,10},{10,8},{12,14},{14,12},{16,18},{18,... | collective-permute-start | bytes 688136 | tf_op jit(solution)/shard_map/ppermute | solution.py:78
  40.7 1.2 shard_map.72.after
  42.1 1.2 collective-permute-done.14.y_first
  43.2 0.9 copy-done.3
  44.4 2.4 %collective-permute-start.20 = (bf16[432,128]{1,0:T(8,128)(2,1)S(1)}, bf16[432,128]{1,0:T(8,128)(2,1)S(1)}, u32[]{:S(2)}, u32[]{:S(2)}) collective-permute-start(bf16[432,128]{1,0:T(8,128)(2,1)S(1)} %get-tuple-element.79), channel_id=1, source_target_pairs={{0,16},{2,18},{4,20},{6,22},{8,24},{10,26},{12,28},{14,30},{16,0},... | collective-permute-start | bytes 331784 | tf_op jit(solution)/shard_map/ppermute | solution.py:78
  46.8 1.4 %collective-permute-start.18 = (bf16[4,208,128]{2,1,0:T(8,128)(2,1)S(1)}, bf16[4,208,128]{2,1,0:T(8,128)(2,1)S(1)}, u32[]{:S(2)}, u32[]{:S(2)}) collective-permute-start(bf16[4,208,128]{2,1,0:T(8,128)(2,1)S(1)} %get-tuple-element.77), channel_id=1, source_target_pairs={{0,4},{2,6},{4,0},{6,2},{8,12},{10,14},{12,8},{14,10},{16,20},{18,... | collective-permute-start | bytes 638984 | tf_op jit(solution)/shard_map/ppermute | solution.py:78
  48.3 0.7 collective-permute-start.17
  49.0 2.0 %collective-permute-done.19.two = bf16[432,128]{1,0:T(8,128)(2,1)S(1)} collective-permute-done((bf16[432,128]{1,0:T(8,128)(2,1)S(1)}, bf16[432,128]{1,0:T(8,128)(2,1)S(1)}, u32[]{:S(2)}, u32[]{:S(2)}) %collective-permute-start.19) | collective-permute-done | bytes 110624 | tf_op jit(solution)/shard_map/ppermute | solution.py:78
  51.0 0.7 collective-permute-start.21
  51.6 2.6 %collective-permute-done.20.three = bf16[432,128]{1,0:T(8,128)(2,1)S(1)} collective-permute-done((bf16[432,128]{1,0:T(8,128)(2,1)S(1)}, bf16[432,128]{1,0:T(8,128)(2,1)S(1)}, u32[]{:S(2)}, u32[]{:S(2)}) %collective-permute-start.20) | collective-permute-done | bytes 110624 | tf_op jit(solution)/shard_map/ppermute | solution.py:78
  54.3 1.2 collective-permute-start.16
  55.8 0.6 collective-permute-start.27
  56.4 2.5 %collective-permute-start.26 = (bf16[432,128]{1,0:T(8,128)(2,1)S(1)}, bf16[432,128]{1,0:T(8,128)(2,1)S(1)}, u32[]{:S(2)}, u32[]{:S(2)}) collective-permute-start(bf16[432,128]{1,0:T(8,128)(2,1)S(1)} %shard_map.77.after.one), channel_id=1, source_target_pairs={{0,16},{2,18},{4,20},{6,22},{8,24},{10,26},{12,28},{14,30},{16,0},... | collective-permute-start | bytes 331784 | tf_op jit(solution)/shard_map/ppermute | solution.py:78
  58.9 1.8 %collective-permute-start.25 = (bf16[432,128]{1,0:T(8,128)(2,1)S(1)}, bf16[432,128]{1,0:T(8,128)(2,1)S(1)}, u32[]{:S(2)}, u32[]{:S(2)}) collective-permute-start(bf16[432,128]{1,0:T(8,128)(2,1)S(1)} %shard_map.77.after.one), channel_id=1, source_target_pairs={{0,24},{2,26},{4,28},{6,30},{8,0},{10,2},{12,4},{14,6},{16,8},{18,... | collective-permute-start | bytes 331784 | tf_op jit(solution)/shard_map/ppermute | solution.py:78
  60.9 1.7 %collective-permute-done.27.four = bf16[432,128]{1,0:T(8,128)(2,1)S(1)} collective-permute-done((bf16[432,128]{1,0:T(8,128)(2,1)S(1)}, bf16[432,128]{1,0:T(8,128)(2,1)S(1)}, u32[]{:S(2)}, u32[]{:S(2)}) %collective-permute-start.27) | collective-permute-done | bytes 110624 | tf_op jit(solution)/shard_map/ppermute | solution.py:78
  62.5 3.1 %collective-permute-done.26.three = bf16[432,128]{1,0:T(8,128)(2,1)S(1)} collective-permute-done((bf16[432,128]{1,0:T(8,128)(2,1)S(1)}, bf16[432,128]{1,0:T(8,128)(2,1)S(1)}, u32[]{:S(2)}, u32[]{:S(2)}) %collective-permute-start.26) | collective-permute-done | bytes 110624 | tf_op jit(solution)/shard_map/ppermute | solution.py:78
  65.7 1.1 collective-permute-start.32
  66.7 1.1 collective-permute-start.31
  67.8 2.8 %collective-permute-start.22 = (bf16[432,128]{1,0:T(8,128)(2,1)S(1)}, bf16[432,128]{1,0:T(8,128)(2,1)S(1)}, u32[]{:S(2)}, u32[]{:S(2)}) collective-permute-start(bf16[432,128]{1,0:T(8,128)(2,1)S(1)} %get-tuple-element.82), channel_id=1, source_target_pairs={{0,8},{2,10},{4,12},{6,14},{8,16},{10,18},{12,20},{14,22},{16,24},... | collective-permute-start | bytes 331784 | tf_op jit(solution)/shard_map/ppermute | solution.py:78
  70.6 1.4 %collective-permute-start.23 = (bf16[432,128]{1,0:T(8,128)(2,1)S(1)}, bf16[432,128]{1,0:T(8,128)(2,1)S(1)}, u32[]{:S(2)}, u32[]{:S(2)}) collective-permute-start(bf16[432,128]{1,0:T(8,128)(2,1)S(1)} %get-tuple-element.83), channel_id=1, source_target_pairs={{0,16},{2,18},{4,20},{6,22},{8,24},{10,26},{12,28},{14,30},{16,0},... | collective-permute-start | bytes 331784 | tf_op jit(solution)/shard_map/ppermute | solution.py:78
  72.0 1.0 collective-permute-start.24
  73.0 2.6 %collective-permute-done.22.two = bf16[432,128]{1,0:T(8,128)(2,1)S(1)} collective-permute-done((bf16[432,128]{1,0:T(8,128)(2,1)S(1)}, bf16[432,128]{1,0:T(8,128)(2,1)S(1)}, u32[]{:S(2)}, u32[]{:S(2)}) %collective-permute-start.22) | collective-permute-done | bytes 110624 | tf_op jit(solution)/shard_map/ppermute | solution.py:78
  75.6 3.5 %collective-permute-done.23.three = bf16[432,128]{1,0:T(8,128)(2,1)S(1)} collective-permute-done((bf16[432,128]{1,0:T(8,128)(2,1)S(1)}, bf16[432,128]{1,0:T(8,128)(2,1)S(1)}, u32[]{:S(2)}, u32[]{:S(2)}) %collective-permute-start.23) | collective-permute-done | bytes 110624 | tf_op jit(solution)/shard_map/ppermute | solution.py:78
  79.1 2.9 %collective-permute-start.30 = (bf16[432,128]{1,0:T(8,128)(2,1)S(1)}, bf16[432,128]{1,0:T(8,128)(2,1)S(1)}, u32[]{:S(2)}, u32[]{:S(2)}) collective-permute-start(bf16[432,128]{1,0:T(8,128)(2,1)S(1)} %shard_map.80.after.one), channel_id=1, source_target_pairs={{0,8},{2,10},{4,12},{6,14},{8,16},{10,18},{12,20},{14,22},{16,24},... | collective-permute-start | bytes 331784 | tf_op jit(solution)/shard_map/ppermute | solution.py:78
  82.0 1.5 %collective-permute-start.29 = (bf16[432,128]{1,0:T(8,128)(2,1)S(1)}, bf16[432,128]{1,0:T(8,128)(2,1)S(1)}, u32[]{:S(2)}, u32[]{:S(2)}) collective-permute-start(bf16[432,128]{1,0:T(8,128)(2,1)S(1)} %shard_map.80.after.one), channel_id=1, source_target_pairs={{0,16},{2,18},{4,20},{6,22},{8,24},{10,26},{12,28},{14,30},{16,0},... | collective-permute-start | bytes 331784 | tf_op jit(solution)/shard_map/ppermute | solution.py:78
  83.5 1.0 collective-permute-start.28
  84.5 2.4 %collective-permute-done.30.four = bf16[432,128]{1,0:T(8,128)(2,1)S(1)} collective-permute-done((bf16[432,128]{1,0:T(8,128)(2,1)S(1)}, bf16[432,128]{1,0:T(8,128)(2,1)S(1)}, u32[]{:S(2)}, u32[]{:S(2)}) %collective-permute-start.30) | collective-permute-done | bytes 110624 | tf_op jit(solution)/shard_map/ppermute | solution.py:78
  86.8 3.8 %collective-permute-done.29.three = bf16[432,128]{1,0:T(8,128)(2,1)S(1)} collective-permute-done((bf16[432,128]{1,0:T(8,128)(2,1)S(1)}, bf16[432,128]{1,0:T(8,128)(2,1)S(1)}, u32[]{:S(2)}, u32[]{:S(2)}) %collective-permute-start.29) | collective-permute-done | bytes 110624 | tf_op jit(solution)/shard_map/ppermute | solution.py:78
  90.7 0.4 collective-permute-start.34
  91.1 1.0 collective-permute-start.33
  92.1 1.7 %collective-permute-start.35 = (bf16[4,224,128]{2,1,0:T(8,128)(2,1)S(1)}, bf16[4,224,128]{2,1,0:T(8,128)(2,1)S(1)}, u32[]{:S(2)}, u32[]{:S(2)}) collective-permute-start(bf16[4,224,128]{2,1,0:T(8,128)(2,1)S(1)} %get-tuple-element.86), channel_id=1, source_target_pairs={{0,4},{2,6},{4,0},{6,2},{8,12},{10,14},{12,8},{14,10},{16,20},{18,... | collective-permute-start | bytes 688136 | tf_op jit(solution)/shard_map/ppermute | solution.py:78
  93.8 1.1 collective-permute-start.36
  94.9 12.6 %collective-permute-done.36.last_ref = bf16[4,208,128]{2,1,0:T(8,128)(2,1)S(1)} collective-permute-done((bf16[4,208,128]{2,1,0:T(8,128)(2,1)S(1)}, bf16[4,208,128]{2,1,0:T(8,128)(2,1)S(1)}, u32[]{:S(2)}, u32[]{:S(2)}) %collective-permute-start.36) | collective-permute-done | bytes 213024 | tf_op jit(solution)/shard_map/ppermute | solution.py:78
  107.4 0.3 collective-permute-done.35.first_ref
  107.7 3.9 %shard_map.83.after = f32[128,6912]{1,0:T(8,128)} custom-call(s32[4]{0:T(128)S(1)} %pad_add_fusion.place_ref, bf16[4,432,128]{2,1,0:T(8,128)(2,1)S(1)} %shard_map.79.after.m_ref, bf16[4,432,128]{2,1,0:T(8,128)(2,1)S(1)} %collective-permute-done.31.x_ref.mx_ref, bf16[4,432,128]{2,1,0:T(8,128)(2,1)S(1)} %collective-permute-done.32.y_ref.my_ref, ...), custom_call_target="tpu_custom_call" | custom-call | bytes 6000000 | tf_op jit(solution)/shard_map/pallas_call | solution.py:470
  111.7 2.0 %copy-done = f32[128,6912]{1,0:T(8,128)S(1)} copy-done((f32[128,6912]{1,0:T(8,128)S(1)}, f32[128,6912]{1,0:T(8,128)}, u32[]{:S(2)}) %copy-start) | copy-done | bytes 3538968
  113.7 1.5 %collective-permute-start.37 = (bf16[4,224,128]{2,1,0:T(8,128)(2,1)S(1)}, bf16[4,224,128]{2,1,0:T(8,128)(2,1)S(1)}, u32[]{:S(2)}, u32[]{:S(2)}) collective-permute-start(bf16[4,224,128]{2,1,0:T(8,128)(2,1)S(1)} %get-tuple-element.87), channel_id=1, source_target_pairs={{0,4},{2,6},{4,0},{6,2},{8,12},{10,14},{12,8},{14,10},{16,20},{18,... | collective-permute-start | bytes 688136 | tf_op jit(solution)/shard_map/ppermute | solution.py:78
  115.2 0.9 collective-permute-start.38
  116.1 4.9 %collective-permute-done.38.last_ref = bf16[4,208,128]{2,1,0:T(8,128)(2,1)S(1)} collective-permute-done((bf16[4,208,128]{2,1,0:T(8,128)(2,1)S(1)}, bf16[4,208,128]{2,1,0:T(8,128)(2,1)S(1)}, u32[]{:S(2)}, u32[]{:S(2)}) %collective-permute-start.38) | collective-permute-done | bytes 213024 | tf_op jit(solution)/shard_map/ppermute | solution.py:78
  121.0 4.0 %shard_map.85 = f32[128,6912]{1,0:T(8,128)} custom-call(s32[4]{0:T(128)S(1)} %pad_add_fusion.place_ref, bf16[4,432,128]{2,1,0:T(8,128)(2,1)S(1)} %shard_map.82.m_ref, bf16[4,432,128]{2,1,0:T(8,128)(2,1)S(1)} %collective-permute-done.33.x_ref.mx_ref, bf16[4,432,128]{2,1,0:T(8,128)(2,1)S(1)} %collective-permute-done.34.y_ref.my_ref, ...), custom_call_target="tpu_custom_call" | custom-call | bytes 6000000 | tf_op jit(solution)/shard_map/pallas_call | solution.py:470
  (46 shorter events, 1.8 us)
Async XLA Ops:
  0.6 0.9 copy-start.4
  1.5 0.9 copy-start.5
  3.1 13.7 %collective-permute-start = (bf16[8,64,256]{2,1,0:T(8,128)(2,1)S(1)}, bf16[8,64,256]{2,1,0:T(8,128)(2,1)S(1)}, u32[]{:S(2)}, u32[]{:S(2)}) collective-permute-start(bf16[8,64,256]{2,1,0:T(8,128)(2,1)S(1)} %get-tuple-element.46.fc_ref), channel_id=1, source_target_pairs={{0,1},{1,0},{2,3},{3,2},{4,5},{5,4},{6,7},{7,6},{8,9},{9,8},{10,11... | collective-permute-start | bytes 786440 | tf_op jit(solution)/shard_map/ppermute | solution.py:98
  3.6 11.7 %collective-permute-start.1 = (bf16[3,64,256]{2,1,0:T(8,128)(2,1)S(1)}, bf16[3,64,256]{2,1,0:T(8,128)(2,1)S(1)}, u32[]{:S(2)}, u32[]{:S(2)}) collective-permute-start(bf16[3,64,256]{2,1,0:T(8,128)(2,1)S(1)} %get-tuple-element.47), channel_id=1, source_target_pairs={{0,2},{1,3},{2,4},{3,5},{4,6},{5,7},{6,8},{7,9},{8,10},{9,11},{10,... | collective-permute-start | bytes 294920 | tf_op jit(solution)/shard_map/ppermute | solution.py:98
  6.1 9.3 %collective-permute-start.3 = (bf16[3,64,256]{2,1,0:T(8,128)(2,1)S(1)}, bf16[3,64,256]{2,1,0:T(8,128)(2,1)S(1)}, u32[]{:S(2)}, u32[]{:S(2)}) collective-permute-start(bf16[3,64,256]{2,1,0:T(8,128)(2,1)S(1)} %get-tuple-element.48.after), channel_id=1, source_target_pairs={{0,30},{1,31},{2,0},{3,1},{4,2},{5,3},{6,4},{7,5},{8,6},{9,7},{10,... | collective-permute-start | bytes 294920 | tf_op jit(solution)/shard_map/ppermute | solution.py:98
  10.2 1.5 %copy-start.1 = (bf16[128,6912]{1,0:T(8,128)(2,1)S(1)}, bf16[128,6912]{1,0:T(8,128)(2,1)}, u32[]{:S(2)}) copy-start(bf16[128,6912]{1,0:T(8,128)(2,1)} %w1_ref.1) | copy-start | bytes 5308420
  11.7 1.5 %copy-start.2 = (bf16[128,6912]{1,0:T(8,128)(2,1)S(1)}, bf16[128,6912]{1,0:T(8,128)(2,1)}, u32[]{:S(2)}) copy-start(bf16[128,6912]{1,0:T(8,128)(2,1)} %w2_ref.1) | copy-start | bytes 5308420
  15.3 1.4 %collective-permute-start.2 = (bf16[3,64,256]{2,1,0:T(8,128)(2,1)S(1)}, bf16[3,64,256]{2,1,0:T(8,128)(2,1)S(1)}, u32[]{:S(2)}, u32[]{:S(2)}) collective-permute-start(bf16[3,64,256]{2,1,0:T(8,128)(2,1)S(1)} %collective-permute-done.1.up_same), channel_id=1, source_target_pairs={{0,1},{1,0},{2,3},{3,2},{4,5},{5,4},{6,7},{7,6},{8,9},{9,8},{10,11... | collective-permute-start | bytes 294920 | tf_op jit(solution)/shard_map/ppermute | solution.py:98
  15.4 1.4 %collective-permute-start.4 = (bf16[3,64,256]{2,1,0:T(8,128)(2,1)S(1)}, bf16[3,64,256]{2,1,0:T(8,128)(2,1)S(1)}, u32[]{:S(2)}, u32[]{:S(2)}) collective-permute-start(bf16[3,64,256]{2,1,0:T(8,128)(2,1)S(1)} %collective-permute-done.3.down_same), channel_id=1, source_target_pairs={{0,1},{1,0},{2,3},{3,2},{4,5},{5,4},{6,7},{7,6},{8,9},{9,8},{10,11... | collective-permute-start | bytes 294920 | tf_op jit(solution)/shard_map/ppermute | solution.py:98
  20.7 1.7 %collective-permute-start.5 = (bf16[1280,128]{1,0:T(8,128)(2,1)S(1)}, bf16[1280,128]{1,0:T(8,128)(2,1)S(1)}, u32[]{:S(2)}, u32[]{:S(2)}) collective-permute-start(bf16[1280,128]{1,0:T(8,128)(2,1)S(1)} %get-tuple-element.53.send_ref), channel_id=1, source_target_pairs={{0,1},{1,0},{2,3},{3,2},{4,5},{5,4},{6,7},{7,6},{8,9},{9,8},{10,11... | collective-permute-start | bytes 983048 | tf_op jit(solution)/shard_map/ppermute | solution.py:98
  24.3 8.3 %collective-permute-start.7 = (bf16[4,224,128]{2,1,0:T(8,128)(2,1)S(1)}, bf16[4,224,128]{2,1,0:T(8,128)(2,1)S(1)}, u32[]{:S(2)}, u32[]{:S(2)}) collective-permute-start(bf16[4,224,128]{2,1,0:T(8,128)(2,1)S(1)} %get-tuple-element.60), channel_id=1, source_target_pairs={{0,2},{2,0},{4,6},{6,4},{8,10},{10,8},{12,14},{14,12},{16,18},{18,... | collective-permute-start | bytes 688136 | tf_op jit(solution)/shard_map/ppermute | solution.py:78
  24.4 8.2 %collective-permute-start.8 = (bf16[4,208,128]{2,1,0:T(8,128)(2,1)S(1)}, bf16[4,208,128]{2,1,0:T(8,128)(2,1)S(1)}, u32[]{:S(2)}, u32[]{:S(2)}) collective-permute-start(bf16[4,208,128]{2,1,0:T(8,128)(2,1)S(1)} %get-tuple-element.62), channel_id=1, source_target_pairs={{0,4},{2,6},{4,0},{6,2},{8,12},{10,14},{12,8},{14,10},{16,20},{18,... | collective-permute-start | bytes 638984 | tf_op jit(solution)/shard_map/ppermute | solution.py:78
  24.7 14.0 %collective-permute-start.15 = (bf16[4,208,128]{2,1,0:T(8,128)(2,1)S(1)}, bf16[4,208,128]{2,1,0:T(8,128)(2,1)S(1)}, u32[]{:S(2)}, u32[]{:S(2)}) collective-permute-start(bf16[4,208,128]{2,1,0:T(8,128)(2,1)S(1)} %get-tuple-element.73), channel_id=1, source_target_pairs={{0,4},{2,6},{4,0},{6,2},{8,12},{10,14},{12,8},{14,10},{16,20},{18,... | collective-permute-start | bytes 638984 | tf_op jit(solution)/shard_map/ppermute | solution.py:78
  28.5 8.1 %collective-permute-start.6 = (bf16[4,64,128]{2,1,0:T(8,128)(2,1)S(1)}, bf16[4,64,128]{2,1,0:T(8,128)(2,1)S(1)}, u32[]{:S(2)}, u32[]{:S(2)}) collective-permute-start(bf16[4,64,128]{2,1,0:T(8,128)(2,1)S(1)} %get-tuple-element.56), channel_id=1, source_target_pairs={{0,1},{1,0},{2,3},{3,2},{4,5},{5,4},{6,7},{7,6},{8,9},{9,8},{10,11... | collective-permute-start | bytes 196616 | tf_op jit(solution)/shard_map/ppermute | solution.py:98
  28.5 10.6 %collective-permute-start.12 = (bf16[4,224,128]{2,1,0:T(8,128)(2,1)S(1)}, bf16[4,224,128]{2,1,0:T(8,128)(2,1)S(1)}, u32[]{:S(2)}, u32[]{:S(2)}) collective-permute-start(bf16[4,224,128]{2,1,0:T(8,128)(2,1)S(1)} %get-tuple-element.71), channel_id=1, source_target_pairs={{0,2},{2,0},{4,6},{6,4},{8,10},{10,8},{12,14},{14,12},{16,18},{18,... | collective-permute-start | bytes 688136 | tf_op jit(solution)/shard_map/ppermute | solution.py:78
  32.7 9.4 %collective-permute-start.13 = (bf16[4,208,128]{2,1,0:T(8,128)(2,1)S(1)}, bf16[4,208,128]{2,1,0:T(8,128)(2,1)S(1)}, u32[]{:S(2)}, u32[]{:S(2)}) collective-permute-start(bf16[4,208,128]{2,1,0:T(8,128)(2,1)S(1)} %get-tuple-element.63.after), channel_id=1, source_target_pairs={{0,2},{2,0},{4,6},{6,4},{8,10},{10,8},{12,14},{14,12},{16,18},{18,... | collective-permute-start | bytes 638984 | tf_op jit(solution)/shard_map/ppermute | solution.py:78
  34.7 8.5 %collective-permute-start.14 = (bf16[4,224,128]{2,1,0:T(8,128)(2,1)S(1)}, bf16[4,224,128]{2,1,0:T(8,128)(2,1)S(1)}, u32[]{:S(2)}, u32[]{:S(2)}) collective-permute-start(bf16[4,224,128]{2,1,0:T(8,128)(2,1)S(1)} %get-tuple-element.72), channel_id=1, source_target_pairs={{0,4},{2,6},{4,0},{6,2},{8,12},{10,14},{12,8},{14,10},{16,20},{18,... | collective-permute-start | bytes 688136 | tf_op jit(solution)/shard_map/ppermute | solution.py:78
  36.6 10.2 %collective-permute-start.11 = (bf16[4,208,128]{2,1,0:T(8,128)(2,1)S(1)}, bf16[4,208,128]{2,1,0:T(8,128)(2,1)S(1)}, u32[]{:S(2)}, u32[]{:S(2)}) collective-permute-start(bf16[4,208,128]{2,1,0:T(8,128)(2,1)S(1)} %get-tuple-element.69), channel_id=1, source_target_pairs={{0,4},{2,6},{4,0},{6,2},{8,12},{10,14},{12,8},{14,10},{16,20},{18,... | collective-permute-start | bytes 638984 | tf_op jit(solution)/shard_map/ppermute | solution.py:78
  38.7 9.5 %collective-permute-start.10 = (bf16[4,224,128]{2,1,0:T(8,128)(2,1)S(1)}, bf16[4,224,128]{2,1,0:T(8,128)(2,1)S(1)}, u32[]{:S(2)}, u32[]{:S(2)}) collective-permute-start(bf16[4,224,128]{2,1,0:T(8,128)(2,1)S(1)} %get-tuple-element.67), channel_id=1, source_target_pairs={{0,2},{2,0},{4,6},{6,4},{8,10},{10,8},{12,14},{14,12},{16,18},{18,... | collective-permute-start | bytes 688136 | tf_op jit(solution)/shard_map/ppermute | solution.py:78
  39.1 19.8 %collective-permute-start.9 = (bf16[4,224,128]{2,1,0:T(8,128)(2,1)S(1)}, bf16[4,224,128]{2,1,0:T(8,128)(2,1)S(1)}, u32[]{:S(2)}, u32[]{:S(2)}) collective-permute-start(bf16[4,224,128]{2,1,0:T(8,128)(2,1)S(1)} %get-tuple-element.65), channel_id=1, source_target_pairs={{0,2},{2,0},{4,6},{6,4},{8,10},{10,8},{12,14},{14,12},{16,18},{18,... | collective-permute-start | bytes 688136 | tf_op jit(solution)/shard_map/ppermute | solution.py:78
  43.2 0.9 copy-start.3
  44.3 6.6 %collective-permute-start.19 = (bf16[432,128]{1,0:T(8,128)(2,1)S(1)}, bf16[432,128]{1,0:T(8,128)(2,1)S(1)}, u32[]{:S(2)}, u32[]{:S(2)}) collective-permute-start(bf16[432,128]{1,0:T(8,128)(2,1)S(1)} %get-tuple-element.78), channel_id=1, source_target_pairs={{0,8},{2,10},{4,12},{6,14},{8,16},{10,18},{12,20},{14,22},{16,24},... | collective-permute-start | bytes 331784 | tf_op jit(solution)/shard_map/ppermute | solution.py:78
  44.4 9.9 %collective-permute-start.20 = (bf16[432,128]{1,0:T(8,128)(2,1)S(1)}, bf16[432,128]{1,0:T(8,128)(2,1)S(1)}, u32[]{:S(2)}, u32[]{:S(2)}) collective-permute-start(bf16[432,128]{1,0:T(8,128)(2,1)S(1)} %get-tuple-element.79), channel_id=1, source_target_pairs={{0,16},{2,18},{4,20},{6,22},{8,24},{10,26},{12,28},{14,30},{16,0},... | collective-permute-start | bytes 331784 | tf_op jit(solution)/shard_map/ppermute | solution.py:78
  46.8 9.6 %collective-permute-start.18 = (bf16[4,208,128]{2,1,0:T(8,128)(2,1)S(1)}, bf16[4,208,128]{2,1,0:T(8,128)(2,1)S(1)}, u32[]{:S(2)}, u32[]{:S(2)}) collective-permute-start(bf16[4,208,128]{2,1,0:T(8,128)(2,1)S(1)} %get-tuple-element.77), channel_id=1, source_target_pairs={{0,4},{2,6},{4,0},{6,2},{8,12},{10,14},{12,8},{14,10},{16,20},{18,... | collective-permute-start | bytes 638984 | tf_op jit(solution)/shard_map/ppermute | solution.py:78
  48.3 12.4 %collective-permute-start.17 = (bf16[4,224,128]{2,1,0:T(8,128)(2,1)S(1)}, bf16[4,224,128]{2,1,0:T(8,128)(2,1)S(1)}, u32[]{:S(2)}, u32[]{:S(2)}) collective-permute-start(bf16[4,224,128]{2,1,0:T(8,128)(2,1)S(1)} %get-tuple-element.76), channel_id=1, source_target_pairs={{0,4},{2,6},{4,0},{6,2},{8,12},{10,14},{12,8},{14,10},{16,20},{18,... | collective-permute-start | bytes 688136 | tf_op jit(solution)/shard_map/ppermute | solution.py:78
  51.0 4.7 %collective-permute-start.21 = (bf16[432,128]{1,0:T(8,128)(2,1)S(1)}, bf16[432,128]{1,0:T(8,128)(2,1)S(1)}, u32[]{:S(2)}, u32[]{:S(2)}) collective-permute-start(bf16[432,128]{1,0:T(8,128)(2,1)S(1)} %get-tuple-element.80), channel_id=1, source_target_pairs={{0,24},{2,26},{4,28},{6,30},{8,0},{10,2},{12,4},{14,6},{16,8},{18,... | collective-permute-start | bytes 331784 | tf_op jit(solution)/shard_map/ppermute | solution.py:78
  54.3 6.4 %collective-permute-start.16 = (bf16[4,208,128]{2,1,0:T(8,128)(2,1)S(1)}, bf16[4,208,128]{2,1,0:T(8,128)(2,1)S(1)}, u32[]{:S(2)}, u32[]{:S(2)}) collective-permute-start(bf16[4,208,128]{2,1,0:T(8,128)(2,1)S(1)} %get-tuple-element.75.after), channel_id=1, source_target_pairs={{0,2},{2,0},{4,6},{6,4},{8,10},{10,8},{12,14},{14,12},{16,18},{18,... | collective-permute-start | bytes 638984 | tf_op jit(solution)/shard_map/ppermute | solution.py:78
  55.8 6.8 %collective-permute-start.27 = (bf16[432,128]{1,0:T(8,128)(2,1)S(1)}, bf16[432,128]{1,0:T(8,128)(2,1)S(1)}, u32[]{:S(2)}, u32[]{:S(2)}) collective-permute-start(bf16[432,128]{1,0:T(8,128)(2,1)S(1)} %shard_map.77.after.one), channel_id=1, source_target_pairs={{0,8},{2,10},{4,12},{6,14},{8,16},{10,18},{12,20},{14,22},{16,24},... | collective-permute-start | bytes 331784 | tf_op jit(solution)/shard_map/ppermute | solution.py:78
  56.4 9.3 %collective-permute-start.26 = (bf16[432,128]{1,0:T(8,128)(2,1)S(1)}, bf16[432,128]{1,0:T(8,128)(2,1)S(1)}, u32[]{:S(2)}, u32[]{:S(2)}) collective-permute-start(bf16[432,128]{1,0:T(8,128)(2,1)S(1)} %shard_map.77.after.one), channel_id=1, source_target_pairs={{0,16},{2,18},{4,20},{6,22},{8,24},{10,26},{12,28},{14,30},{16,0},... | collective-permute-start | bytes 331784 | tf_op jit(solution)/shard_map/ppermute | solution.py:78
  58.9 6.8 %collective-permute-start.25 = (bf16[432,128]{1,0:T(8,128)(2,1)S(1)}, bf16[432,128]{1,0:T(8,128)(2,1)S(1)}, u32[]{:S(2)}, u32[]{:S(2)}) collective-permute-start(bf16[432,128]{1,0:T(8,128)(2,1)S(1)} %shard_map.77.after.one), channel_id=1, source_target_pairs={{0,24},{2,26},{4,28},{6,30},{8,0},{10,2},{12,4},{14,6},{16,8},{18,... | collective-permute-start | bytes 331784 | tf_op jit(solution)/shard_map/ppermute | solution.py:78
  65.7 18.8 %collective-permute-start.32 = (bf16[4,432,128]{2,1,0:T(8,128)(2,1)S(1)}, bf16[4,432,128]{2,1,0:T(8,128)(2,1)S(1)}, u32[]{:S(2)}, u32[]{:S(2)}) collective-permute-start(bf16[4,432,128]{2,1,0:T(8,128)(2,1)S(1)} %shard_map.79.after.m_ref), channel_id=1, source_target_pairs={{0,4},{2,6},{4,0},{6,2},{8,12},{10,14},{12,8},{14,10},{16,20},{18,... | collective-permute-start | bytes 1327112 | tf_op jit(solution)/shard_map/ppermute | solution.py:78
  66.7 17.7 %collective-permute-start.31 = (bf16[4,432,128]{2,1,0:T(8,128)(2,1)S(1)}, bf16[4,432,128]{2,1,0:T(8,128)(2,1)S(1)}, u32[]{:S(2)}, u32[]{:S(2)}) collective-permute-start(bf16[4,432,128]{2,1,0:T(8,128)(2,1)S(1)} %shard_map.79.after.m_ref), channel_id=1, source_target_pairs={{0,2},{2,0},{4,6},{6,4},{8,10},{10,8},{12,14},{14,12},{16,18},{18,... | collective-permute-start | bytes 1327112 | tf_op jit(solution)/shard_map/ppermute | solution.py:78
  67.8 7.8 %collective-permute-start.22 = (bf16[432,128]{1,0:T(8,128)(2,1)S(1)}, bf16[432,128]{1,0:T(8,128)(2,1)S(1)}, u32[]{:S(2)}, u32[]{:S(2)}) collective-permute-start(bf16[432,128]{1,0:T(8,128)(2,1)S(1)} %get-tuple-element.82), channel_id=1, source_target_pairs={{0,8},{2,10},{4,12},{6,14},{8,16},{10,18},{12,20},{14,22},{16,24},... | collective-permute-start | bytes 331784 | tf_op jit(solution)/shard_map/ppermute | solution.py:78
  70.6 8.4 %collective-permute-start.23 = (bf16[432,128]{1,0:T(8,128)(2,1)S(1)}, bf16[432,128]{1,0:T(8,128)(2,1)S(1)}, u32[]{:S(2)}, u32[]{:S(2)}) collective-permute-start(bf16[432,128]{1,0:T(8,128)(2,1)S(1)} %get-tuple-element.83), channel_id=1, source_target_pairs={{0,16},{2,18},{4,20},{6,22},{8,24},{10,26},{12,28},{14,30},{16,0},... | collective-permute-start | bytes 331784 | tf_op jit(solution)/shard_map/ppermute | solution.py:78
  72.0 7.0 %collective-permute-start.24 = (bf16[432,128]{1,0:T(8,128)(2,1)S(1)}, bf16[432,128]{1,0:T(8,128)(2,1)S(1)}, u32[]{:S(2)}, u32[]{:S(2)}) collective-permute-start(bf16[432,128]{1,0:T(8,128)(2,1)S(1)} %get-tuple-element.84), channel_id=1, source_target_pairs={{0,24},{2,26},{4,28},{6,30},{8,0},{10,2},{12,4},{14,6},{16,8},{18,... | collective-permute-start | bytes 331784 | tf_op jit(solution)/shard_map/ppermute | solution.py:78
  79.1 7.7 %collective-permute-start.30 = (bf16[432,128]{1,0:T(8,128)(2,1)S(1)}, bf16[432,128]{1,0:T(8,128)(2,1)S(1)}, u32[]{:S(2)}, u32[]{:S(2)}) collective-permute-start(bf16[432,128]{1,0:T(8,128)(2,1)S(1)} %shard_map.80.after.one), channel_id=1, source_target_pairs={{0,8},{2,10},{4,12},{6,14},{8,16},{10,18},{12,20},{14,22},{16,24},... | collective-permute-start | bytes 331784 | tf_op jit(solution)/shard_map/ppermute | solution.py:78
  82.0 8.7 %collective-permute-start.29 = (bf16[432,128]{1,0:T(8,128)(2,1)S(1)}, bf16[432,128]{1,0:T(8,128)(2,1)S(1)}, u32[]{:S(2)}, u32[]{:S(2)}) collective-permute-start(bf16[432,128]{1,0:T(8,128)(2,1)S(1)} %shard_map.80.after.one), channel_id=1, source_target_pairs={{0,16},{2,18},{4,20},{6,22},{8,24},{10,26},{12,28},{14,30},{16,0},... | collective-permute-start | bytes 331784 | tf_op jit(solution)/shard_map/ppermute | solution.py:78
  83.5 7.2 %collective-permute-start.28 = (bf16[432,128]{1,0:T(8,128)(2,1)S(1)}, bf16[432,128]{1,0:T(8,128)(2,1)S(1)}, u32[]{:S(2)}, u32[]{:S(2)}) collective-permute-start(bf16[432,128]{1,0:T(8,128)(2,1)S(1)} %shard_map.80.after.one), channel_id=1, source_target_pairs={{0,24},{2,26},{4,28},{6,30},{8,0},{10,2},{12,4},{14,6},{16,8},{18,... | collective-permute-start | bytes 331784 | tf_op jit(solution)/shard_map/ppermute | solution.py:78
  90.7 20.9 %collective-permute-start.34 = (bf16[4,432,128]{2,1,0:T(8,128)(2,1)S(1)}, bf16[4,432,128]{2,1,0:T(8,128)(2,1)S(1)}, u32[]{:S(2)}, u32[]{:S(2)}) collective-permute-start(bf16[4,432,128]{2,1,0:T(8,128)(2,1)S(1)} %shard_map.82.m_ref), channel_id=1, source_target_pairs={{0,4},{2,6},{4,0},{6,2},{8,12},{10,14},{12,8},{14,10},{16,20},{18,... | collective-permute-start | bytes 1327112 | tf_op jit(solution)/shard_map/ppermute | solution.py:78
  91.1 20.5 %collective-permute-start.33 = (bf16[4,432,128]{2,1,0:T(8,128)(2,1)S(1)}, bf16[4,432,128]{2,1,0:T(8,128)(2,1)S(1)}, u32[]{:S(2)}, u32[]{:S(2)}) collective-permute-start(bf16[4,432,128]{2,1,0:T(8,128)(2,1)S(1)} %shard_map.82.m_ref), channel_id=1, source_target_pairs={{0,2},{2,0},{4,6},{6,4},{8,10},{10,8},{12,14},{14,12},{16,18},{18,... | collective-permute-start | bytes 1327112 | tf_op jit(solution)/shard_map/ppermute | solution.py:78
  92.1 15.6 %collective-permute-start.35 = (bf16[4,224,128]{2,1,0:T(8,128)(2,1)S(1)}, bf16[4,224,128]{2,1,0:T(8,128)(2,1)S(1)}, u32[]{:S(2)}, u32[]{:S(2)}) collective-permute-start(bf16[4,224,128]{2,1,0:T(8,128)(2,1)S(1)} %get-tuple-element.86), channel_id=1, source_target_pairs={{0,4},{2,6},{4,0},{6,2},{8,12},{10,14},{12,8},{14,10},{16,20},{18,... | collective-permute-start | bytes 688136 | tf_op jit(solution)/shard_map/ppermute | solution.py:78
  93.8 13.7 %collective-permute-start.36 = (bf16[4,208,128]{2,1,0:T(8,128)(2,1)S(1)}, bf16[4,208,128]{2,1,0:T(8,128)(2,1)S(1)}, u32[]{:S(2)}, u32[]{:S(2)}) collective-permute-start(bf16[4,208,128]{2,1,0:T(8,128)(2,1)S(1)} %get-tuple-element.85.after), channel_id=1, source_target_pairs={{0,2},{2,0},{4,6},{6,4},{8,10},{10,8},{12,14},{14,12},{16,18},{18,... | collective-permute-start | bytes 638984 | tf_op jit(solution)/shard_map/ppermute | solution.py:78
  111.7 2.0 %copy-start = (f32[128,6912]{1,0:T(8,128)S(1)}, f32[128,6912]{1,0:T(8,128)}, u32[]{:S(2)}) copy-start(f32[128,6912]{1,0:T(8,128)} %shard_map.83.after) | copy-start | bytes 10616836
  113.7 7.3 %collective-permute-start.37 = (bf16[4,224,128]{2,1,0:T(8,128)(2,1)S(1)}, bf16[4,224,128]{2,1,0:T(8,128)(2,1)S(1)}, u32[]{:S(2)}, u32[]{:S(2)}) collective-permute-start(bf16[4,224,128]{2,1,0:T(8,128)(2,1)S(1)} %get-tuple-element.87), channel_id=1, source_target_pairs={{0,4},{2,6},{4,0},{6,2},{8,12},{10,14},{12,8},{14,10},{16,20},{18,... | collective-permute-start | bytes 688136 | tf_op jit(solution)/shard_map/ppermute | solution.py:78
  115.2 5.8 %collective-permute-start.38 = (bf16[4,208,128]{2,1,0:T(8,128)(2,1)S(1)}, bf16[4,208,128]{2,1,0:T(8,128)(2,1)S(1)}, u32[]{:S(2)}, u32[]{:S(2)}) collective-permute-start(bf16[4,208,128]{2,1,0:T(8,128)(2,1)S(1)} %get-tuple-element.88), channel_id=1, source_target_pairs={{0,2},{2,0},{4,6},{6,4},{8,10},{10,8},{12,14},{14,12},{16,18},{18,... | collective-permute-start | bytes 638984 | tf_op jit(solution)/shard_map/ppermute | solution.py:78

commit v2 on v1

--- a/solution.py
+++ b/solution.py
@@ -35,6 +35,10 @@
 
 def anywhere():
     return pl.BlockSpec(memory_space=pl.ANY)
+
+
+def in_hbm():
+    return pl.BlockSpec(memory_space=pltpu.HBM)
 
 
 def smem():
@@ -176,7 +180,7 @@
             shape((3, HALF, CH)),
             shape((3, HALF, CH)),
         ],
-        in_specs=[anywhere()] * 2,
+        in_specs=[in_hbm()] * 2,
         out_specs=[vmem()] * 3,
         scratch_shapes=[pltpu.SemaphoreType.DMA((6,))],
         compiler_params=params(),
@@ -202,7 +206,7 @@
     return pl.pallas_call(
         load_kernel,
         out_shape=[shape(w_first.shape), shape(w_second.shape)],
-        in_specs=[anywhere()] * 3,
+        in_specs=[in_hbm()] * 2 + [anywhere()],
         out_specs=[vmem()] * 2,
         scratch_shapes=[pltpu.SemaphoreType.DMA((2, 4))],
         compiler_params=params(),
@@ -288,7 +292,7 @@
     own_x = place_ref[1]
     own_y = place_ref[2]
     own_z = place_ref[3]
-    keep, y_first, y_last, x_first, x_last, d_first, d_last = outs
+    keep, y_first, x_last, x_both, y_both = outs
     lane = lax.broadcasted_iota(jnp.int32, (LANES, NRZ), 1)
     z = lane % AXIAL
     r = lane // AXIAL
@@ -324,16 +328,16 @@
                 bottom = halves[dx][HALF:]
                 parts = (jnp.where(y_zero, top, bottom), jnp.where(y_zero, bottom, top))
                 for dy in range(2):
+                    early = tap < FIRST_TAPS
+                    row = (tap if early else tap - FIRST_TAPS) * BLOCK
                     if dx == 0 and dy == 0:
                         ref, row = keep, tap * BLOCK
+                    elif dx == 1 and dy == 1:
+                        ref = x_both if early else y_both
+                    elif dx == 1:
+                        ref, row = (x_both, FIRST + row) if early else (x_last, row)
                     else:
-                        pair = {(1, 0): (x_first, x_last), (0, 1): (y_first, y_last)}.get(
-                            (dx, dy), (d_first, d_last)
-                        )
-                        if tap < FIRST_TAPS:
-                            ref, row = pair[0], tap * BLOCK
-                        else:
-                            ref, row = pair[1], (tap - FIRST_TAPS) * BLOCK
+                        ref, row = (y_first, row) if early else (y_both, LAST + row)
                     narrow = parts[dy].astype(BF16)
                     for index in range(4):
                         ref[slots[index], row : row + BLOCK, :] = narrow[
@@ -342,7 +346,7 @@
 
 
 def second_kernel(factor, place_ref, cot_ref, send_ref, got_ref, h_ref, *rest):
-    outs, turned_ref = rest[:7], rest[7]
+    outs, turned_ref = rest[:5], rest[5]
     rows = (LAYERS + 2) * NRZ
     own = place_ref[0]
     mine = send_ref[:rows, :].astype(F32)
@@ -356,7 +360,7 @@
 
 
 def first_kernel(factor, place_ref, back_ref, got_ref, slope_ref, x_ref, after, *rest):
-    outs, turned_ref = rest[:7], rest[7]
+    outs, turned_ref = rest[:5], rest[5]
     rows = (LAYERS + 2) * NRZ
     source = (back_ref[...] + got_ref[rows:, :].astype(F32)) * slope_ref[...]
     source = source.astype(BF16).astype(F32)
@@ -365,7 +369,7 @@
 
 
 def piece_shapes():
-    return [shape((4, ROWS, LANES))] + [shape((4, FIRST, LANES)), shape((4, LAST, LANES))] * 3
+    return [shape((4, rows, LANES)) for rows in (ROWS, FIRST, LAST, 2 * FIRST, 2 * LAST)]
 
 
 def second_grad(place, factor, cot, send, got):
@@ -373,7 +377,7 @@
         functools.partial(second_kernel, factor),
         out_shape=[shape(((LAYERS + 2) * NRZ, CH))] + piece_shapes(),
         in_specs=[smem()] + [vmem()] * 3,
-        out_specs=[vmem()] * 8,
+        out_specs=[vmem()] * 6,
         scratch_shapes=[pltpu.VMEM((9 * LANES, LAYERS * NRZ), BF16)],
         compiler_params=params(),
         cost_estimate=cost(1000000000, 3000000),
@@ -386,7 +390,7 @@
         functools.partial(first_kernel, factor),
         out_shape=piece_shapes(),
         in_specs=[smem()] + [vmem()] * 4 + [anywhere()],
-        out_specs=[vmem()] * 7,
+        out_specs=[vmem()] * 5,
         scratch_shapes=[pltpu.VMEM((9 * LANES, LAYERS * NRZ), BF16)],
         compiler_params=params(),
         cost_estimate=cost(1000000000, 3000000),
@@ -414,7 +418,8 @@
     )(place, x, h, w_second)
 
 
-def join_kernel(place_ref, mine_ref, theirs_ref, out_ref):
+def join_kernel(place_ref, mine_ref, theirs_ref, out_ref, token_ref):
+    token_ref[...] = jnp.zeros_like(token_ref)
     mine = mine_ref[...].astype(F32)
     theirs = theirs_ref[...].astype(F32)
     first = jnp.broadcast_to(place_ref[0], mine.shape) == 0
@@ -425,66 +430,63 @@
 def join_flow(place, mine, theirs):
     return pl.pallas_call(
         join_kernel,
-        out_shape=shape((LAYERS, HALF, CH)),
+        out_shape=[shape((LAYERS, HALF, CH)), shape((8, LANES), F32)],
         in_specs=[smem()] + [vmem()] * 2,
-        out_specs=vmem(),
+        out_specs=[vmem()] * 2,
         compiler_params=params(),
         cost_estimate=cost(0, 400000),
     )(place, mine, theirs)
 
 
-def write_kernel(place_ref, m_ref, mx_ref, my_ref, first_ref, last_ref, out_ref):
+def write_kernel(
+    place_ref, m_ref, mx_ref, my_ref, first_ref, last_ref, after, out_ref, token_ref, block_ref, sems
+):
+    token_ref[...] = jnp.zeros_like(token_ref)
     x_zero = jnp.broadcast_to(place_ref[1], (BLOCK, LANES)) == 0
-    far = pl.program_id(0)
-
-    def put(tap, near, across):
-        low = jnp.where(x_zero, near, across)
-        high = jnp.where(x_zero, across, near)
-        out_ref[:, tap * CH : tap * CH + LANES] = low
-        out_ref[:, tap * CH + LANES : (tap + 1) * CH] = high
-
-    @pl.when(far == 0)
-    def _():
-        for tap in range(TAPS):
-            rows = slice(tap * BLOCK, (tap + 1) * BLOCK)
-            put(tap, m_ref[0, rows, :].astype(F32), mx_ref[0, rows, :].astype(F32))
-
-    @pl.when(far == 1)
-    def _():
-        for tap in range(TAPS):
-            rows = slice(tap * BLOCK, (tap + 1) * BLOCK)
-            if tap < FIRST_TAPS:
-                across = first_ref[0, rows, :]
-            else:
-                across = last_ref[0, (tap - FIRST_TAPS) * BLOCK : (tap - FIRST_TAPS + 1) * BLOCK, :]
-            put(tap, my_ref[0, rows, :].astype(F32), across.astype(F32))
-
-
-def write_out(place, pieces):
-    near = lambda dy, dz, place: (dz * (1 - dy) + 3 * dy, 0, 0)
-    far = lambda dy, dz, place: (dz * dy, 0, 0)
-    block = lambda dy, dz, place: (
-        lax.rem(place[2] + dy, 2) * 4 + lax.rem(place[3] + dz, 4),
-        0,
-    )
+    copies = []
+    for dy in range(2):
+        for dz in range(4):
+            index = dy * 4 + dz
+            for tap in range(TAPS):
+                rows = slice(tap * BLOCK, (tap + 1) * BLOCK)
+                if dy == 0:
+                    near, across = m_ref[dz, rows, :], mx_ref[dz, rows, :]
+                elif tap < FIRST_TAPS:
+                    near, across = my_ref[dz, rows, :], first_ref[dz, rows, :]
+                else:
+                    late = slice((tap - FIRST_TAPS) * BLOCK, (tap - FIRST_TAPS + 1) * BLOCK)
+                    near, across = my_ref[dz, rows, :], last_ref[dz, late, :]
+                near = near.astype(F32)
+                across = across.astype(F32)
+                block_ref[index, :, tap * CH : tap * CH + LANES] = jnp.where(x_zero, near, across)
+                block_ref[index, :, tap * CH + LANES : (tap + 1) * CH] = jnp.where(
+                    x_zero, across, near
+                )
+            row = lax.rem(place_ref[2] + dy, 2) * 4 + lax.rem(place_ref[3] + dz, 4)
+            copy = pltpu.make_async_copy(
+                block_ref.at[index],
+                out_ref.at[pl.ds(pl.multiple_of(row * BLOCK, BLOCK), BLOCK), :],
+                sems.at[index],
+            )
+            copy.start()
+            copies.append(copy)
+    for copy in copies:
+        copy.wait()
+
+
+def write_out(place, pieces, after):
     return pl.pallas_call(
         write_kernel,
-        out_shape=shape((LANES, TAPS * CH), F32),
-        grid_spec=pltpu.PrefetchScalarGridSpec(
-            num_scalar_prefetch=1,
-            grid=(2, 4),
-            in_specs=[
-                pl.BlockSpec((1, ROWS, LANES), near),
-                pl.BlockSpec((1, ROWS, LANES), near),
-                pl.BlockSpec((1, ROWS, LANES), far),
-                pl.BlockSpec((1, FIRST, LANES), far),
-                pl.BlockSpec((1, LAST, LANES), far),
-            ],
-            out_specs=pl.BlockSpec((BLOCK, TAPS * CH), block),
-        ),
+        out_shape=[shape((LANES, TAPS * CH), F32), shape((8, LANES), F32)],
+        in_specs=[smem()] + [vmem()] * 5 + [anywhere()],
+        out_specs=[in_hbm(), vmem()],
+        scratch_shapes=[
+            pltpu.VMEM((8, BLOCK, TAPS * CH), F32),
+            pltpu.SemaphoreType.DMA((8,)),
+        ],
         compiler_params=params(),
         cost_estimate=cost(0, 6000000),
-    )(place, *pieces)
+    )(place, *pieces, after)
 
 
 def plus(*terms):
@@ -494,137 +496,105 @@
     return total.astype(BF16)
 
 
-def meet_kernel(y_first, got_first, x_last, got_last, after, y_out, x_out):
-    y_out[...] = plus(y_first[...], got_first[...])
-    x_out[...] = plus(x_last[...], got_last[...])
-
-
-def meet(y_first, got_first, x_last, got_last, after):
-    return pl.pallas_call(
-        meet_kernel,
-        out_shape=[shape(y_first.shape), shape(x_last.shape)],
-        in_specs=[vmem()] * 4 + [anywhere()],
-        out_specs=[vmem()] * 2,
-        compiler_params=params(),
-        cost_estimate=cost(0, 1300000),
-    )(y_first, got_first, x_last, got_last, after)
-
-
-def sum_kernel(keep, x_first, x_last, y_first, y_last, after, *outs):
-    for index in range(4):
-        for rows, x_part, y_part in (
-            (slice(0, FIRST), x_first, y_first),
-            (slice(FIRST, ROWS), x_last, y_last),
-        ):
-            outs[index][rows, :] = plus(keep[index, rows, :], x_part[index], y_part[index])
-
-
-def sum_quads(keep, x_first, x_last, y_first, y_last, after):
-    return pl.pallas_call(
-        sum_kernel,
-        out_shape=[shape((ROWS, LANES))] * 4,
-        in_specs=[vmem()] * 5 + [anywhere()],
-        out_specs=[vmem()] * 4,
-        compiler_params=params(),
-        cost_estimate=cost(0, 1800000),
-    )(keep, x_first, x_last, y_first, y_last, after)
-
-
-def own_kernel(one, two, three, four, after, out):
-    out[...] = plus(one[...], two[...], three[...], four[...])
-
-
-def own_block(rows, after):
-    return pl.pallas_call(
-        own_kernel,
-        out_shape=shape((ROWS, LANES)),
-        in_specs=[vmem()] * 4 + [anywhere()],
-        out_specs=vmem(),
-        compiler_params=params(),
-        cost_estimate=cost(0, 600000),
-    )(*rows, after)
-
-
-def stack_kernel(one, two, three, four, after, out):
-    for index, ref in enumerate((one, two, three, four)):
-        out[index] = ref[...]
-
-
-def stack_blocks(rows, after):
-    return pl.pallas_call(
-        stack_kernel,
-        out_shape=shape((4, ROWS, LANES)),
-        in_specs=[vmem()] * 4 + [anywhere()],
-        out_specs=vmem(),
-        compiler_params=params(),
-        cost_estimate=cost(0, 900000),
-    )(*rows, after)
-
-
-def relay_kernel(x_ref, y_ref, after, first_ref, last_ref):
-    first_ref[...] = x_ref[:, :FIRST]
-    last_ref[...] = y_ref[:, FIRST:]
-
-
-def relay(across_x, across_y, after):
-    return pl.pallas_call(
-        relay_kernel,
-        out_shape=[shape((4, FIRST, LANES)), shape((4, LAST, LANES))],
-        in_specs=[vmem()] * 2 + [anywhere()],
-        out_specs=[vmem()] * 2,
-        compiler_params=params(),
-        cost_estimate=cost(0, 900000),
-    )(across_x, across_y, after)
-
-
-class QuadSum:
-    def diagonal(self, pieces):
-        self.keep, self.y_first, self.y_last, self.x_first, self.x_last, d_first, d_last = pieces
-        self.got_first = shifted(d_first, "x", 1)
-        self.got_last = shifted(d_last, "y", 1)
-        self.in_x_first = shifted(self.x_first, "x", 1)
-        self.in_y_last = shifted(self.y_last, "y", 1)
-
-    def sides(self, after):
-        y_first, x_last = meet(self.y_first, self.got_first, self.x_last, self.got_last, after)
-        self.in_y_first = shifted(y_first, "y", 1)
-        self.in_x_last = shifted(x_last, "x", 1)
-        return x_last
-
-    def along_z(self, after):
-        rows = sum_quads(
-            self.keep, self.in_x_first, self.in_x_last, self.in_y_first, self.in_y_last, after
-        )
-        self.rows = [rows[0]] + [shifted(rows[by], "z", by) for by in range(1, 4)]
-        return rows[0]
-
-    def back_z(self, after):
-        own = own_block(self.rows, after)
-        self.blocks = [own] + [shifted(own, "z", -by) for by in range(1, 4)]
-        return own
-
-    def back_sides(self, after):
-        self.whole = stack_blocks(self.blocks, after)
-        self.across_x = shifted(self.whole, "x", 1)
-        self.across_y = shifted(self.whole, "y", 1)
-        return self.whole
-
-    def back_diagonal(self, after):
-        first, last = relay(self.across_x, self.across_y, after)
-        self.far_first = shifted(first, "y", 1)
-        self.far_last = shifted(last, "x", 1)
-        return last
-
-    def result(self):
-        return self.whole, self.across_x, self.across_y, self.far_first, self.far_last
+def step_call(body, inputs, outputs, after=()):
+    count = len(inputs)
+
+    def kernel(*refs):
+        body(refs[:count], refs[count + len(after) :])
+
+    return pl.pallas_call(
+        kernel,
+        out_shape=[shape(dims) for dims in outputs],
+        in_specs=[vmem()] * count + [anywhere()] * len(after),
+        out_specs=[vmem()] * len(outputs),
+        compiler_params=params(),
+        cost_estimate=cost(0, 1500000),
+    )(*inputs, *after)
+
+
+WHOLE = (4, ROWS, LANES)
+SINGLE = (ROWS, LANES)
+FIRST_PART = (4, FIRST, LANES)
+LAST_PART = (4, LAST, LANES)
+
+
+def meet(ins, outs):
+    y_first, x_in, x_last, y_in = ins
+    outs[0][...] = plus(y_first[...], x_in[:, :FIRST])
+    outs[1][...] = plus(x_last[...], y_in[:, :LAST])
+
+
+def sum_quads(ins, outs):
+    keep, x_in, x_last, y_first, y_in = ins
+    for index, out in enumerate(outs):
+        out[:FIRST] = plus(keep[index, :FIRST], x_in[index, FIRST:], y_first[index])
+        out[FIRST:] = plus(keep[index, FIRST:], x_last[index], y_in[index, LAST:])
+
+
+def sum_z(ins, outs):
+    outs[0][...] = plus(*[ref[...] for ref in ins])
+
+
+def stack_z(ins, outs):
+    for index, ref in enumerate(ins):
+        outs[0][index] = ref[...]
+
+
+def cut_far(ins, outs):
+    outs[0][...] = ins[0][:, :FIRST]
+    outs[1][...] = ins[1][:, FIRST:]
+
+
+def hand_on(ins, outs):
+    for source, goal in zip(ins, outs):
+        goal[...] = source[...]
+
+
+def both(one, one_in, one_out, two):
+    def body(ins, outs):
+        one(ins[:one_in], outs[:one_out])
+        two(ins[one_in:], outs[one_out:])
+
+    return body
+
+
+def reduce_diagonal(x_both, y_both):
+    return shifted(x_both, "x", 1), shifted(y_both, "y", 1)
+
+
+def reduce_sides(y_first, x_last):
+    return shifted(y_first, "y", 1), shifted(x_last, "x", 1)
+
+
+def reduce_z(rows):
+    return [rows[0]] + [shifted(rows[by], "z", by) for by in range(1, 4)]
+
+
+def gather_z(own):
+    return [own] + [shifted(own, "z", -by) for by in range(1, 4)]
+
+
+def gather_sides(whole):
+    return whole, shifted(whole, "x", 1), shifted(whole, "y", 1)
+
+
+def gather_diagonal(first, last):
+    return shifted(first, "y", 1), shifted(last, "x", 1)
 
 
 def any_reduce_gather(pieces, place):
     extents, _ = az_places(lax.axis_size("az"))
     count = lax.axis_size("az")
-    keep, y_first, y_last, x_first, x_last, d_first, d_last = pieces
+    keep, y_first, x_last, x_both, y_both = pieces
     join = lambda first, last: jnp.concatenate([first, last], axis=1)
-    cut = jnp.stack([keep, join(y_first, y_last), join(x_first, x_last), join(d_first, d_last)])
+    cut = jnp.stack(
+        [
+            keep,
+            join(y_first, y_both[:, LAST:]),
+            join(x_both[:, FIRST:], x_last),
+            join(x_both[:, :FIRST], y_both[:, :LAST]),
+        ]
+    )
     order = ("x", "y", "z")
     full = cut.shape
     cut = cut.reshape([extents[name] for name in order] + [-1, LANES])
@@ -668,27 +638,58 @@
     mine, theirs = flow(place, x, hidden, w_two)
     theirs = neighbour(theirs, 0, 1)
     if quad:
-        one, two = QuadSum(), QuadSum()
-        one.diagonal(second)
-        step = one.sides(mine)
-        two.diagonal(first_grad(place, factor, back, got, slope, x, step))
-        flow_out = join_flow(place, mine, theirs)
-        step = one.along_z(flow_out)
-        step = two.sides(step)
-        step = one.back_z(step)
-        step = two.along_z(step)
-        step = one.back_sides(step)
-        step = two.back_z(step)
-        step = one.back_diagonal(step)
-        step = two.back_sides(step)
-        grad_second = write_out(place, one.result())
-        two.back_diagonal(grad_second)
-        grad_first = write_out(place, two.result())
+        corner = reduce_diagonal(*second[3:])
+        first = first_grad(place, factor, back, got, slope, x, mine)
+        sides = reduce_sides(
+            *step_call(
+                meet,
+                [second[1], corner[0], second[2], corner[1]],
+                [FIRST_PART, LAST_PART],
+                [mine],
+            )
+        )
+        *rows, x_both, y_both = step_call(
+            both(sum_quads, 5, 4, hand_on),
+            [second[0], corner[0], sides[1], sides[0], corner[1], first[3], first[4]],
+            [SINGLE] * 4 + [first[3].shape, first[4].shape],
+        )
+        corner_two = reduce_diagonal(x_both, y_both)
+        rows = reduce_z(rows)
+        flow_out, token = join_flow(place, mine, theirs)
+        own_one, *sides_two = step_call(
+            both(sum_z, 4, 1, meet),
+            [*rows, first[1], corner_two[0], first[2], corner_two[1]],
+            [SINGLE, FIRST_PART, LAST_PART],
+            [token],
+        )
+        sides_two = reduce_sides(*sides_two)
+        blocks = gather_z(own_one)
+        whole, *rows_two = step_call(
+            both(stack_z, 4, 1, sum_quads),
+            [*blocks, first[0], corner_two[0], sides_two[1], sides_two[0], corner_two[1]],
+            [WHOLE] + [SINGLE] * 4,
+        )
+        near = gather_sides(whole)
+        rows_two = reduce_z(rows_two)
+        relay_first, relay_last, own_two = step_call(
+            both(cut_far, 2, 2, sum_z),
+            [near[1], near[2], *rows_two],
+            [FIRST_PART, LAST_PART, SINGLE],
+        )
+        far = gather_diagonal(relay_first, relay_last)
+        blocks_two = gather_z(own_two)
+        (whole_two,) = step_call(stack_z, blocks_two, [WHOLE], far)
+        near_two = gather_sides(whole_two)
+        far_two = gather_diagonal(
+            *step_call(cut_far, [near_two[1], near_two[2]], [FIRST_PART, LAST_PART])
+        )
+        grad_second, token = write_out(place, (*near, *far), whole_two)
+        grad_first, _ = write_out(place, (*near_two, *far_two), token)
     else:
-        flow_out = join_flow(place, mine, theirs)
+        flow_out, _ = join_flow(place, mine, theirs)
         first = first_grad(place, factor, back, got, slope, x, mine)
-        grad_second = write_out(place, any_reduce_gather(second, spot))
-        grad_first = write_out(place, any_reduce_gather(first, spot))
+        grad_second, step = write_out(place, any_reduce_gather(second, spot), mine)
+        grad_first, _ = write_out(place, any_reduce_gather(first, spot), step)
     return (flow_out.transpose(2, 0, 1), grad_first, grad_second)
 
 

time: 125 us -> 121 us (0.968)
  waiting for transfers between devices: 45 us -> 54.1 us
  starting transfers between devices: 49.2 us -> 41 us
  local copies, waits for them, and re-layouts: 7.66 us -> 4.75 us
  Pallas kernels: 22.2 us -> 19.7 us
    ppermute x32 -> x28, waiting for transfers between devices: 42.9 us -> 52 us  [shifted(): return lax.ppermute(value, 'az', pairs)]
    ppermute x32 -> x28, starting transfers between devices: 40.9 us -> 32.8 us  [shifted(): return lax.ppermute(value, 'az', pairs)]
    unnamed x12 -> x8, local copies, waits for them, and re-layouts: 7.66 us -> 4.75 us
    pallas_call x13 -> x10, Pallas kernels: 9.89 us -> 7.47 us  [the longest x2 5.44 us: write_out(): pl.pallas_call(write_kernel, out_shape=[shape((LANES, TAPS * CH), F32), s...]
  transfers between devices with their start and end apart: 39 -> 35, of which waited for: 18 -> 18; matrix products, arithmetic and copies ran while one was open for 0% -> 0% of each run, Pallas kernels for 9% -> 8%
where the time goes in v2:
time: 121 us; the launch traced here: 120 us
  waiting for transfers between devices  54.1 us (45%)
  starting transfers between devices  41 us (34%)
  Pallas kernels  19.7 us (16%)
  local copies, waits for them, and re-layouts  4.75 us (4%)
    ppermute x28, waiting for transfers between devices, shifted(): return lax.ppermute(value, 'az', pairs)  52 us
    ppermute x28, starting transfers between devices, shifted(): return lax.ppermute(value, 'az', pairs)  32.8 us
    ppermute x7, starting transfers between devices, neighbour(): return lax.ppermute(value, ('az', 'grp'), pairs)  8.15 us
    pallas_call x2, Pallas kernels, write_out(): pl.pallas_call(write_kernel, out_shape=[shape((LANES, TAPS * CH), F32), s...  5.44 us
    unnamed x8, local copies, waits for them, and re-layouts  4.75 us
    pallas_call x1, Pallas kernels, fields(): pl.pallas_call(fields_kernel, out_shape=[shape(((LAYERS + 4) * NRZ, CH)),...  3.86 us
  transfers between devices with their start and end apart: 35, of which 18 were waited for; matrix products, arithmetic and copies ran while one was open for 0% of the time, Pallas kernels for 8%

profile of v2, /device:TPU:0, one launch (start us, length us, event | category | flops | bytes accessed | tf_op | source)
XLA Modules:
  0.0 120.4 jit_solution(6296663830948243885)
XLA Ops:
  0.6 0.9 copy-done.2
  1.5 0.9 copy-done.3
  2.4 0.6 shard_map.67
  3.1 0.5 collective-permute-start
  3.6 2.6 %collective-permute-start.1 = (bf16[3,64,256]{2,1,0:T(8,128)(2,1)S(1)}, bf16[3,64,256]{2,1,0:T(8,128)(2,1)S(1)}, u32[]{:S(2)}, u32[]{:S(2)}) collective-permute-start(bf16[3,64,256]{2,1,0:T(8,128)(2,1)S(1)} %get-tuple-element.53), channel_id=1, source_target_pairs={{0,2},{1,3},{2,4},{3,5},{4,6},{5,7},{6,8},{7,9},{8,10},{9,11},{10,... | collective-permute-start | bytes 294920 | tf_op jit(solution)/shard_map/ppermute | solution.py:102
  6.1 4.1 %collective-permute-start.3 = (bf16[3,64,256]{2,1,0:T(8,128)(2,1)S(1)}, bf16[3,64,256]{2,1,0:T(8,128)(2,1)S(1)}, u32[]{:S(2)}, u32[]{:S(2)}) collective-permute-start(bf16[3,64,256]{2,1,0:T(8,128)(2,1)S(1)} %get-tuple-element.54.after), channel_id=1, source_target_pairs={{0,30},{1,31},{2,0},{3,1},{4,2},{5,3},{6,4},{7,5},{8,6},{9,7},{10,... | collective-permute-start | bytes 294920 | tf_op jit(solution)/shard_map/ppermute | solution.py:102
  10.2 1.5 %copy-done = bf16[128,6912]{1,0:T(8,128)(2,1)S(1)} copy-done((bf16[128,6912]{1,0:T(8,128)(2,1)S(1)}, bf16[128,6912]{1,0:T(8,128)(2,1)}, u32[]{:S(2)}) %copy-start) | copy-done | bytes 1769496
  11.7 1.5 %copy-done.1 = bf16[128,6912]{1,0:T(8,128)(2,1)S(1)} copy-done((bf16[128,6912]{1,0:T(8,128)(2,1)S(1)}, bf16[128,6912]{1,0:T(8,128)(2,1)}, u32[]{:S(2)}) %copy-start.1) | copy-done | bytes 1769496
  13.2 2.1 %shard_map.68 = (bf16[128,6912]{1,0:T(8,128)(2,1)S(1)}, bf16[128,6912]{1,0:T(8,128)(2,1)S(1)}) custom-call(bf16[128,6912]{1,0:T(8,128)(2,1)S(1)} %copy-done, bf16[128,6912]{1,0:T(8,128)(2,1)S(1)} %copy-done.1, bf16[3,64,256]{2,1,0:T(8,128)(2,1)S(1)} %get-tuple-element.54.after), custom_call_target="tpu_custom_call" | custom-call | bytes 7000000 | tf_op jit(solution)/shard_map/pallas_call | solution.py:206
  15.4 0.4 collective-permute-start.4
  15.9 0.7 collective-permute-done.2.up_cross
  16.6 0.2 collective-permute-done.4.down_cross
  16.8 3.9 %shard_map.69 = (bf16[1024,256]{1,0:T(8,128)(2,1)S(1)}, bf16[768,128]{1,0:T(8,128)(2,1)S(1)}, bf16[1280,128]{1,0:T(8,128)(2,1)S(1)}, f32[512,128]{1,0:T(8,128)S(1)}, f32[512,128]{1,0:T(8,128)S(1)}) custom-call(s32[4]{0:T(128)S(1)} %pad_add_fusion.place_ref, bf16[8,64,256]{2,1,0:T(8,128)(2,1)S(1)} %get-tuple-element.52.fc_ref, ...), custom_call_target="tpu_custom_call" | custom-call | flops 2300000000 | bytes 6000000 | tf_op jit(solution)/shard_map/pallas_call | solution.py:275
  20.7 0.4 collective-permute-start.5
  21.1 1.3 %collective-permute-done.5.got_ref = bf16[1280,128]{1,0:T(8,128)(2,1)S(1)} collective-permute-done((bf16[1280,128]{1,0:T(8,128)(2,1)S(1)}, bf16[1280,128]{1,0:T(8,128)(2,1)S(1)}, u32[]{:S(2)}, u32[]{:S(2)}) %collective-permute-start.5) | collective-permute-done | bytes 327712 | tf_op jit(solution)/shard_map/ppermute | solution.py:102
  22.4 1.9 %shard_map.70 = (bf16[768,256]{1,0:T(8,128)(2,1)S(1)}, bf16[4,432,128]{2,1,0:T(8,128)(2,1)S(1)}, bf16[4,224,128]{2,1,0:T(8,128)(2,1)S(1)}, bf16[4,208,128]{2,1,0...) custom-call(s32[4]{0:T(128)S(1)} %pad_add_fusion.place_ref, ...), custom_call_target="tpu_custom_call" | custom-call | flops 1000000000 | bytes 3000000 | tf_op jit(solution)/shard_map/pallas_call | solution.py:376
  24.3 0.3 collective-permute-start.8
  24.6 2.0 %shard_map.71 = (bf16[4,64,128]{2,1,0:T(8,128)(2,1)S(1)}, bf16[4,64,128]{2,1,0:T(8,128)(2,1)S(1)}) custom-call(s32[4]{0:T(128)S(1)} %pad_add_fusion.place_ref, bf16[1024,256]{1,0:T(8,128)(2,1)S(1)} %get-tuple-element.57.x_ref, bf16[768,256]{1,0:T(8,128)(2,1)S(1)} %get-tuple-element.60.h_ref, bf16[128,6912]{1,0:T(8,128)(2,1)S(1)} %get-tuple-element.56.w2_ref), custom_call_target="tpu_custom_call" | custom-call | flops 1000000000 | bytes 3000000 | tf_op jit(solution)/shard_map/pallas_call | solution.py:411
  26.6 9.9 %collective-permute-done.8.refs_3_.refs_4_ = bf16[4,416,128]{2,1,0:T(8,128)(2,1)S(1)} collective-permute-done((bf16[4,416,128]{2,1,0:T(8,128)(2,1)S(1)}, bf16[4,416,128]{2,1,0:T(8,128)(2,1)S(1)}, u32[]{:S(2)}, u32[]{:S(2)}) %collective-permute-start.8) | collective-permute-done | bytes 426016 | tf_op jit(solution)/shard_map/ppermute | solution.py:82
  36.5 0.6 collective-permute-done.7.refs_1_
  37.3 1.3 %collective-permute-start.9 = (bf16[4,208,128]{2,1,0:T(8,128)(2,1)S(1)}, bf16[4,208,128]{2,1,0:T(8,128)(2,1)S(1)}, u32[]{:S(2)}, u32[]{:S(2)}) collective-permute-start(bf16[4,208,128]{2,1,0:T(8,128)(2,1)S(1)} %get-tuple-element.69), channel_id=1, source_target_pairs={{0,2},{2,0},{4,6},{6,4},{8,10},{10,8},{12,14},{14,12},{16,18},{18,... | collective-permute-start | bytes 638984 | tf_op jit(solution)/shard_map/ppermute | solution.py:82
  38.6 1.9 %shard_map.74 = (bf16[4,432,128]{2,1,0:T(8,128)(2,1)S(1)}, bf16[4,224,128]{2,1,0:T(8,128)(2,1)S(1)}, bf16[4,208,128]{2,1,0:T(8,128)(2,1)S(1)}, bf16[4,448,128]{2,1,0:T(8,128)(2,1)S(1)}, bf16[4,416,128]{2,1,0:T(8,128)(2,1)S(1)}) custom-call(s32[4]{0:T(128)S(1)} %pad_add_fusion.place_ref, f32[512,128]{1,0:T(8,128)S(1)} %get-tuple-element.71.back_ref, ...), custom_call_target="tpu_custom_call" | custom-call | flops 1000000000 | bytes 3000000 | tf_op jit(solution)/shard_map/pallas_call | solution.py:389
  40.5 3.6 %collective-permute-done.9.refs_2_ = bf16[4,208,128]{2,1,0:T(8,128)(2,1)S(1)} collective-permute-done((bf16[4,208,128]{2,1,0:T(8,128)(2,1)S(1)}, bf16[4,208,128]{2,1,0:T(8,128)(2,1)S(1)}, u32[]{:S(2)}, u32[]{:S(2)}) %collective-permute-start.9) | collective-permute-done | bytes 213024 | tf_op jit(solution)/shard_map/ppermute | solution.py:82
  44.1 0.3 collective-permute-done.10.refs_3_
  44.3 0.2 shard_map.75
  44.5 0.8 collective-permute-start.14
  45.3 1.4 %collective-permute-start.15 = (bf16[4,416,128]{2,1,0:T(8,128)(2,1)S(1)}, bf16[4,416,128]{2,1,0:T(8,128)(2,1)S(1)}, u32[]{:S(2)}, u32[]{:S(2)}) collective-permute-start(bf16[4,416,128]{2,1,0:T(8,128)(2,1)S(1)} %get-tuple-element.82), channel_id=1, source_target_pairs={{0,4},{2,6},{4,0},{6,2},{8,12},{10,14},{12,8},{14,10},{16,20},{18,... | collective-permute-start | bytes 1277960 | tf_op jit(solution)/shard_map/ppermute | solution.py:82
  46.7 2.5 %collective-permute-start.12 = (bf16[432,128]{1,0:T(8,128)(2,1)S(1)}, bf16[432,128]{1,0:T(8,128)(2,1)S(1)}, u32[]{:S(2)}, u32[]{:S(2)}) collective-permute-start(bf16[432,128]{1,0:T(8,128)(2,1)S(1)} %get-tuple-element.77), channel_id=1, source_target_pairs={{0,16},{2,18},{4,20},{6,22},{8,24},{10,26},{12,28},{14,30},{16,0},... | collective-permute-start | bytes 331784 | tf_op jit(solution)/shard_map/ppermute | solution.py:82
  49.3 1.3 %collective-permute-start.13 = (bf16[432,128]{1,0:T(8,128)(2,1)S(1)}, bf16[432,128]{1,0:T(8,128)(2,1)S(1)}, u32[]{:S(2)}, u32[]{:S(2)}) collective-permute-start(bf16[432,128]{1,0:T(8,128)(2,1)S(1)} %get-tuple-element.78), channel_id=1, source_target_pairs={{0,24},{2,26},{4,28},{6,30},{8,0},{10,2},{12,4},{14,6},{16,8},{18,... | collective-permute-start | bytes 331784 | tf_op jit(solution)/shard_map/ppermute | solution.py:82
  50.6 1.2 %shard_map.72 = (bf16[4,64,256]{2,1,0:T(8,128)(2,1)}, f32[8,128]{1,0:T(8,128)S(1)}) custom-call(s32[4]{0:T(128)S(1)} %pad_add_fusion.place_ref, bf16[4,64,128]{2,1,0:T(8,128)(2,1)S(1)} %get-tuple-element.61.mine_ref.refs_4_.after, bf16[4,64,128]{2,1,0:T(8,128)(2,1)S(1)} %collective-permute-done.6.theirs_ref), custom_call_target="tpu_custom_call" | custom-call | bytes 400000 | tf_op jit(solution)/shard_map/pallas_call | solution.py:431
  51.8 2.7 %collective-permute-done.11.refs_1_ = bf16[432,128]{1,0:T(8,128)(2,1)S(1)} collective-permute-done((bf16[432,128]{1,0:T(8,128)(2,1)S(1)}, bf16[432,128]{1,0:T(8,128)(2,1)S(1)}, u32[]{:S(2)}, u32[]{:S(2)}) %collective-permute-start.11) | collective-permute-done | bytes 110624 | tf_op jit(solution)/shard_map/ppermute | solution.py:82
  54.5 3.7 %collective-permute-done.12.refs_2_ = bf16[432,128]{1,0:T(8,128)(2,1)S(1)} collective-permute-done((bf16[432,128]{1,0:T(8,128)(2,1)S(1)}, bf16[432,128]{1,0:T(8,128)(2,1)S(1)}, u32[]{:S(2)}, u32[]{:S(2)}) %collective-permute-start.12) | collective-permute-done | bytes 110624 | tf_op jit(solution)/shard_map/ppermute | solution.py:82
  58.3 0.2 shard_map.76
  58.4 1.0 collective-permute-start.20
  59.5 0.9 collective-permute-start.19
  60.4 2.5 %collective-permute-start.18 = (bf16[432,128]{1,0:T(8,128)(2,1)S(1)}, bf16[432,128]{1,0:T(8,128)(2,1)S(1)}, u32[]{:S(2)}, u32[]{:S(2)}) collective-permute-start(bf16[432,128]{1,0:T(8,128)(2,1)S(1)} %get-tuple-element.84.refs_0_), channel_id=1, source_target_pairs={{0,8},{2,10},{4,12},{6,14},{8,16},{10,18},{12,20},{14,22},{16,24},... | collective-permute-start | bytes 331784 | tf_op jit(solution)/shard_map/ppermute | solution.py:82
  63.0 1.1 collective-permute-start.17
  64.0 1.3 %collective-permute-start.16 = (bf16[432,128]{1,0:T(8,128)(2,1)S(1)}, bf16[432,128]{1,0:T(8,128)(2,1)S(1)}, u32[]{:S(2)}, u32[]{:S(2)}) collective-permute-start(bf16[432,128]{1,0:T(8,128)(2,1)S(1)} %get-tuple-element.84.refs_0_), channel_id=1, source_target_pairs={{0,24},{2,26},{4,28},{6,30},{8,0},{10,2},{12,4},{14,6},{16,8},{18,... | collective-permute-start | bytes 331784 | tf_op jit(solution)/shard_map/ppermute | solution.py:82
  65.3 2.8 %collective-permute-done.18.refs_3_ = bf16[432,128]{1,0:T(8,128)(2,1)S(1)} collective-permute-done((bf16[432,128]{1,0:T(8,128)(2,1)S(1)}, bf16[432,128]{1,0:T(8,128)(2,1)S(1)}, u32[]{:S(2)}, u32[]{:S(2)}) %collective-permute-start.18) | collective-permute-done | bytes 110624 | tf_op jit(solution)/shard_map/ppermute | solution.py:82
  68.2 3.2 %collective-permute-done.17.refs_2_ = bf16[432,128]{1,0:T(8,128)(2,1)S(1)} collective-permute-done((bf16[432,128]{1,0:T(8,128)(2,1)S(1)}, bf16[432,128]{1,0:T(8,128)(2,1)S(1)}, u32[]{:S(2)}, u32[]{:S(2)}) %collective-permute-start.17) | collective-permute-done | bytes 110624 | tf_op jit(solution)/shard_map/ppermute | solution.py:82
  71.3 0.2 shard_map.77
  71.5 1.5 %collective-permute-start.22 = (bf16[4,432,128]{2,1,0:T(8,128)(2,1)S(1)}, bf16[4,432,128]{2,1,0:T(8,128)(2,1)S(1)}, u32[]{:S(2)}, u32[]{:S(2)}) collective-permute-start(bf16[4,432,128]{2,1,0:T(8,128)(2,1)S(1)} %get-tuple-element.88.m_ref), channel_id=1, source_target_pairs={{0,4},{2,6},{4,0},{6,2},{8,12},{10,14},{12,8},{14,10},{16,20},{18,... | collective-permute-start | bytes 1327112 | tf_op jit(solution)/shard_map/ppermute | solution.py:82
  73.0 0.7 collective-permute-start.21
  73.7 2.6 %collective-permute-start.23 = (bf16[432,128]{1,0:T(8,128)(2,1)S(1)}, bf16[432,128]{1,0:T(8,128)(2,1)S(1)}, u32[]{:S(2)}, u32[]{:S(2)}) collective-permute-start(bf16[432,128]{1,0:T(8,128)(2,1)S(1)} %get-tuple-element.90), channel_id=1, source_target_pairs={{0,8},{2,10},{4,12},{6,14},{8,16},{10,18},{12,20},{14,22},{16,24},... | collective-permute-start | bytes 331784 | tf_op jit(solution)/shard_map/ppermute | solution.py:82
  76.3 1.5 %collective-permute-start.24 = (bf16[432,128]{1,0:T(8,128)(2,1)S(1)}, bf16[432,128]{1,0:T(8,128)(2,1)S(1)}, u32[]{:S(2)}, u32[]{:S(2)}) collective-permute-start(bf16[432,128]{1,0:T(8,128)(2,1)S(1)} %get-tuple-element.91), channel_id=1, source_target_pairs={{0,16},{2,18},{4,20},{6,22},{8,24},{10,26},{12,28},{14,30},{16,0},... | collective-permute-start | bytes 331784 | tf_op jit(solution)/shard_map/ppermute | solution.py:82
  77.8 0.9 collective-permute-start.25
  78.7 2.7 %collective-permute-done.23.refs_3_ = bf16[432,128]{1,0:T(8,128)(2,1)S(1)} collective-permute-done((bf16[432,128]{1,0:T(8,128)(2,1)S(1)}, bf16[432,128]{1,0:T(8,128)(2,1)S(1)}, u32[]{:S(2)}, u32[]{:S(2)}) %collective-permute-start.23) | collective-permute-done | bytes 110624 | tf_op jit(solution)/shard_map/ppermute | solution.py:82
  81.4 3.2 %collective-permute-done.24.refs_4_ = bf16[432,128]{1,0:T(8,128)(2,1)S(1)} collective-permute-done((bf16[432,128]{1,0:T(8,128)(2,1)S(1)}, bf16[432,128]{1,0:T(8,128)(2,1)S(1)}, u32[]{:S(2)}, u32[]{:S(2)}) %collective-permute-start.24) | collective-permute-done | bytes 110624 | tf_op jit(solution)/shard_map/ppermute | solution.py:82
  84.8 1.0 collective-permute-start.29
  85.8 1.0 collective-permute-start.30
  86.7 2.7 %collective-permute-start.28 = (bf16[432,128]{1,0:T(8,128)(2,1)S(1)}, bf16[432,128]{1,0:T(8,128)(2,1)S(1)}, u32[]{:S(2)}, u32[]{:S(2)}) collective-permute-start(bf16[432,128]{1,0:T(8,128)(2,1)S(1)} %get-tuple-element.93.refs_0_), channel_id=1, source_target_pairs={{0,8},{2,10},{4,12},{6,14},{8,16},{10,18},{12,20},{14,22},{16,24},... | collective-permute-start | bytes 331784 | tf_op jit(solution)/shard_map/ppermute | solution.py:82
  89.4 1.5 %collective-permute-start.27 = (bf16[432,128]{1,0:T(8,128)(2,1)S(1)}, bf16[432,128]{1,0:T(8,128)(2,1)S(1)}, u32[]{:S(2)}, u32[]{:S(2)}) collective-permute-start(bf16[432,128]{1,0:T(8,128)(2,1)S(1)} %get-tuple-element.93.refs_0_), channel_id=1, source_target_pairs={{0,16},{2,18},{4,20},{6,22},{8,24},{10,26},{12,28},{14,30},{16,0},... | collective-permute-start | bytes 331784 | tf_op jit(solution)/shard_map/ppermute | solution.py:82
  90.9 0.9 collective-permute-start.26
  91.8 2.6 %collective-permute-done.28.refs_3_ = bf16[432,128]{1,0:T(8,128)(2,1)S(1)} collective-permute-done((bf16[432,128]{1,0:T(8,128)(2,1)S(1)}, bf16[432,128]{1,0:T(8,128)(2,1)S(1)}, u32[]{:S(2)}, u32[]{:S(2)}) %collective-permute-start.28) | collective-permute-done | bytes 110624 | tf_op jit(solution)/shard_map/ppermute | solution.py:82
  94.4 3.3 %collective-permute-done.27.refs_2_ = bf16[432,128]{1,0:T(8,128)(2,1)S(1)} collective-permute-done((bf16[432,128]{1,0:T(8,128)(2,1)S(1)}, bf16[432,128]{1,0:T(8,128)(2,1)S(1)}, u32[]{:S(2)}, u32[]{:S(2)}) %collective-permute-start.27) | collective-permute-done | bytes 110624 | tf_op jit(solution)/shard_map/ppermute | solution.py:82
  97.8 1.5 %collective-permute-start.32 = (bf16[4,432,128]{2,1,0:T(8,128)(2,1)S(1)}, bf16[4,432,128]{2,1,0:T(8,128)(2,1)S(1)}, u32[]{:S(2)}, u32[]{:S(2)}) collective-permute-start(bf16[4,432,128]{2,1,0:T(8,128)(2,1)S(1)} %shard_map.79.after.m_ref), channel_id=1, source_target_pairs={{0,4},{2,6},{4,0},{6,2},{8,12},{10,14},{12,8},{14,10},{16,20},{18,... | collective-permute-start | bytes 1327112 | tf_op jit(solution)/shard_map/ppermute | solution.py:82
  99.2 0.7 collective-permute-start.31
  100.0 9.8 %collective-permute-done.32.refs_1_.my_ref = bf16[4,432,128]{2,1,0:T(8,128)(2,1)S(1)} collective-permute-done((bf16[4,432,128]{2,1,0:T(8,128)(2,1)S(1)}, bf16[4,432,128]{2,1,0:T(8,128)(2,1)S(1)}, u32[]{:S(2)}, u32[]{:S(2)}) %collective-permute-start.32) | collective-permute-done | bytes 442400 | tf_op jit(solution)/shard_map/ppermute | solution.py:82
  109.7 1.1 collective-permute-done.31.refs_0_.mx_ref
  110.9 0.7 collective-permute-start.33
  111.6 1.1 collective-permute-start.34
  112.6 2.4 %shard_map.81 = (f32[128,6912]{1,0:T(8,128)}, f32[8,128]{1,0:T(8,128)S(1)}) custom-call(s32[4]{0:T(128)S(1)} %pad_add_fusion.place_ref, bf16[4,432,128]{2,1,0:T(8,128)(2,1)S(1)} %get-tuple-element.88.m_ref, bf16[4,432,128]{2,1,0:T(8,128)(2,1)S(1)} %collective-permute-done.21.refs_0_.mx_ref, bf16[4,432,128]{2,1,0:T(8,128)(2,1)S(1)} %collective-permute-done.22.refs_1_.my_ref, ...), custom_call_target="tpu_custom_call" | custom-call | bytes 6000000 | tf_op jit(solution)/shard_map/pallas_call | solution.py:478
  115.1 2.3 %collective-permute-done.34.last_ref = bf16[4,208,128]{2,1,0:T(8,128)(2,1)S(1)} collective-permute-done((bf16[4,208,128]{2,1,0:T(8,128)(2,1)S(1)}, bf16[4,208,128]{2,1,0:T(8,128)(2,1)S(1)}, u32[]{:S(2)}, u32[]{:S(2)}) %collective-permute-start.34) | collective-permute-done | bytes 213024 | tf_op jit(solution)/shard_map/ppermute | solution.py:82
  117.4 3.0 %shard_map.82 = (f32[128,6912]{1,0:T(8,128)}, f32[8,128]{1,0:T(8,128)}) custom-call(s32[4]{0:T(128)S(1)} %pad_add_fusion.place_ref, bf16[4,432,128]{2,1,0:T(8,128)(2,1)S(1)} %shard_map.79.after.m_ref, bf16[4,432,128]{2,1,0:T(8,128)(2,1)S(1)} %collective-permute-done.31.refs_0_.mx_ref, bf16[4,432,128]{2,1,0:T(8,128)(2,1)S(1)} %collective-permute-done.32.refs_1_.my_ref, ...), custom_call_target="tpu_custom_call" | custom-call | bytes 6000000 | tf_op jit(solution)/shard_map/pallas_call | solution.py:478
  (31 shorter events, 0.7 us)
Async XLA Ops:
  0.6 0.9 copy-start.2
  1.5 0.9 copy-start.3
  3.1 13.7 %collective-permute-start = (bf16[8,64,256]{2,1,0:T(8,128)(2,1)S(1)}, bf16[8,64,256]{2,1,0:T(8,128)(2,1)S(1)}, u32[]{:S(2)}, u32[]{:S(2)}) collective-permute-start(bf16[8,64,256]{2,1,0:T(8,128)(2,1)S(1)} %get-tuple-element.52.fc_ref), channel_id=1, source_target_pairs={{0,1},{1,0},{2,3},{3,2},{4,5},{5,4},{6,7},{7,6},{8,9},{9,8},{10,11... | collective-permute-start | bytes 786440 | tf_op jit(solution)/shard_map/ppermute | solution.py:102
  3.6 11.7 %collective-permute-start.1 = (bf16[3,64,256]{2,1,0:T(8,128)(2,1)S(1)}, bf16[3,64,256]{2,1,0:T(8,128)(2,1)S(1)}, u32[]{:S(2)}, u32[]{:S(2)}) collective-permute-start(bf16[3,64,256]{2,1,0:T(8,128)(2,1)S(1)} %get-tuple-element.53), channel_id=1, source_target_pairs={{0,2},{1,3},{2,4},{3,5},{4,6},{5,7},{6,8},{7,9},{8,10},{9,11},{10,... | collective-permute-start | bytes 294920 | tf_op jit(solution)/shard_map/ppermute | solution.py:102
  6.1 9.3 %collective-permute-start.3 = (bf16[3,64,256]{2,1,0:T(8,128)(2,1)S(1)}, bf16[3,64,256]{2,1,0:T(8,128)(2,1)S(1)}, u32[]{:S(2)}, u32[]{:S(2)}) collective-permute-start(bf16[3,64,256]{2,1,0:T(8,128)(2,1)S(1)} %get-tuple-element.54.after), channel_id=1, source_target_pairs={{0,30},{1,31},{2,0},{3,1},{4,2},{5,3},{6,4},{7,5},{8,6},{9,7},{10,... | collective-permute-start | bytes 294920 | tf_op jit(solution)/shard_map/ppermute | solution.py:102
  10.2 1.5 %copy-start = (bf16[128,6912]{1,0:T(8,128)(2,1)S(1)}, bf16[128,6912]{1,0:T(8,128)(2,1)}, u32[]{:S(2)}) copy-start(bf16[128,6912]{1,0:T(8,128)(2,1)} %w1_ref.1) | copy-start | bytes 5308420
  11.7 1.5 %copy-start.1 = (bf16[128,6912]{1,0:T(8,128)(2,1)S(1)}, bf16[128,6912]{1,0:T(8,128)(2,1)}, u32[]{:S(2)}) copy-start(bf16[128,6912]{1,0:T(8,128)(2,1)} %w2_ref.1) | copy-start | bytes 5308420
  15.3 1.4 %collective-permute-start.2 = (bf16[3,64,256]{2,1,0:T(8,128)(2,1)S(1)}, bf16[3,64,256]{2,1,0:T(8,128)(2,1)S(1)}, u32[]{:S(2)}, u32[]{:S(2)}) collective-permute-start(bf16[3,64,256]{2,1,0:T(8,128)(2,1)S(1)} %collective-permute-done.1.up_same), channel_id=1, source_target_pairs={{0,1},{1,0},{2,3},{3,2},{4,5},{5,4},{6,7},{7,6},{8,9},{9,8},{10,11... | collective-permute-start | bytes 294920 | tf_op jit(solution)/shard_map/ppermute | solution.py:102
  15.4 1.4 %collective-permute-start.4 = (bf16[3,64,256]{2,1,0:T(8,128)(2,1)S(1)}, bf16[3,64,256]{2,1,0:T(8,128)(2,1)S(1)}, u32[]{:S(2)}, u32[]{:S(2)}) collective-permute-start(bf16[3,64,256]{2,1,0:T(8,128)(2,1)S(1)} %collective-permute-done.3.down_same), channel_id=1, source_target_pairs={{0,1},{1,0},{2,3},{3,2},{4,5},{5,4},{6,7},{7,6},{8,9},{9,8},{10,11... | collective-permute-start | bytes 294920 | tf_op jit(solution)/shard_map/ppermute | solution.py:102
  20.7 1.7 %collective-permute-start.5 = (bf16[1280,128]{1,0:T(8,128)(2,1)S(1)}, bf16[1280,128]{1,0:T(8,128)(2,1)S(1)}, u32[]{:S(2)}, u32[]{:S(2)}) collective-permute-start(bf16[1280,128]{1,0:T(8,128)(2,1)S(1)} %get-tuple-element.59.send_ref), channel_id=1, source_target_pairs={{0,1},{1,0},{2,3},{3,2},{4,5},{5,4},{6,7},{7,6},{8,9},{9,8},{10,11... | collective-permute-start | bytes 983048 | tf_op jit(solution)/shard_map/ppermute | solution.py:102
  24.3 12.8 %collective-permute-start.7 = (bf16[4,448,128]{2,1,0:T(8,128)(2,1)S(1)}, bf16[4,448,128]{2,1,0:T(8,128)(2,1)S(1)}, u32[]{:S(2)}, u32[]{:S(2)}) collective-permute-start(bf16[4,448,128]{2,1,0:T(8,128)(2,1)S(1)} %get-tuple-element.65), channel_id=1, source_target_pairs={{0,2},{2,0},{4,6},{6,4},{8,10},{10,8},{12,14},{14,12},{16,18},{18,... | collective-permute-start | bytes 1376264 | tf_op jit(solution)/shard_map/ppermute | solution.py:82
  24.3 12.1 %collective-permute-start.8 = (bf16[4,416,128]{2,1,0:T(8,128)(2,1)S(1)}, bf16[4,416,128]{2,1,0:T(8,128)(2,1)S(1)}, u32[]{:S(2)}, u32[]{:S(2)}) collective-permute-start(bf16[4,416,128]{2,1,0:T(8,128)(2,1)S(1)} %get-tuple-element.68), channel_id=1, source_target_pairs={{0,4},{2,6},{4,0},{6,2},{8,12},{10,14},{12,8},{14,10},{16,20},{18,... | collective-permute-start | bytes 1277960 | tf_op jit(solution)/shard_map/ppermute | solution.py:82
  37.2 7.1 %collective-permute-start.10 = (bf16[4,224,128]{2,1,0:T(8,128)(2,1)S(1)}, bf16[4,224,128]{2,1,0:T(8,128)(2,1)S(1)}, u32[]{:S(2)}, u32[]{:S(2)}) collective-permute-start(bf16[4,224,128]{2,1,0:T(8,128)(2,1)S(1)} %get-tuple-element.70), channel_id=1, source_target_pairs={{0,4},{2,6},{4,0},{6,2},{8,12},{10,14},{12,8},{14,10},{16,20},{18,... | collective-permute-start | bytes 688136 | tf_op jit(solution)/shard_map/ppermute | solution.py:82
  37.3 6.8 %collective-permute-start.9 = (bf16[4,208,128]{2,1,0:T(8,128)(2,1)S(1)}, bf16[4,208,128]{2,1,0:T(8,128)(2,1)S(1)}, u32[]{:S(2)}, u32[]{:S(2)}) collective-permute-start(bf16[4,208,128]{2,1,0:T(8,128)(2,1)S(1)} %get-tuple-element.69), channel_id=1, source_target_pairs={{0,2},{2,0},{4,6},{6,4},{8,10},{10,8},{12,14},{14,12},{16,18},{18,... | collective-permute-start | bytes 638984 | tf_op jit(solution)/shard_map/ppermute | solution.py:82
  44.5 13.7 %collective-permute-start.14 = (bf16[4,448,128]{2,1,0:T(8,128)(2,1)S(1)}, bf16[4,448,128]{2,1,0:T(8,128)(2,1)S(1)}, u32[]{:S(2)}, u32[]{:S(2)}) collective-permute-start(bf16[4,448,128]{2,1,0:T(8,128)(2,1)S(1)} %get-tuple-element.80), channel_id=1, source_target_pairs={{0,2},{2,0},{4,6},{6,4},{8,10},{10,8},{12,14},{14,12},{16,18},{18,... | collective-permute-start | bytes 1376264 | tf_op jit(solution)/shard_map/ppermute | solution.py:82
  45.3 12.9 %collective-permute-start.15 = (bf16[4,416,128]{2,1,0:T(8,128)(2,1)S(1)}, bf16[4,416,128]{2,1,0:T(8,128)(2,1)S(1)}, u32[]{:S(2)}, u32[]{:S(2)}) collective-permute-start(bf16[4,416,128]{2,1,0:T(8,128)(2,1)S(1)} %get-tuple-element.82), channel_id=1, source_target_pairs={{0,4},{2,6},{4,0},{6,2},{8,12},{10,14},{12,8},{14,10},{16,20},{18,... | collective-permute-start | bytes 1277960 | tf_op jit(solution)/shard_map/ppermute | solution.py:82
  46.7 2.5 %collective-permute-start.6 = (bf16[4,64,128]{2,1,0:T(8,128)(2,1)S(1)}, bf16[4,64,128]{2,1,0:T(8,128)(2,1)S(1)}, u32[]{:S(2)}, u32[]{:S(2)}) collective-permute-start(bf16[4,64,128]{2,1,0:T(8,128)(2,1)S(1)} %get-tuple-element.62), channel_id=1, source_target_pairs={{0,1},{1,0},{2,3},{3,2},{4,5},{5,4},{6,7},{7,6},{8,9},{9,8},{10,11... | collective-permute-start | bytes 196616 | tf_op jit(solution)/shard_map/ppermute | solution.py:102
  46.7 7.8 %collective-permute-start.11 = (bf16[432,128]{1,0:T(8,128)(2,1)S(1)}, bf16[432,128]{1,0:T(8,128)(2,1)S(1)}, u32[]{:S(2)}, u32[]{:S(2)}) collective-permute-start(bf16[432,128]{1,0:T(8,128)(2,1)S(1)} %get-tuple-element.76), channel_id=1, source_target_pairs={{0,8},{2,10},{4,12},{6,14},{8,16},{10,18},{12,20},{14,22},{16,24},... | collective-permute-start | bytes 331784 | tf_op jit(solution)/shard_map/ppermute | solution.py:82
  46.7 11.5 %collective-permute-start.12 = (bf16[432,128]{1,0:T(8,128)(2,1)S(1)}, bf16[432,128]{1,0:T(8,128)(2,1)S(1)}, u32[]{:S(2)}, u32[]{:S(2)}) collective-permute-start(bf16[432,128]{1,0:T(8,128)(2,1)S(1)} %get-tuple-element.77), channel_id=1, source_target_pairs={{0,16},{2,18},{4,20},{6,22},{8,24},{10,26},{12,28},{14,30},{16,0},... | collective-permute-start | bytes 331784 | tf_op jit(solution)/shard_map/ppermute | solution.py:82
  49.3 9.0 %collective-permute-start.13 = (bf16[432,128]{1,0:T(8,128)(2,1)S(1)}, bf16[432,128]{1,0:T(8,128)(2,1)S(1)}, u32[]{:S(2)}, u32[]{:S(2)}) collective-permute-start(bf16[432,128]{1,0:T(8,128)(2,1)S(1)} %get-tuple-element.78), channel_id=1, source_target_pairs={{0,24},{2,26},{4,28},{6,30},{8,0},{10,2},{12,4},{14,6},{16,8},{18,... | collective-permute-start | bytes 331784 | tf_op jit(solution)/shard_map/ppermute | solution.py:82
  58.4 12.9 %collective-permute-start.20 = (bf16[4,224,128]{2,1,0:T(8,128)(2,1)S(1)}, bf16[4,224,128]{2,1,0:T(8,128)(2,1)S(1)}, u32[]{:S(2)}, u32[]{:S(2)}) collective-permute-start(bf16[4,224,128]{2,1,0:T(8,128)(2,1)S(1)} %get-tuple-element.87), channel_id=1, source_target_pairs={{0,4},{2,6},{4,0},{6,2},{8,12},{10,14},{12,8},{14,10},{16,20},{18,... | collective-permute-start | bytes 688136 | tf_op jit(solution)/shard_map/ppermute | solution.py:82
  59.5 11.9 %collective-permute-start.19 = (bf16[4,208,128]{2,1,0:T(8,128)(2,1)S(1)}, bf16[4,208,128]{2,1,0:T(8,128)(2,1)S(1)}, u32[]{:S(2)}, u32[]{:S(2)}) collective-permute-start(bf16[4,208,128]{2,1,0:T(8,128)(2,1)S(1)} %get-tuple-element.86), channel_id=1, source_target_pairs={{0,2},{2,0},{4,6},{6,4},{8,10},{10,8},{12,14},{14,12},{16,18},{18,... | collective-permute-start | bytes 638984 | tf_op jit(solution)/shard_map/ppermute | solution.py:82
  60.4 7.7 %collective-permute-start.18 = (bf16[432,128]{1,0:T(8,128)(2,1)S(1)}, bf16[432,128]{1,0:T(8,128)(2,1)S(1)}, u32[]{:S(2)}, u32[]{:S(2)}) collective-permute-start(bf16[432,128]{1,0:T(8,128)(2,1)S(1)} %get-tuple-element.84.refs_0_), channel_id=1, source_target_pairs={{0,8},{2,10},{4,12},{6,14},{8,16},{10,18},{12,20},{14,22},{16,24},... | collective-permute-start | bytes 331784 | tf_op jit(solution)/shard_map/ppermute | solution.py:82
  63.0 8.4 %collective-permute-start.17 = (bf16[432,128]{1,0:T(8,128)(2,1)S(1)}, bf16[432,128]{1,0:T(8,128)(2,1)S(1)}, u32[]{:S(2)}, u32[]{:S(2)}) collective-permute-start(bf16[432,128]{1,0:T(8,128)(2,1)S(1)} %get-tuple-element.84.refs_0_), channel_id=1, source_target_pairs={{0,16},{2,18},{4,20},{6,22},{8,24},{10,26},{12,28},{14,30},{16,0},... | collective-permute-start | bytes 331784 | tf_op jit(solution)/shard_map/ppermute | solution.py:82
  64.0 7.3 %collective-permute-start.16 = (bf16[432,128]{1,0:T(8,128)(2,1)S(1)}, bf16[432,128]{1,0:T(8,128)(2,1)S(1)}, u32[]{:S(2)}, u32[]{:S(2)}) collective-permute-start(bf16[432,128]{1,0:T(8,128)(2,1)S(1)} %get-tuple-element.84.refs_0_), channel_id=1, source_target_pairs={{0,24},{2,26},{4,28},{6,30},{8,0},{10,2},{12,4},{14,6},{16,8},{18,... | collective-permute-start | bytes 331784 | tf_op jit(solution)/shard_map/ppermute | solution.py:82
  71.5 13.1 %collective-permute-start.22 = (bf16[4,432,128]{2,1,0:T(8,128)(2,1)S(1)}, bf16[4,432,128]{2,1,0:T(8,128)(2,1)S(1)}, u32[]{:S(2)}, u32[]{:S(2)}) collective-permute-start(bf16[4,432,128]{2,1,0:T(8,128)(2,1)S(1)} %get-tuple-element.88.m_ref), channel_id=1, source_target_pairs={{0,4},{2,6},{4,0},{6,2},{8,12},{10,14},{12,8},{14,10},{16,20},{18,... | collective-permute-start | bytes 1327112 | tf_op jit(solution)/shard_map/ppermute | solution.py:82
  73.0 11.7 %collective-permute-start.21 = (bf16[4,432,128]{2,1,0:T(8,128)(2,1)S(1)}, bf16[4,432,128]{2,1,0:T(8,128)(2,1)S(1)}, u32[]{:S(2)}, u32[]{:S(2)}) collective-permute-start(bf16[4,432,128]{2,1,0:T(8,128)(2,1)S(1)} %get-tuple-element.88.m_ref), channel_id=1, source_target_pairs={{0,2},{2,0},{4,6},{6,4},{8,10},{10,8},{12,14},{14,12},{16,18},{18,... | collective-permute-start | bytes 1327112 | tf_op jit(solution)/shard_map/ppermute | solution.py:82
  73.7 7.7 %collective-permute-start.23 = (bf16[432,128]{1,0:T(8,128)(2,1)S(1)}, bf16[432,128]{1,0:T(8,128)(2,1)S(1)}, u32[]{:S(2)}, u32[]{:S(2)}) collective-permute-start(bf16[432,128]{1,0:T(8,128)(2,1)S(1)} %get-tuple-element.90), channel_id=1, source_target_pairs={{0,8},{2,10},{4,12},{6,14},{8,16},{10,18},{12,20},{14,22},{16,24},... | collective-permute-start | bytes 331784 | tf_op jit(solution)/shard_map/ppermute | solution.py:82
  76.3 8.3 %collective-permute-start.24 = (bf16[432,128]{1,0:T(8,128)(2,1)S(1)}, bf16[432,128]{1,0:T(8,128)(2,1)S(1)}, u32[]{:S(2)}, u32[]{:S(2)}) collective-permute-start(bf16[432,128]{1,0:T(8,128)(2,1)S(1)} %get-tuple-element.91), channel_id=1, source_target_pairs={{0,16},{2,18},{4,20},{6,22},{8,24},{10,26},{12,28},{14,30},{16,0},... | collective-permute-start | bytes 331784 | tf_op jit(solution)/shard_map/ppermute | solution.py:82
  77.8 6.9 %collective-permute-start.25 = (bf16[432,128]{1,0:T(8,128)(2,1)S(1)}, bf16[432,128]{1,0:T(8,128)(2,1)S(1)}, u32[]{:S(2)}, u32[]{:S(2)}) collective-permute-start(bf16[432,128]{1,0:T(8,128)(2,1)S(1)} %get-tuple-element.92), channel_id=1, source_target_pairs={{0,24},{2,26},{4,28},{6,30},{8,0},{10,2},{12,4},{14,6},{16,8},{18,... | collective-permute-start | bytes 331784 | tf_op jit(solution)/shard_map/ppermute | solution.py:82
  84.8 12.9 %collective-permute-start.29 = (bf16[4,224,128]{2,1,0:T(8,128)(2,1)S(1)}, bf16[4,224,128]{2,1,0:T(8,128)(2,1)S(1)}, u32[]{:S(2)}, u32[]{:S(2)}) collective-permute-start(bf16[4,224,128]{2,1,0:T(8,128)(2,1)S(1)} %get-tuple-element.94), channel_id=1, source_target_pairs={{0,4},{2,6},{4,0},{6,2},{8,12},{10,14},{12,8},{14,10},{16,20},{18,... | collective-permute-start | bytes 688136 | tf_op jit(solution)/shard_map/ppermute | solution.py:82
  85.8 11.9 %collective-permute-start.30 = (bf16[4,208,128]{2,1,0:T(8,128)(2,1)S(1)}, bf16[4,208,128]{2,1,0:T(8,128)(2,1)S(1)}, u32[]{:S(2)}, u32[]{:S(2)}) collective-permute-start(bf16[4,208,128]{2,1,0:T(8,128)(2,1)S(1)} %get-tuple-element.95), channel_id=1, source_target_pairs={{0,2},{2,0},{4,6},{6,4},{8,10},{10,8},{12,14},{14,12},{16,18},{18,... | collective-permute-start | bytes 638984 | tf_op jit(solution)/shard_map/ppermute | solution.py:82
  86.7 7.7 %collective-permute-start.28 = (bf16[432,128]{1,0:T(8,128)(2,1)S(1)}, bf16[432,128]{1,0:T(8,128)(2,1)S(1)}, u32[]{:S(2)}, u32[]{:S(2)}) collective-permute-start(bf16[432,128]{1,0:T(8,128)(2,1)S(1)} %get-tuple-element.93.refs_0_), channel_id=1, source_target_pairs={{0,8},{2,10},{4,12},{6,14},{8,16},{10,18},{12,20},{14,22},{16,24},... | collective-permute-start | bytes 331784 | tf_op jit(solution)/shard_map/ppermute | solution.py:82
  89.4 8.3 %collective-permute-start.27 = (bf16[432,128]{1,0:T(8,128)(2,1)S(1)}, bf16[432,128]{1,0:T(8,128)(2,1)S(1)}, u32[]{:S(2)}, u32[]{:S(2)}) collective-permute-start(bf16[432,128]{1,0:T(8,128)(2,1)S(1)} %get-tuple-element.93.refs_0_), channel_id=1, source_target_pairs={{0,16},{2,18},{4,20},{6,22},{8,24},{10,26},{12,28},{14,30},{16,0},... | collective-permute-start | bytes 331784 | tf_op jit(solution)/shard_map/ppermute | solution.py:82
  90.9 6.8 %collective-permute-start.26 = (bf16[432,128]{1,0:T(8,128)(2,1)S(1)}, bf16[432,128]{1,0:T(8,128)(2,1)S(1)}, u32[]{:S(2)}, u32[]{:S(2)}) collective-permute-start(bf16[432,128]{1,0:T(8,128)(2,1)S(1)} %get-tuple-element.93.refs_0_), channel_id=1, source_target_pairs={{0,24},{2,26},{4,28},{6,30},{8,0},{10,2},{12,4},{14,6},{16,8},{18,... | collective-permute-start | bytes 331784 | tf_op jit(solution)/shard_map/ppermute | solution.py:82
  97.8 12.0 %collective-permute-start.32 = (bf16[4,432,128]{2,1,0:T(8,128)(2,1)S(1)}, bf16[4,432,128]{2,1,0:T(8,128)(2,1)S(1)}, u32[]{:S(2)}, u32[]{:S(2)}) collective-permute-start(bf16[4,432,128]{2,1,0:T(8,128)(2,1)S(1)} %shard_map.79.after.m_ref), channel_id=1, source_target_pairs={{0,4},{2,6},{4,0},{6,2},{8,12},{10,14},{12,8},{14,10},{16,20},{18,... | collective-permute-start | bytes 1327112 | tf_op jit(solution)/shard_map/ppermute | solution.py:82
  99.2 11.6 %collective-permute-start.31 = (bf16[4,432,128]{2,1,0:T(8,128)(2,1)S(1)}, bf16[4,432,128]{2,1,0:T(8,128)(2,1)S(1)}, u32[]{:S(2)}, u32[]{:S(2)}) collective-permute-start(bf16[4,432,128]{2,1,0:T(8,128)(2,1)S(1)} %shard_map.79.after.m_ref), channel_id=1, source_target_pairs={{0,2},{2,0},{4,6},{6,4},{8,10},{10,8},{12,14},{14,12},{16,18},{18,... | collective-permute-start | bytes 1327112 | tf_op jit(solution)/shard_map/ppermute | solution.py:82
  110.9 6.5 %collective-permute-start.33 = (bf16[4,224,128]{2,1,0:T(8,128)(2,1)S(1)}, bf16[4,224,128]{2,1,0:T(8,128)(2,1)S(1)}, u32[]{:S(2)}, u32[]{:S(2)}) collective-permute-start(bf16[4,224,128]{2,1,0:T(8,128)(2,1)S(1)} %get-tuple-element.96), channel_id=1, source_target_pairs={{0,4},{2,6},{4,0},{6,2},{8,12},{10,14},{12,8},{14,10},{16,20},{18,... | collective-permute-start | bytes 688136 | tf_op jit(solution)/shard_map/ppermute | solution.py:82
  111.6 5.8 %collective-permute-start.34 = (bf16[4,208,128]{2,1,0:T(8,128)(2,1)S(1)}, bf16[4,208,128]{2,1,0:T(8,128)(2,1)S(1)}, u32[]{:S(2)}, u32[]{:S(2)}) collective-permute-start(bf16[4,208,128]{2,1,0:T(8,128)(2,1)S(1)} %get-tuple-element.97), channel_id=1, source_target_pairs={{0,2},{2,0},{4,6},{6,4},{8,10},{10,8},{12,14},{14,12},{16,18},{18,... | collective-permute-start | bytes 638984 | tf_op jit(solution)/shard_map/ppermute | solution.py:82

commit v3 on v2

--- a/solution.py
+++ b/solution.py
@@ -122,6 +122,23 @@
     return jnp.concatenate([value[:, AXIAL:], empty], axis=1)
 
 
+def forward_weights(w_ref, s, p):
+    return jnp.concatenate([tap_slice(w_ref, (p * 3 + q) * 3 + s) for q in range(3)], axis=0)
+
+
+def dot_rows(lhs, rhs):
+    return lax.dot_general(lhs, rhs, (((1,), (1,)), ((), ())), preferred_element_type=F32)
+
+
+def fold_forward(part, s):
+    layers = part.shape[0]
+    summed = part[:, :, LANES : 2 * LANES]
+    summed = summed + shift_radius(part[:, :, :LANES], 1)
+    summed = summed + shift_radius(part[:, :, 2 * LANES :], -1)
+    summed = summed.reshape(layers * NRZ, LANES)
+    return summed if s == 1 else roll_rows(summed, 1 - s)
+
+
 def conv_rows(x_ref, w_ref, layers, first):
     count = layers * NRZ
     lhs = jnp.concatenate(
@@ -129,24 +146,9 @@
     )
     total = None
     for s in range(3):
-        rhs = jnp.concatenate(
-            [
-                jnp.concatenate(
-                    [tap_slice(w_ref, (p * 3 + q) * 3 + s) for p in range(3)], axis=1
-                )
-                for q in range(3)
-            ],
-            axis=0,
-        )
-        part = lax.dot_general(lhs, rhs, (((1,), (1,)), ((), ())), preferred_element_type=F32)
-        part = part.reshape(layers, NRZ, 3 * LANES)
-        summed = part[:, :, LANES : 2 * LANES]
-        summed = summed + shift_radius(part[:, :, :LANES], 1)
-        summed = summed + shift_radius(part[:, :, 2 * LANES :], -1)
-        summed = summed.reshape(count, LANES)
-        if s != 1:
-            summed = roll_rows(summed, 1 - s)
-        total = summed if total is None else total + summed
+        rhs = jnp.concatenate([forward_weights(w_ref, s, p) for p in range(3)], axis=1)
+        part = fold_forward(dot_rows(lhs, rhs).reshape(layers, NRZ, 3 * LANES), s)
+        total = part if total is None else total + part
     return total
 
 
@@ -188,68 +190,41 @@
     )(f, c)
 
 
-def load_kernel(w1_ref, w2_ref, after, one_ref, two_ref, sems):
-    copies = []
-    for which, (source, goal) in enumerate(((w1_ref, one_ref), (w2_ref, two_ref))):
-        for part in range(4):
-            rows = pl.ds(part * 32, 32)
-            copies.append(
-                pltpu.make_async_copy(source.at[rows], goal.at[rows], sems.at[which, part])
-            )
-    for copy in copies:
-        copy.start()
-    for copy in copies:
-        copy.wait()
-
-
-def load(w_first, w_second, after):
-    return pl.pallas_call(
-        load_kernel,
-        out_shape=[shape(w_first.shape), shape(w_second.shape)],
-        in_specs=[in_hbm()] * 2 + [anywhere()],
-        out_specs=[vmem()] * 2,
-        scratch_shapes=[pltpu.SemaphoreType.DMA((2, 4))],
-        compiler_params=params(),
-        cost_estimate=cost(0, 7000000),
-    )(w_first, w_second, after)
-
-
-def fields_kernel(
-    place_ref, fc_ref, swap_ref, up_same, up_cross, down_same, down_cross,
-    w1_ref, w2_ref, x_ref, cot_ref, send_ref, back_ref, slope_ref,
+def inner_kernel(
+    place_ref, fc_ref, swap_ref, w1_ref, w2_ref, x_ref, cot_ref, pre_ref, back_ref, acc_ref
 ):
     own = place_ref[0]
     mine = pl.multiple_of(own * HALF, HALF)
     other = pl.multiple_of((1 - own) * HALF, HALF)
-    for layer in range(2):
-        x_ref[pl.ds(layer * NRZ + mine, HALF), :] = up_same[layer]
-        x_ref[pl.ds(layer * NRZ + other, HALF), :] = up_cross[layer]
-        x_ref[pl.ds((6 + layer) * NRZ + mine, HALF), :] = down_same[layer]
-        x_ref[pl.ds((6 + layer) * NRZ + other, HALF), :] = down_cross[layer]
     for layer in range(LAYERS):
-        x_ref[pl.ds((2 + layer) * NRZ + mine, HALF), :] = fc_ref[layer]
-        x_ref[pl.ds((2 + layer) * NRZ + other, HALF), :] = swap_ref[layer]
-        cot_ref[pl.ds((1 + layer) * NRZ + mine, HALF), :] = pick_half(
+        x_ref[pl.ds(layer * NRZ + mine, HALF), :] = fc_ref[layer]
+        x_ref[pl.ds(layer * NRZ + other, HALF), :] = swap_ref[layer]
+        cot_ref[pl.ds(layer * NRZ + mine, HALF), :] = pick_half(
             fc_ref[LAYERS + layer], own
         ).astype(BF16)
-        cot_ref[pl.ds((1 + layer) * NRZ + other, HALF), :] = pick_half(
+        cot_ref[pl.ds(layer * NRZ + other, HALF), :] = pick_half(
             swap_ref[LAYERS + layer], own
         ).astype(BF16)
-    cot_ref[pl.ds(mine, HALF), :] = pick_half(up_same[2], own).astype(BF16)
-    cot_ref[pl.ds(other, HALF), :] = pick_half(up_cross[2], own).astype(BF16)
-    cot_ref[pl.ds(5 * NRZ + mine, HALF), :] = pick_half(down_same[2], own).astype(BF16)
-    cot_ref[pl.ds(5 * NRZ + other, HALF), :] = pick_half(down_cross[2], own).astype(BF16)
-
-    pre = conv_rows(x_ref, w1_ref, LAYERS + 2, 0)
-    sigma = jax.nn.sigmoid(pre)
-    send_ref[: (LAYERS + 2) * NRZ, :] = (pre * sigma).astype(BF16)
-    inner = pre[NRZ : NRZ * (LAYERS + 1)]
-    sigma = sigma[NRZ : NRZ * (LAYERS + 1)]
-    slope_ref[...] = sigma * (1.0 + inner * (1.0 - sigma))
 
     count = LAYERS * NRZ
+    total = None
+    for s in range(3):
+        acc_ref[...] = jnp.zeros_like(acc_ref)
+        for p in range(3):
+            rows = slice((2 - p) * NRZ, (2 - p) * NRZ + count)
+            acc_ref[rows, :] += dot_rows(x_ref[...], forward_weights(w1_ref, s, p))
+        part = fold_forward(acc_ref[...].reshape(LAYERS + 2, NRZ, 3 * LANES), s)
+        total = part if total is None else total + part
+    pre_ref[...] = total
+
+    empty = jnp.zeros((NRZ, LANES), BF16)
     lhs = jnp.concatenate(
-        [cot_ref[(2 - p) * NRZ : (2 - p) * NRZ + count, :] for p in range(3)], axis=1
+        [
+            jnp.concatenate([cot_ref[NRZ:, :], empty], axis=0),
+            cot_ref[...],
+            jnp.concatenate([empty, cot_ref[: count - NRZ, :]], axis=0),
+        ],
+        axis=1,
     )
     total = None
     for s in range(3):
@@ -266,11 +241,104 @@
         if s != 1:
             summed = roll_rows(summed, s - 1)
         total = summed if total is None else total + summed
+    back_ref[...] = total
+
+
+def inner(place, fc, swap, w_first, w_second):
+    return pl.pallas_call(
+        inner_kernel,
+        out_shape=[
+            shape((LAYERS * NRZ, CH)),
+            shape((LAYERS * NRZ, LANES)),
+            shape(((LAYERS + 2) * NRZ, LANES), F32),
+            shape((LAYERS * NRZ, CH), F32),
+        ],
+        in_specs=[smem()] + [vmem()] * 4,
+        out_specs=[vmem()] * 4,
+        scratch_shapes=[pltpu.VMEM(((LAYERS + 2) * NRZ, 3 * LANES), F32)],
+        compiler_params=params(),
+        cost_estimate=cost(2300000000, 6000000),
+    )(place, fc, swap, w_first, w_second)
+
+
+def fields_kernel(
+    place_ref, x_in, cot_in, pre_in, back_in, same_ref, cross_ref,
+    w1_ref, w2_ref, x_ref, cot_ref, send_ref, back_ref, slope_ref, sum_ref,
+):
+    own = place_ref[0]
+    mine = pl.multiple_of(own * HALF, HALF)
+    other = pl.multiple_of((1 - own) * HALF, HALF)
+    up_same, down_same = same_ref.at[:3], same_ref.at[3:]
+    up_cross, down_cross = cross_ref.at[:3], cross_ref.at[3:]
+    for layer in range(2):
+        x_ref[pl.ds(layer * NRZ + mine, HALF), :] = up_same[layer]
+        x_ref[pl.ds(layer * NRZ + other, HALF), :] = up_cross[layer]
+        x_ref[pl.ds((6 + layer) * NRZ + mine, HALF), :] = down_same[layer]
+        x_ref[pl.ds((6 + layer) * NRZ + other, HALF), :] = down_cross[layer]
+    x_ref[2 * NRZ : 6 * NRZ, :] = x_in[...]
+    cot_ref[NRZ : 5 * NRZ, :] = cot_in[...]
+    cot_ref[pl.ds(mine, HALF), :] = pick_half(up_same[2], own).astype(BF16)
+    cot_ref[pl.ds(other, HALF), :] = pick_half(up_cross[2], own).astype(BF16)
+    cot_ref[pl.ds(5 * NRZ + mine, HALF), :] = pick_half(down_same[2], own).astype(BF16)
+    cot_ref[pl.ds(5 * NRZ + other, HALF), :] = pick_half(down_cross[2], own).astype(BF16)
+
+    low = x_ref[: 2 * NRZ, :]
+    high = x_ref[6 * NRZ :, :]
+    middle = jnp.concatenate([x_ref[NRZ : 2 * NRZ, :], x_ref[6 * NRZ : 7 * NRZ, :]], axis=0)
+    edge = None
+    for s in range(3):
+        zero = dot_rows(low, forward_weights(w1_ref, s, 0))
+        one = dot_rows(middle, forward_weights(w1_ref, s, 1))
+        two = dot_rows(high, forward_weights(w1_ref, s, 2))
+        part = jnp.concatenate(
+            [zero[:NRZ] + one[:NRZ], zero[NRZ:], two[:NRZ], one[NRZ:] + two[NRZ:]], axis=0
+        )
+        part = fold_forward(part.reshape(4, NRZ, 3 * LANES), s)
+        edge = part if edge is None else edge + part
+    sum_ref[...] = pre_in[...]
+    sum_ref[: 2 * NRZ, :] += edge[: 2 * NRZ]
+    sum_ref[4 * NRZ :, :] += edge[2 * NRZ :]
+    pre = sum_ref[...]
+    sigma = jax.nn.sigmoid(pre)
+    send_ref[: (LAYERS + 2) * NRZ, :] = (pre * sigma).astype(BF16)
+    within = pre[NRZ : NRZ * (LAYERS + 1)]
+    sigma = sigma[NRZ : NRZ * (LAYERS + 1)]
+    slope_ref[...] = sigma * (1.0 + within * (1.0 - sigma))
+
+    first = cot_ref[:NRZ, :]
+    last = cot_ref[5 * NRZ :, :]
+    edge = None
+    for s in range(3):
+        summed = None
+        for q in range(3):
+            part = jnp.concatenate(
+                [
+                    jnp.dot(first, tap_slice(w2_ref, (6 + q) * 3 + s), preferred_element_type=F32),
+                    jnp.dot(last, tap_slice(w2_ref, q * 3 + s), preferred_element_type=F32),
+                ],
+                axis=0,
+            ).reshape(2, NRZ, CH)
+            if q != 1:
+                part = shift_radius(part, q - 1)
+            summed = part if summed is None else summed + part
+        summed = summed.reshape(2 * NRZ, CH)
+        if s != 1:
+            summed = roll_rows(summed, s - 1)
+        edge = summed if edge is None else edge + summed
+    rows = LAYERS * NRZ
+    total = jnp.concatenate(
+        [
+            back_in[:NRZ, :] + edge[:NRZ],
+            back_in[NRZ : rows - NRZ, :],
+            back_in[rows - NRZ :, :] + edge[NRZ:],
+        ],
+        axis=0,
+    )
     back_ref[...] = pick_half(total, own)
     send_ref[(LAYERS + 2) * NRZ :, :] = pick_half(total, 1 - own).astype(BF16)
 
 
-def fields(place, fc, swap, halos, w_first, w_second):
+def fields(place, own_parts, halos, w_first, w_second):
     rows = (LAYERS + 2) * NRZ
     return pl.pallas_call(
         fields_kernel,
@@ -283,9 +351,10 @@
         ],
         in_specs=[smem()] + [vmem()] * 8,
         out_specs=[vmem()] * 5,
+        scratch_shapes=[pltpu.VMEM((rows, LANES), F32)],
         compiler_params=params(),
-        cost_estimate=cost(2300000000, 6000000),
-    )(place, fc, swap, *halos, w_first, w_second)
+        cost_estimate=cost(1000000000, 6000000),
+    )(place, *own_parts, *halos, w_first, w_second)
 
 
 def grad_pieces(place_ref, source, field, factor, turned_ref, outs):
@@ -438,55 +507,83 @@
     )(place, mine, theirs)
 
 
-def write_kernel(
-    place_ref, m_ref, mx_ref, my_ref, first_ref, last_ref, after, out_ref, token_ref, block_ref, sems
+def write_half(far, place_ref, near_ref, across_refs, out_ref, block_ref, sems):
+    x_zero = jnp.broadcast_to(place_ref[1], (BLOCK, LANES)) == 0
+    copies = []
+    for dz in range(4):
+        for tap in range(TAPS):
+            rows = slice(tap * BLOCK, (tap + 1) * BLOCK)
+            near = near_ref[dz, rows, :].astype(F32)
+            if len(across_refs) == 1:
+                across = across_refs[0][dz, rows, :]
+            elif tap < FIRST_TAPS:
+                across = across_refs[0][dz, rows, :]
+            else:
+                late = slice((tap - FIRST_TAPS) * BLOCK, (tap - FIRST_TAPS + 1) * BLOCK)
+                across = across_refs[1][dz, late, :]
+            across = across.astype(F32)
+            lanes = slice(tap * CH, tap * CH + LANES)
+            block_ref[dz, :, lanes] = jnp.where(x_zero, near, across)
+            lanes = slice(tap * CH + LANES, (tap + 1) * CH)
+            block_ref[dz, :, lanes] = jnp.where(x_zero, across, near)
+        row = lax.rem(place_ref[2] + far, 2) * 4 + lax.rem(place_ref[3] + dz, 4)
+        copy = pltpu.make_async_copy(
+            block_ref.at[dz],
+            out_ref.at[pl.ds(pl.multiple_of(row * BLOCK, BLOCK), BLOCK), :],
+            sems.at[dz],
+        )
+        copy.start()
+        copies.append(copy)
+    for copy in copies:
+        copy.wait()
+
+
+def write_near_kernel(place_ref, m_ref, mx_ref, after, out_ref, token_ref, block_ref, sems):
+    token_ref[...] = jnp.zeros_like(token_ref)
+    write_half(0, place_ref, m_ref, [mx_ref], out_ref, block_ref, sems)
+
+
+def write_far_kernel(
+    place_ref, my_ref, first_ref, last_ref, half_ref, out_ref, token_ref, block_ref, sems
 ):
     token_ref[...] = jnp.zeros_like(token_ref)
-    x_zero = jnp.broadcast_to(place_ref[1], (BLOCK, LANES)) == 0
-    copies = []
-    for dy in range(2):
-        for dz in range(4):
-            index = dy * 4 + dz
-            for tap in range(TAPS):
-                rows = slice(tap * BLOCK, (tap + 1) * BLOCK)
-                if dy == 0:
-                    near, across = m_ref[dz, rows, :], mx_ref[dz, rows, :]
-                elif tap < FIRST_TAPS:
-                    near, across = my_ref[dz, rows, :], first_ref[dz, rows, :]
-                else:
-                    late = slice((tap - FIRST_TAPS) * BLOCK, (tap - FIRST_TAPS + 1) * BLOCK)
-                    near, across = my_ref[dz, rows, :], last_ref[dz, late, :]
-                near = near.astype(F32)
-                across = across.astype(F32)
-                block_ref[index, :, tap * CH : tap * CH + LANES] = jnp.where(x_zero, near, across)
-                block_ref[index, :, tap * CH + LANES : (tap + 1) * CH] = jnp.where(
-                    x_zero, across, near
-                )
-            row = lax.rem(place_ref[2] + dy, 2) * 4 + lax.rem(place_ref[3] + dz, 4)
-            copy = pltpu.make_async_copy(
-                block_ref.at[index],
-                out_ref.at[pl.ds(pl.multiple_of(row * BLOCK, BLOCK), BLOCK), :],
-                sems.at[index],
-            )
-            copy.start()
-            copies.append(copy)
-    for copy in copies:
-        copy.wait()
+    write_half(1, place_ref, my_ref, [first_ref, last_ref], out_ref, block_ref, sems)
+
+
+def write_shapes():
+    return {
+        "out_shape": [shape((LANES, TAPS * CH), F32), shape((8, LANES), F32)],
+        "out_specs": [in_hbm(), vmem()],
+        "scratch_shapes": [
+            pltpu.VMEM((4, BLOCK, TAPS * CH), F32),
+            pltpu.SemaphoreType.DMA((4,)),
+        ],
+        "compiler_params": params(),
+        "cost_estimate": cost(0, 3000000),
+    }
+
+
+def write_near(place, whole, across_x, after):
+    return pl.pallas_call(
+        write_near_kernel,
+        in_specs=[smem()] + [vmem()] * 2 + [anywhere()],
+        **write_shapes(),
+    )(place, whole, across_x, after)
+
+
+def write_far(place, across_y, first, last, half):
+    return pl.pallas_call(
+        write_far_kernel,
+        in_specs=[smem()] + [vmem()] * 3 + [in_hbm()],
+        input_output_aliases={4: 0},
+        **write_shapes(),
+    )(place, across_y, first, last, half)
 
 
 def write_out(place, pieces, after):
-    return pl.pallas_call(
-        write_kernel,
-        out_shape=[shape((LANES, TAPS * CH), F32), shape((8, LANES), F32)],
-        in_specs=[smem()] + [vmem()] * 5 + [anywhere()],
-        out_specs=[in_hbm(), vmem()],
-        scratch_shapes=[
-            pltpu.VMEM((8, BLOCK, TAPS * CH), F32),
-            pltpu.SemaphoreType.DMA((8,)),
-        ],
-        compiler_params=params(),
-        cost_estimate=cost(0, 6000000),
-    )(place, *pieces, after)
+    whole, across_x, across_y, first, last = pieces
+    half, _ = write_near(place, whole, across_x, after)
+    return write_far(place, across_y, first, last, half)
 
 
 def plus(*terms):
@@ -556,6 +653,11 @@
         two(ins[one_in:], outs[one_out:])
 
     return body
+
+
+def join_halos(ins, outs):
+    outs[0][:3] = ins[0][...]
+    outs[0][3:] = ins[1][...]
 
 
 def reduce_diagonal(x_both, y_both):
@@ -630,12 +732,13 @@
     swap = neighbour(fc, 0, 1)
     up = neighbour(to_next, 1, 0)
     down = neighbour(to_last, -1, 0)
-    w_one, w_two = load(w_first, w_second, to_last)
-    halos = [up, neighbour(up, 0, 1), down, neighbour(down, 0, 1)]
-    x, cot, send, back, slope = fields(place, fc, swap, halos, w_one, w_two)
+    own_parts = inner(place, fc, swap, w_first, w_second)
+    (halos,) = step_call(join_halos, [up, down], [(6, HALF, CH)], [own_parts[2]])
+    halos = [halos, neighbour(halos, 0, 1)]
+    x, cot, send, back, slope = fields(place, own_parts, halos, w_first, w_second)
     got = neighbour(send, 0, 1)
     hidden, second = second_grad(place, factor, cot, send, got)
-    mine, theirs = flow(place, x, hidden, w_two)
+    mine, theirs = flow(place, x, hidden, w_second)
     theirs = neighbour(theirs, 0, 1)
     if quad:
         corner = reduce_diagonal(*second[3:])
@@ -648,19 +751,19 @@
                 [mine],
             )
         )
+        flow_out, token = join_flow(place, mine, theirs)
         *rows, x_both, y_both = step_call(
             both(sum_quads, 5, 4, hand_on),
             [second[0], corner[0], sides[1], sides[0], corner[1], first[3], first[4]],
             [SINGLE] * 4 + [first[3].shape, first[4].shape],
+            [token],
         )
         corner_two = reduce_diagonal(x_both, y_both)
         rows = reduce_z(rows)
-        flow_out, token = join_flow(place, mine, theirs)
         own_one, *sides_two = step_call(
             both(sum_z, 4, 1, meet),
             [*rows, first[1], corner_two[0], first[2], corner_two[1]],
             [SINGLE, FIRST_PART, LAST_PART],
-            [token],
         )
         sides_two = reduce_sides(*sides_two)
         blocks = gather_z(own_one)
@@ -680,10 +783,10 @@
         blocks_two = gather_z(own_two)
         (whole_two,) = step_call(stack_z, blocks_two, [WHOLE], far)
         near_two = gather_sides(whole_two)
+        grad_second, token = write_out(place, (*near, *far), whole_two)
         far_two = gather_diagonal(
-            *step_call(cut_far, [near_two[1], near_two[2]], [FIRST_PART, LAST_PART])
+            *step_call(cut_far, [near_two[1], near_two[2]], [FIRST_PART, LAST_PART], [token])
         )
-        grad_second, token = write_out(place, (*near, *far), whole_two)
         grad_first, _ = write_out(place, (*near_two, *far_two), token)
     else:
         flow_out, _ = join_flow(place, mine, theirs)

time: 121 us -> 113 us (0.934)
  waiting for transfers between devices: 54.1 us -> 46.9 us
  starting transfers between devices: 41 us -> 38 us
  Pallas kernels: 19.7 us -> 22.3 us
    ppermute x28, waiting for transfers between devices: 52 us -> 44.1 us  [shifted(): return lax.ppermute(value, 'az', pairs)]
    pallas_call x3 -> x5, Pallas kernels: 7.51 us -> 12.2 us  [the longest x2 4.79 us: write_near(): pl.pallas_call(write_near_kernel, in_specs=[smem()] + [vmem()] * 2 + [any...]
    ppermute x28, starting transfers between devices: 32.8 us -> 30.5 us  [shifted(): return lax.ppermute(value, 'az', pairs)]
    pallas_call x1, Pallas kernels: 3.86 us -> 1.75 us  [fields(): pl.pallas_call(fields_kernel, out_shape=[shape(((LAYERS + 4) * NRZ, CH)),...]
    ppermute x7 -> x6, waiting for transfers between devices: 2.15 us -> 2.86 us  [neighbour(): return lax.ppermute(value, ('az', 'grp'), pairs)]
    ppermute x7 -> x6, starting transfers between devices: 8.15 us -> 7.5 us  [neighbour(): return lax.ppermute(value, ('az', 'grp'), pairs)]
    unnamed x8 -> x12, local copies, waits for them, and re-layouts: 4.75 us -> 4.76 us
  transfers between devices with their start and end apart: 35 -> 34, of which waited for: 18 -> 17; matrix products, arithmetic and copies ran while one was open for 0% -> 0% of each run, Pallas kernels for 8% -> 13%
where the time goes in v3:
time: 113 us
  waiting for transfers between devices  46.9 us (42%)
  starting transfers between devices  38 us (34%)
  Pallas kernels  22.3 us (20%)
  local copies, waits for them, and re-layouts  4.76 us (4%)
    ppermute x28, waiting for transfers between devices, shifted(): return lax.ppermute(value, 'az', pairs)  44.1 us
    ppermute x28, starting transfers between devices, shifted(): return lax.ppermute(value, 'az', pairs)  30.5 us
    ppermute x6, starting transfers between devices, neighbour(): return lax.ppermute(value, ('az', 'grp'), pairs)  7.5 us
    pallas_call x2, Pallas kernels, write_near(): pl.pallas_call(write_near_kernel, in_specs=[smem()] + [vmem()] * 2 + [any...  4.79 us
    unnamed x12, local copies, waits for them, and re-layouts  4.76 us
    pallas_call x2, Pallas kernels, write_far(): pl.pallas_call(write_far_kernel, in_specs=[smem()] + [vmem()] * 3 + [in_h...  4.2 us
    pallas_call x1, Pallas kernels, inner(): pl.pallas_call(inner_kernel, out_shape=[shape((LAYERS * NRZ, CH)), shape(...  3.19 us
    ppermute x6, waiting for transfers between devices, neighbour(): return lax.ppermute(value, ('az', 'grp'), pairs)  2.86 us
  transfers between devices with their start and end apart: 34, of which 17 were waited for; matrix products, arithmetic and copies ran while one was open for 0% of the time, Pallas kernels for 13%

profile of v3, /device:TPU:0, one launch (start us, length us, event | category | flops | bytes accessed | tf_op | source)
XLA Modules:
  0.0 112.9 jit_solution(363279515674743896)
XLA Ops:
  0.6 0.9 copy-done.4
  1.5 0.9 copy-done.5
  2.4 0.6 shard_map.67
  3.1 0.5 collective-permute-start
  3.6 2.6 %collective-permute-start.1 = (bf16[3,64,256]{2,1,0:T(8,128)(2,1)S(1)}, bf16[3,64,256]{2,1,0:T(8,128)(2,1)S(1)}, u32[]{:S(2)}, u32[]{:S(2)}) collective-permute-start(bf16[3,64,256]{2,1,0:T(8,128)(2,1)S(1)} %get-tuple-element.61), channel_id=1, source_target_pairs={{0,2},{1,3},{2,4},{3,5},{4,6},{5,7},{6,8},{7,9},{8,10},{9,11},{10,... | collective-permute-start | bytes 294920 | tf_op jit(solution)/shard_map/ppermute | solution.py:102
  6.1 4.1 %collective-permute-start.2 = (bf16[3,64,256]{2,1,0:T(8,128)(2,1)S(1)}, bf16[3,64,256]{2,1,0:T(8,128)(2,1)S(1)}, u32[]{:S(2)}, u32[]{:S(2)}) collective-permute-start(bf16[3,64,256]{2,1,0:T(8,128)(2,1)S(1)} %get-tuple-element.62), channel_id=1, source_target_pairs={{0,30},{1,31},{2,0},{3,1},{4,2},{5,3},{6,4},{7,5},{8,6},{9,7},{10,... | collective-permute-start | bytes 294920 | tf_op jit(solution)/shard_map/ppermute | solution.py:102
  10.3 1.5 %copy-done = bf16[128,6912]{1,0:T(8,128)(2,1)S(1)} copy-done((bf16[128,6912]{1,0:T(8,128)(2,1)S(1)}, bf16[128,6912]{1,0:T(8,128)(2,1)}, u32[]{:S(2)}) %copy-start) | copy-done | bytes 1769496
  11.8 1.5 %copy-done.2 = bf16[128,6912]{1,0:T(8,128)(2,1)S(1)} copy-done((bf16[128,6912]{1,0:T(8,128)(2,1)S(1)}, bf16[128,6912]{1,0:T(8,128)(2,1)}, u32[]{:S(2)}) %copy-start.2) | copy-done | bytes 1769496
  13.3 3.2 %shard_map.68 = (bf16[512,256]{1,0:T(8,128)(2,1)S(1)}, bf16[512,128]{1,0:T(8,128)(2,1)S(1)}, f32[768,128]{1,0:T(8,128)S(1)}, f32[512,256]{1,0:T(8,128)S(1)}) custom-call(s32[4]{0:T(128)S(1)} %pad_add_fusion.place_ref, bf16[8,64,256]{2,1,0:T(8,128)(2,1)S(1)} %get-tuple-element.56.fc_ref, bf16[8,64,256]{2,1,0:T(8,128)(2,1)S(1)} %collective-permute-done.swap_ref, ...), custom_call_target="tpu_custom_call" | custom-call | flops 2300000000 | bytes 6000000 | tf_op jit(solution)/shard_map/pallas_call | solution.py:248
  16.5 0.1 collective-permute-start.3
  16.6 1.4 %collective-permute-done.3.cross_ref = bf16[6,64,256]{2,1,0:T(8,128)(2,1)S(1)} collective-permute-done((bf16[6,64,256]{2,1,0:T(8,128)(2,1)S(1)}, bf16[6,64,256]{2,1,0:T(8,128)(2,1)S(1)}, u32[]{:S(2)}, u32[]{:S(2)}) %collective-permute-start.3) | collective-permute-done | bytes 196640 | tf_op jit(solution)/shard_map/ppermute | solution.py:102
  18.0 1.7 %shard_map.70 = (bf16[1024,256]{1,0:T(8,128)(2,1)S(1)}, bf16[768,128]{1,0:T(8,128)(2,1)S(1)}, bf16[1280,128]{1,0:T(8,128)(2,1)S(1)}, f32[512,128]{1,0:T(8,128)S(1)}, f32[512,128]{1,0:T(8,128)S(1)}) custom-call(s32[4]{0:T(128)S(1)} %pad_add_fusion.place_ref, bf16[512,256]{1,0:T(8,128)(2,1)S(1)} %get-tuple-element.57.x_in, ...), custom_call_target="tpu_custom_call" | custom-call | flops 1000000000 | bytes 6000000 | tf_op jit(solution)/shard_map/pallas_call | solution.py:343
  19.8 0.2 collective-permute-start.4
  20.0 1.5 %collective-permute-done.4.got_ref = bf16[1280,128]{1,0:T(8,128)(2,1)S(1)} collective-permute-done((bf16[1280,128]{1,0:T(8,128)(2,1)S(1)}, bf16[1280,128]{1,0:T(8,128)(2,1)S(1)}, u32[]{:S(2)}, u32[]{:S(2)}) %collective-permute-start.4) | collective-permute-done | bytes 327712 | tf_op jit(solution)/shard_map/ppermute | solution.py:102
  21.5 1.9 %shard_map.71 = (bf16[768,256]{1,0:T(8,128)(2,1)S(1)}, bf16[4,432,128]{2,1,0:T(8,128)(2,1)S(1)}, bf16[4,224,128]{2,1,0:T(8,128)(2,1)S(1)}, bf16[4,208,128]{2,1,0...) custom-call(s32[4]{0:T(128)S(1)} %pad_add_fusion.place_ref, ...), custom_call_target="tpu_custom_call" | custom-call | flops 1000000000 | bytes 3000000 | tf_op jit(solution)/shard_map/pallas_call | solution.py:445
  23.5 2.0 %shard_map.72 = (bf16[4,64,128]{2,1,0:T(8,128)(2,1)S(1)}, bf16[4,64,128]{2,1,0:T(8,128)(2,1)S(1)}) custom-call(s32[4]{0:T(128)S(1)} %pad_add_fusion.place_ref, bf16[1024,256]{1,0:T(8,128)(2,1)S(1)} %get-tuple-element.63.x_ref, bf16[768,256]{1,0:T(8,128)(2,1)S(1)} %get-tuple-element.66.h_ref, bf16[128,6912]{1,0:T(8,128)(2,1)S(1)} %copy-done.3), custom_call_target="tpu_custom_call" | custom-call | flops 1000000000 | bytes 3000000 | tf_op jit(solution)/shard_map/pallas_call | solution.py:480
  25.5 9.9 %collective-permute-done.7.refs_3_.refs_4_ = bf16[4,416,128]{2,1,0:T(8,128)(2,1)S(1)} collective-permute-done((bf16[4,416,128]{2,1,0:T(8,128)(2,1)S(1)}, bf16[4,416,128]{2,1,0:T(8,128)(2,1)S(1)}, u32[]{:S(2)}, u32[]{:S(2)}) %collective-permute-start.7) | collective-permute-done | bytes 426016 | tf_op jit(solution)/shard_map/ppermute | solution.py:82
  35.4 0.6 collective-permute-done.6.refs_1_
  36.2 1.3 %collective-permute-start.8 = (bf16[4,208,128]{2,1,0:T(8,128)(2,1)S(1)}, bf16[4,208,128]{2,1,0:T(8,128)(2,1)S(1)}, u32[]{:S(2)}, u32[]{:S(2)}) collective-permute-start(bf16[4,208,128]{2,1,0:T(8,128)(2,1)S(1)} %get-tuple-element.75), channel_id=1, source_target_pairs={{0,2},{2,0},{4,6},{6,4},{8,10},{10,8},{12,14},{14,12},{16,18},{18,... | collective-permute-start | bytes 638984 | tf_op jit(solution)/shard_map/ppermute | solution.py:82
  37.5 1.9 %shard_map.75 = (bf16[4,432,128]{2,1,0:T(8,128)(2,1)S(1)}, bf16[4,224,128]{2,1,0:T(8,128)(2,1)S(1)}, bf16[4,208,128]{2,1,0:T(8,128)(2,1)S(1)}, bf16[4,448,128]{2,1,0:T(8,128)(2,1)S(1)}, bf16[4,416,128]{2,1,0:T(8,128)(2,1)S(1)}) custom-call(s32[4]{0:T(128)S(1)} %pad_add_fusion.place_ref, f32[512,128]{1,0:T(8,128)S(1)} %get-tuple-element.77.back_ref, ...), custom_call_target="tpu_custom_call" | custom-call | flops 1000000000 | bytes 3000000 | tf_op jit(solution)/shard_map/pallas_call | solution.py:458
  39.4 1.2 %shard_map.73 = (bf16[4,64,256]{2,1,0:T(8,128)(2,1)}, f32[8,128]{1,0:T(8,128)S(1)}) custom-call(s32[4]{0:T(128)S(1)} %pad_add_fusion.place_ref, bf16[4,64,128]{2,1,0:T(8,128)(2,1)S(1)} %get-tuple-element.67.mine_ref.refs_4_.after, bf16[4,64,128]{2,1,0:T(8,128)(2,1)S(1)} %collective-permute-done.5.theirs_ref), custom_call_target="tpu_custom_call" | custom-call | bytes 400000 | tf_op jit(solution)/shard_map/pallas_call | solution.py:500
  40.6 2.1 %collective-permute-done.8.refs_2_ = bf16[4,208,128]{2,1,0:T(8,128)(2,1)S(1)} collective-permute-done((bf16[4,208,128]{2,1,0:T(8,128)(2,1)S(1)}, bf16[4,208,128]{2,1,0:T(8,128)(2,1)S(1)}, u32[]{:S(2)}, u32[]{:S(2)}) %collective-permute-start.8) | collective-permute-done | bytes 213024 | tf_op jit(solution)/shard_map/ppermute | solution.py:82
  42.7 0.3 collective-permute-done.9.refs_3_
  43.0 0.2 shard_map.76
  43.2 0.8 collective-permute-start.13
  44.0 1.4 %collective-permute-start.14 = (bf16[4,416,128]{2,1,0:T(8,128)(2,1)S(1)}, bf16[4,416,128]{2,1,0:T(8,128)(2,1)S(1)}, u32[]{:S(2)}, u32[]{:S(2)}) collective-permute-start(bf16[4,416,128]{2,1,0:T(8,128)(2,1)S(1)} %get-tuple-element.89), channel_id=1, source_target_pairs={{0,4},{2,6},{4,0},{6,2},{8,12},{10,14},{12,8},{14,10},{16,20},{18,... | collective-permute-start | bytes 1277960 | tf_op jit(solution)/shard_map/ppermute | solution.py:82
  45.4 2.4 %collective-permute-start.11 = (bf16[432,128]{1,0:T(8,128)(2,1)S(1)}, bf16[432,128]{1,0:T(8,128)(2,1)S(1)}, u32[]{:S(2)}, u32[]{:S(2)}) collective-permute-start(bf16[432,128]{1,0:T(8,128)(2,1)S(1)} %get-tuple-element.84), channel_id=1, source_target_pairs={{0,16},{2,18},{4,20},{6,22},{8,24},{10,26},{12,28},{14,30},{16,0},... | collective-permute-start | bytes 331784 | tf_op jit(solution)/shard_map/ppermute | solution.py:82
  47.8 1.4 %collective-permute-start.12 = (bf16[432,128]{1,0:T(8,128)(2,1)S(1)}, bf16[432,128]{1,0:T(8,128)(2,1)S(1)}, u32[]{:S(2)}, u32[]{:S(2)}) collective-permute-start(bf16[432,128]{1,0:T(8,128)(2,1)S(1)} %get-tuple-element.85), channel_id=1, source_target_pairs={{0,24},{2,26},{4,28},{6,30},{8,0},{10,2},{12,4},{14,6},{16,8},{18,... | collective-permute-start | bytes 331784 | tf_op jit(solution)/shard_map/ppermute | solution.py:82
  49.2 3.6 %collective-permute-done.10.refs_1_ = bf16[432,128]{1,0:T(8,128)(2,1)S(1)} collective-permute-done((bf16[432,128]{1,0:T(8,128)(2,1)S(1)}, bf16[432,128]{1,0:T(8,128)(2,1)S(1)}, u32[]{:S(2)}, u32[]{:S(2)}) %collective-permute-start.10) | collective-permute-done | bytes 110624 | tf_op jit(solution)/shard_map/ppermute | solution.py:82
  52.8 2.4 %collective-permute-done.11.refs_2_ = bf16[432,128]{1,0:T(8,128)(2,1)S(1)} collective-permute-done((bf16[432,128]{1,0:T(8,128)(2,1)S(1)}, bf16[432,128]{1,0:T(8,128)(2,1)S(1)}, u32[]{:S(2)}, u32[]{:S(2)}) %collective-permute-start.11) | collective-permute-done | bytes 110624 | tf_op jit(solution)/shard_map/ppermute | solution.py:82
  55.2 0.2 shard_map.77
  55.4 0.4 collective-permute-start.19
  55.8 1.2 %collective-permute-start.18 = (bf16[4,208,128]{2,1,0:T(8,128)(2,1)S(1)}, bf16[4,208,128]{2,1,0:T(8,128)(2,1)S(1)}, u32[]{:S(2)}, u32[]{:S(2)}) collective-permute-start(bf16[4,208,128]{2,1,0:T(8,128)(2,1)S(1)} %get-tuple-element.92), channel_id=1, source_target_pairs={{0,2},{2,0},{4,6},{6,4},{8,10},{10,8},{12,14},{14,12},{16,18},{18,... | collective-permute-start | bytes 638984 | tf_op jit(solution)/shard_map/ppermute | solution.py:82
  57.0 1.9 %collective-permute-start.17 = (bf16[432,128]{1,0:T(8,128)(2,1)S(1)}, bf16[432,128]{1,0:T(8,128)(2,1)S(1)}, u32[]{:S(2)}, u32[]{:S(2)}) collective-permute-start(bf16[432,128]{1,0:T(8,128)(2,1)S(1)} %get-tuple-element.90.refs_0_), channel_id=1, source_target_pairs={{0,8},{2,10},{4,12},{6,14},{8,16},{10,18},{12,20},{14,22},{16,24},... | collective-permute-start | bytes 331784 | tf_op jit(solution)/shard_map/ppermute | solution.py:82
  58.9 2.0 %collective-permute-start.16 = (bf16[432,128]{1,0:T(8,128)(2,1)S(1)}, bf16[432,128]{1,0:T(8,128)(2,1)S(1)}, u32[]{:S(2)}, u32[]{:S(2)}) collective-permute-start(bf16[432,128]{1,0:T(8,128)(2,1)S(1)} %get-tuple-element.90.refs_0_), channel_id=1, source_target_pairs={{0,16},{2,18},{4,20},{6,22},{8,24},{10,26},{12,28},{14,30},{16,0},... | collective-permute-start | bytes 331784 | tf_op jit(solution)/shard_map/ppermute | solution.py:82
  60.9 0.4 collective-permute-start.15
  61.2 3.0 %collective-permute-done.17.refs_3_ = bf16[432,128]{1,0:T(8,128)(2,1)S(1)} collective-permute-done((bf16[432,128]{1,0:T(8,128)(2,1)S(1)}, bf16[432,128]{1,0:T(8,128)(2,1)S(1)}, u32[]{:S(2)}, u32[]{:S(2)}) %collective-permute-start.17) | collective-permute-done | bytes 110624 | tf_op jit(solution)/shard_map/ppermute | solution.py:82
  64.2 3.3 %collective-permute-done.16.refs_2_ = bf16[432,128]{1,0:T(8,128)(2,1)S(1)} collective-permute-done((bf16[432,128]{1,0:T(8,128)(2,1)S(1)}, bf16[432,128]{1,0:T(8,128)(2,1)S(1)}, u32[]{:S(2)}, u32[]{:S(2)}) %collective-permute-start.16) | collective-permute-done | bytes 110624 | tf_op jit(solution)/shard_map/ppermute | solution.py:82
  67.5 0.2 shard_map.78
  67.7 1.5 %collective-permute-start.21 = (bf16[4,432,128]{2,1,0:T(8,128)(2,1)S(1)}, bf16[4,432,128]{2,1,0:T(8,128)(2,1)S(1)}, u32[]{:S(2)}, u32[]{:S(2)}) collective-permute-start(bf16[4,432,128]{2,1,0:T(8,128)(2,1)S(1)} %get-tuple-element.94.m_ref), channel_id=1, source_target_pairs={{0,4},{2,6},{4,0},{6,2},{8,12},{10,14},{12,8},{14,10},{16,20},{18,... | collective-permute-start | bytes 1327112 | tf_op jit(solution)/shard_map/ppermute | solution.py:82
  69.3 1.0 collective-permute-start.20
  70.2 1.7 %collective-permute-start.22 = (bf16[432,128]{1,0:T(8,128)(2,1)S(1)}, bf16[432,128]{1,0:T(8,128)(2,1)S(1)}, u32[]{:S(2)}, u32[]{:S(2)}) collective-permute-start(bf16[432,128]{1,0:T(8,128)(2,1)S(1)} %get-tuple-element.96), channel_id=1, source_target_pairs={{0,8},{2,10},{4,12},{6,14},{8,16},{10,18},{12,20},{14,22},{16,24},... | collective-permute-start | bytes 331784 | tf_op jit(solution)/shard_map/ppermute | solution.py:82
  72.0 1.5 %collective-permute-start.23 = (bf16[432,128]{1,0:T(8,128)(2,1)S(1)}, bf16[432,128]{1,0:T(8,128)(2,1)S(1)}, u32[]{:S(2)}, u32[]{:S(2)}) collective-permute-start(bf16[432,128]{1,0:T(8,128)(2,1)S(1)} %get-tuple-element.97), channel_id=1, source_target_pairs={{0,16},{2,18},{4,20},{6,22},{8,24},{10,26},{12,28},{14,30},{16,0},... | collective-permute-start | bytes 331784 | tf_op jit(solution)/shard_map/ppermute | solution.py:82
  73.5 0.9 collective-permute-start.24
  74.3 2.5 %collective-permute-done.22.refs_3_ = bf16[432,128]{1,0:T(8,128)(2,1)S(1)} collective-permute-done((bf16[432,128]{1,0:T(8,128)(2,1)S(1)}, bf16[432,128]{1,0:T(8,128)(2,1)S(1)}, u32[]{:S(2)}, u32[]{:S(2)}) %collective-permute-start.22) | collective-permute-done | bytes 110624 | tf_op jit(solution)/shard_map/ppermute | solution.py:82
  76.9 3.0 %collective-permute-done.23.refs_4_ = bf16[432,128]{1,0:T(8,128)(2,1)S(1)} collective-permute-done((bf16[432,128]{1,0:T(8,128)(2,1)S(1)}, bf16[432,128]{1,0:T(8,128)(2,1)S(1)}, u32[]{:S(2)}, u32[]{:S(2)}) %collective-permute-start.23) | collective-permute-done | bytes 110624 | tf_op jit(solution)/shard_map/ppermute | solution.py:82
  80.0 1.3 %collective-permute-start.28 = (bf16[4,224,128]{2,1,0:T(8,128)(2,1)S(1)}, bf16[4,224,128]{2,1,0:T(8,128)(2,1)S(1)}, u32[]{:S(2)}, u32[]{:S(2)}) collective-permute-start(bf16[4,224,128]{2,1,0:T(8,128)(2,1)S(1)} %get-tuple-element.100), channel_id=1, source_target_pairs={{0,4},{2,6},{4,0},{6,2},{8,12},{10,14},{12,8},{14,10},{16,20},{18,... | collective-permute-start | bytes 688136 | tf_op jit(solution)/shard_map/ppermute | solution.py:82
  81.3 0.5 collective-permute-start.29
  81.8 2.5 %collective-permute-start.27 = (bf16[432,128]{1,0:T(8,128)(2,1)S(1)}, bf16[432,128]{1,0:T(8,128)(2,1)S(1)}, u32[]{:S(2)}, u32[]{:S(2)}) collective-permute-start(bf16[432,128]{1,0:T(8,128)(2,1)S(1)} %get-tuple-element.99.refs_0_), channel_id=1, source_target_pairs={{0,8},{2,10},{4,12},{6,14},{8,16},{10,18},{12,20},{14,22},{16,24},... | collective-permute-start | bytes 331784 | tf_op jit(solution)/shard_map/ppermute | solution.py:82
  84.2 0.7 collective-permute-start.26
  85.0 1.6 %collective-permute-start.25 = (bf16[432,128]{1,0:T(8,128)(2,1)S(1)}, bf16[432,128]{1,0:T(8,128)(2,1)S(1)}, u32[]{:S(2)}, u32[]{:S(2)}) collective-permute-start(bf16[432,128]{1,0:T(8,128)(2,1)S(1)} %get-tuple-element.99.refs_0_), channel_id=1, source_target_pairs={{0,24},{2,26},{4,28},{6,30},{8,0},{10,2},{12,4},{14,6},{16,8},{18,... | collective-permute-start | bytes 331784 | tf_op jit(solution)/shard_map/ppermute | solution.py:82
  86.6 1.8 %collective-permute-done.27.refs_3_ = bf16[432,128]{1,0:T(8,128)(2,1)S(1)} collective-permute-done((bf16[432,128]{1,0:T(8,128)(2,1)S(1)}, bf16[432,128]{1,0:T(8,128)(2,1)S(1)}, u32[]{:S(2)}, u32[]{:S(2)}) %collective-permute-start.27) | collective-permute-done | bytes 110624 | tf_op jit(solution)/shard_map/ppermute | solution.py:82
  88.4 3.1 %collective-permute-done.26.refs_2_ = bf16[432,128]{1,0:T(8,128)(2,1)S(1)} collective-permute-done((bf16[432,128]{1,0:T(8,128)(2,1)S(1)}, bf16[432,128]{1,0:T(8,128)(2,1)S(1)}, u32[]{:S(2)}, u32[]{:S(2)}) %collective-permute-start.26) | collective-permute-done | bytes 110624 | tf_op jit(solution)/shard_map/ppermute | solution.py:82
  91.5 1.8 %collective-permute-start.31 = (bf16[4,432,128]{2,1,0:T(8,128)(2,1)S(1)}, bf16[4,432,128]{2,1,0:T(8,128)(2,1)S(1)}, u32[]{:S(2)}, u32[]{:S(2)}) collective-permute-start(bf16[4,432,128]{2,1,0:T(8,128)(2,1)S(1)} %shard_map.80.after.m_ref), channel_id=1, source_target_pairs={{0,2},{2,0},{4,6},{6,4},{8,10},{10,8},{12,14},{14,12},{16,18},{18,... | collective-permute-start | bytes 1327112 | tf_op jit(solution)/shard_map/ppermute | solution.py:82
  93.3 0.5 collective-permute-start.30
  93.8 2.4 %shard_map.81 = (f32[128,6912]{1,0:T(8,128)}, f32[8,128]{1,0:T(8,128)}) custom-call(s32[4]{0:T(128)S(1)} %pad_add_fusion.place_ref, bf16[4,432,128]{2,1,0:T(8,128)(2,1)S(1)} %get-tuple-element.94.m_ref, bf16[4,432,128]{2,1,0:T(8,128)(2,1)S(1)} %collective-permute-done.20.refs_0_.mx_ref, bf16[4,432,128]{2,1,0:T(8,128)(2,1)S(1)} %shard_map.80.after.m_ref), custom_call_target="tpu_custom_call" | custom-call | bytes 3000000 | tf_op jit(solution)/shard_map/pallas_call | solution.py:567
  96.2 1.8 %shard_map.82 = (f32[128,6912]{1,0:T(8,128)}, f32[8,128]{1,0:T(8,128)S(1)}) custom-call(s32[4]{0:T(128)S(1)} %pad_add_fusion.place_ref, bf16[4,432,128]{2,1,0:T(8,128)(2,1)S(1)} %collective-permute-done.21.refs_1_.my_ref, bf16[4,224,128]{2,1,0:T(8,128)(2,1)S(1)} %collective-permute-done.28.refs_4_.first_ref, ...), custom_call_target="tpu_custom_call", output_to_operand_aliasing={{0}: (4, {})} | custom-call | bytes 3000000 | tf_op jit(solution)/shard_map/pallas_call | solution.py:575
  98.1 3.4 %collective-permute-done.31.refs_0_.mx_ref = bf16[4,432,128]{2,1,0:T(8,128)(2,1)S(1)} collective-permute-done((bf16[4,432,128]{2,1,0:T(8,128)(2,1)S(1)}, bf16[4,432,128]{2,1,0:T(8,128)(2,1)S(1)}, u32[]{:S(2)}, u32[]{:S(2)}) %collective-permute-start.31) | collective-permute-done | bytes 442400 | tf_op jit(solution)/shard_map/ppermute | solution.py:82
  101.5 2.6 %collective-permute-done.30.refs_1_.my_ref = bf16[4,432,128]{2,1,0:T(8,128)(2,1)S(1)} collective-permute-done((bf16[4,432,128]{2,1,0:T(8,128)(2,1)S(1)}, bf16[4,432,128]{2,1,0:T(8,128)(2,1)S(1)}, u32[]{:S(2)}, u32[]{:S(2)}) %collective-permute-start.30) | collective-permute-done | bytes 442400 | tf_op jit(solution)/shard_map/ppermute | solution.py:82
  104.1 0.6 collective-permute-start.32
  104.7 1.0 collective-permute-start.33
  105.7 2.4 %shard_map.84 = (f32[128,6912]{1,0:T(8,128)}, f32[8,128]{1,0:T(8,128)}) custom-call(s32[4]{0:T(128)S(1)} %pad_add_fusion.place_ref, bf16[4,432,128]{2,1,0:T(8,128)(2,1)S(1)} %shard_map.80.after.m_ref, bf16[4,432,128]{2,1,0:T(8,128)(2,1)S(1)} %collective-permute-done.31.refs_0_.mx_ref, f32[8,128]{1,0:T(8,128)S(1)} %get-tuple-element.103.refs_2_.after), custom_call_target="tpu_custom_call" | custom-call | bytes 3000000 | tf_op jit(solution)/shard_map/pallas_call | solution.py:567
  108.1 2.4 %collective-permute-done.33.last_ref = bf16[4,208,128]{2,1,0:T(8,128)(2,1)S(1)} collective-permute-done((bf16[4,208,128]{2,1,0:T(8,128)(2,1)S(1)}, bf16[4,208,128]{2,1,0:T(8,128)(2,1)S(1)}, u32[]{:S(2)}, u32[]{:S(2)}) %collective-permute-start.33) | collective-permute-done | bytes 213024 | tf_op jit(solution)/shard_map/ppermute | solution.py:82
  110.5 2.4 %shard_map.85 = (f32[128,6912]{1,0:T(8,128)}, f32[8,128]{1,0:T(8,128)}) custom-call(s32[4]{0:T(128)S(1)} %pad_add_fusion.place_ref, bf16[4,432,128]{2,1,0:T(8,128)(2,1)S(1)} %collective-permute-done.30.refs_1_.my_ref, bf16[4,224,128]{2,1,0:T(8,128)(2,1)S(1)} %collective-permute-done.32.first_ref, ...), custom_call_target="tpu_custom_call", output_to_operand_aliasing={{0}: (4, {})} | custom-call | bytes 3000000 | tf_op jit(solution)/shard_map/pallas_call | solution.py:575
  (36 shorter events, 0.6 us)
Async XLA Ops:
  0.6 0.9 copy-start.4
  1.5 0.9 copy-start.5
  3.1 7.2 %collective-permute-start = (bf16[8,64,256]{2,1,0:T(8,128)(2,1)S(1)}, bf16[8,64,256]{2,1,0:T(8,128)(2,1)S(1)}, u32[]{:S(2)}, u32[]{:S(2)}) collective-permute-start(bf16[8,64,256]{2,1,0:T(8,128)(2,1)S(1)} %get-tuple-element.56.fc_ref), channel_id=1, source_target_pairs={{0,1},{1,0},{2,3},{3,2},{4,5},{5,4},{6,7},{7,6},{8,9},{9,8},{10,11... | collective-permute-start | bytes 786440 | tf_op jit(solution)/shard_map/ppermute | solution.py:102
  3.6 12.9 %collective-permute-start.1 = (bf16[3,64,256]{2,1,0:T(8,128)(2,1)S(1)}, bf16[3,64,256]{2,1,0:T(8,128)(2,1)S(1)}, u32[]{:S(2)}, u32[]{:S(2)}) collective-permute-start(bf16[3,64,256]{2,1,0:T(8,128)(2,1)S(1)} %get-tuple-element.61), channel_id=1, source_target_pairs={{0,2},{1,3},{2,4},{3,5},{4,6},{5,7},{6,8},{7,9},{8,10},{9,11},{10,... | collective-permute-start | bytes 294920 | tf_op jit(solution)/shard_map/ppermute | solution.py:102
  6.1 10.3 %collective-permute-start.2 = (bf16[3,64,256]{2,1,0:T(8,128)(2,1)S(1)}, bf16[3,64,256]{2,1,0:T(8,128)(2,1)S(1)}, u32[]{:S(2)}, u32[]{:S(2)}) collective-permute-start(bf16[3,64,256]{2,1,0:T(8,128)(2,1)S(1)} %get-tuple-element.62), channel_id=1, source_target_pairs={{0,30},{1,31},{2,0},{3,1},{4,2},{5,3},{6,4},{7,5},{8,6},{9,7},{10,... | collective-permute-start | bytes 294920 | tf_op jit(solution)/shard_map/ppermute | solution.py:102
  10.3 1.5 %copy-start = (bf16[128,6912]{1,0:T(8,128)(2,1)S(1)}, bf16[128,6912]{1,0:T(8,128)(2,1)}, u32[]{:S(2)}) copy-start(bf16[128,6912]{1,0:T(8,128)(2,1)} %w1_ref.3) | copy-start | bytes 5308420
  11.8 1.5 %copy-start.2 = (bf16[128,6912]{1,0:T(8,128)(2,1)S(1)}, bf16[128,6912]{1,0:T(8,128)(2,1)}, u32[]{:S(2)}) copy-start(bf16[128,6912]{1,0:T(8,128)(2,1)} %w2_ref.5) | copy-start | bytes 5308420
  13.3 4.8 %copy-start.1 = (bf16[128,6912]{1,0:T(8,128)(2,1)S(1)}, bf16[128,6912]{1,0:T(8,128)(2,1)}, u32[]{:S(2)}) copy-start(bf16[128,6912]{1,0:T(8,128)(2,1)} %w1_ref.3) | copy-start | bytes 5308420
  13.3 4.8 %copy-start.3 = (bf16[128,6912]{1,0:T(8,128)(2,1)S(1)}, bf16[128,6912]{1,0:T(8,128)(2,1)}, u32[]{:S(2)}) copy-start(bf16[128,6912]{1,0:T(8,128)(2,1)} %w2_ref.5) | copy-start | bytes 5308420
  16.5 1.5 %collective-permute-start.3 = (bf16[6,64,256]{2,1,0:T(8,128)(2,1)S(1)}, bf16[6,64,256]{2,1,0:T(8,128)(2,1)S(1)}, u32[]{:S(2)}, u32[]{:S(2)}) collective-permute-start(bf16[6,64,256]{2,1,0:T(8,128)(2,1)S(1)} %shard_map.69.same_ref), channel_id=1, source_target_pairs={{0,1},{1,0},{2,3},{3,2},{4,5},{5,4},{6,7},{7,6},{8,9},{9,8},{10,11... | collective-permute-start | bytes 589832 | tf_op jit(solution)/shard_map/ppermute | solution.py:102
  19.8 1.7 %collective-permute-start.4 = (bf16[1280,128]{1,0:T(8,128)(2,1)S(1)}, bf16[1280,128]{1,0:T(8,128)(2,1)S(1)}, u32[]{:S(2)}, u32[]{:S(2)}) collective-permute-start(bf16[1280,128]{1,0:T(8,128)(2,1)S(1)} %get-tuple-element.65.send_ref), channel_id=1, source_target_pairs={{0,1},{1,0},{2,3},{3,2},{4,5},{5,4},{6,7},{7,6},{8,9},{9,8},{10,11... | collective-permute-start | bytes 983048 | tf_op jit(solution)/shard_map/ppermute | solution.py:102
  23.4 12.6 %collective-permute-start.6 = (bf16[4,448,128]{2,1,0:T(8,128)(2,1)S(1)}, bf16[4,448,128]{2,1,0:T(8,128)(2,1)S(1)}, u32[]{:S(2)}, u32[]{:S(2)}) collective-permute-start(bf16[4,448,128]{2,1,0:T(8,128)(2,1)S(1)} %get-tuple-element.71), channel_id=1, source_target_pairs={{0,2},{2,0},{4,6},{6,4},{8,10},{10,8},{12,14},{14,12},{16,18},{18,... | collective-permute-start | bytes 1376264 | tf_op jit(solution)/shard_map/ppermute | solution.py:82
  23.4 11.9 %collective-permute-start.7 = (bf16[4,416,128]{2,1,0:T(8,128)(2,1)S(1)}, bf16[4,416,128]{2,1,0:T(8,128)(2,1)S(1)}, u32[]{:S(2)}, u32[]{:S(2)}) collective-permute-start(bf16[4,416,128]{2,1,0:T(8,128)(2,1)S(1)} %get-tuple-element.74), channel_id=1, source_target_pairs={{0,4},{2,6},{4,0},{6,2},{8,12},{10,14},{12,8},{14,10},{16,20},{18,... | collective-permute-start | bytes 1277960 | tf_op jit(solution)/shard_map/ppermute | solution.py:82
  36.1 6.9 %collective-permute-start.9 = (bf16[4,224,128]{2,1,0:T(8,128)(2,1)S(1)}, bf16[4,224,128]{2,1,0:T(8,128)(2,1)S(1)}, u32[]{:S(2)}, u32[]{:S(2)}) collective-permute-start(bf16[4,224,128]{2,1,0:T(8,128)(2,1)S(1)} %get-tuple-element.76), channel_id=1, source_target_pairs={{0,4},{2,6},{4,0},{6,2},{8,12},{10,14},{12,8},{14,10},{16,20},{18,... | collective-permute-start | bytes 688136 | tf_op jit(solution)/shard_map/ppermute | solution.py:82
  36.2 6.5 %collective-permute-start.8 = (bf16[4,208,128]{2,1,0:T(8,128)(2,1)S(1)}, bf16[4,208,128]{2,1,0:T(8,128)(2,1)S(1)}, u32[]{:S(2)}, u32[]{:S(2)}) collective-permute-start(bf16[4,208,128]{2,1,0:T(8,128)(2,1)S(1)} %get-tuple-element.75), channel_id=1, source_target_pairs={{0,2},{2,0},{4,6},{6,4},{8,10},{10,8},{12,14},{14,12},{16,18},{18,... | collective-permute-start | bytes 638984 | tf_op jit(solution)/shard_map/ppermute | solution.py:82
  37.5 1.9 %collective-permute-start.5 = (bf16[4,64,128]{2,1,0:T(8,128)(2,1)S(1)}, bf16[4,64,128]{2,1,0:T(8,128)(2,1)S(1)}, u32[]{:S(2)}, u32[]{:S(2)}) collective-permute-start(bf16[4,64,128]{2,1,0:T(8,128)(2,1)S(1)} %get-tuple-element.68), channel_id=1, source_target_pairs={{0,1},{1,0},{2,3},{3,2},{4,5},{5,4},{6,7},{7,6},{8,9},{9,8},{10,11... | collective-permute-start | bytes 196616 | tf_op jit(solution)/shard_map/ppermute | solution.py:102
  43.2 12.1 %collective-permute-start.13 = (bf16[4,448,128]{2,1,0:T(8,128)(2,1)S(1)}, bf16[4,448,128]{2,1,0:T(8,128)(2,1)S(1)}, u32[]{:S(2)}, u32[]{:S(2)}) collective-permute-start(bf16[4,448,128]{2,1,0:T(8,128)(2,1)S(1)} %get-tuple-element.87), channel_id=1, source_target_pairs={{0,2},{2,0},{4,6},{6,4},{8,10},{10,8},{12,14},{14,12},{16,18},{18,... | collective-permute-start | bytes 1376264 | tf_op jit(solution)/shard_map/ppermute | solution.py:82
  44.0 11.3 %collective-permute-start.14 = (bf16[4,416,128]{2,1,0:T(8,128)(2,1)S(1)}, bf16[4,416,128]{2,1,0:T(8,128)(2,1)S(1)}, u32[]{:S(2)}, u32[]{:S(2)}) collective-permute-start(bf16[4,416,128]{2,1,0:T(8,128)(2,1)S(1)} %get-tuple-element.89), channel_id=1, source_target_pairs={{0,4},{2,6},{4,0},{6,2},{8,12},{10,14},{12,8},{14,10},{16,20},{18,... | collective-permute-start | bytes 1277960 | tf_op jit(solution)/shard_map/ppermute | solution.py:82
  45.4 7.4 %collective-permute-start.10 = (bf16[432,128]{1,0:T(8,128)(2,1)S(1)}, bf16[432,128]{1,0:T(8,128)(2,1)S(1)}, u32[]{:S(2)}, u32[]{:S(2)}) collective-permute-start(bf16[432,128]{1,0:T(8,128)(2,1)S(1)} %get-tuple-element.83), channel_id=1, source_target_pairs={{0,8},{2,10},{4,12},{6,14},{8,16},{10,18},{12,20},{14,22},{16,24},... | collective-permute-start | bytes 331784 | tf_op jit(solution)/shard_map/ppermute | solution.py:82
  45.4 9.9 %collective-permute-start.11 = (bf16[432,128]{1,0:T(8,128)(2,1)S(1)}, bf16[432,128]{1,0:T(8,128)(2,1)S(1)}, u32[]{:S(2)}, u32[]{:S(2)}) collective-permute-start(bf16[432,128]{1,0:T(8,128)(2,1)S(1)} %get-tuple-element.84), channel_id=1, source_target_pairs={{0,16},{2,18},{4,20},{6,22},{8,24},{10,26},{12,28},{14,30},{16,0},... | collective-permute-start | bytes 331784 | tf_op jit(solution)/shard_map/ppermute | solution.py:82
  47.8 7.4 %collective-permute-start.12 = (bf16[432,128]{1,0:T(8,128)(2,1)S(1)}, bf16[432,128]{1,0:T(8,128)(2,1)S(1)}, u32[]{:S(2)}, u32[]{:S(2)}) collective-permute-start(bf16[432,128]{1,0:T(8,128)(2,1)S(1)} %get-tuple-element.85), channel_id=1, source_target_pairs={{0,24},{2,26},{4,28},{6,30},{8,0},{10,2},{12,4},{14,6},{16,8},{18,... | collective-permute-start | bytes 331784 | tf_op jit(solution)/shard_map/ppermute | solution.py:82
  55.4 12.1 %collective-permute-start.19 = (bf16[4,224,128]{2,1,0:T(8,128)(2,1)S(1)}, bf16[4,224,128]{2,1,0:T(8,128)(2,1)S(1)}, u32[]{:S(2)}, u32[]{:S(2)}) collective-permute-start(bf16[4,224,128]{2,1,0:T(8,128)(2,1)S(1)} %get-tuple-element.93), channel_id=1, source_target_pairs={{0,4},{2,6},{4,0},{6,2},{8,12},{10,14},{12,8},{14,10},{16,20},{18,... | collective-permute-start | bytes 688136 | tf_op jit(solution)/shard_map/ppermute | solution.py:82
  55.8 11.7 %collective-permute-start.18 = (bf16[4,208,128]{2,1,0:T(8,128)(2,1)S(1)}, bf16[4,208,128]{2,1,0:T(8,128)(2,1)S(1)}, u32[]{:S(2)}, u32[]{:S(2)}) collective-permute-start(bf16[4,208,128]{2,1,0:T(8,128)(2,1)S(1)} %get-tuple-element.92), channel_id=1, source_target_pairs={{0,2},{2,0},{4,6},{6,4},{8,10},{10,8},{12,14},{14,12},{16,18},{18,... | collective-permute-start | bytes 638984 | tf_op jit(solution)/shard_map/ppermute | solution.py:82
  57.0 7.2 %collective-permute-start.17 = (bf16[432,128]{1,0:T(8,128)(2,1)S(1)}, bf16[432,128]{1,0:T(8,128)(2,1)S(1)}, u32[]{:S(2)}, u32[]{:S(2)}) collective-permute-start(bf16[432,128]{1,0:T(8,128)(2,1)S(1)} %get-tuple-element.90.refs_0_), channel_id=1, source_target_pairs={{0,8},{2,10},{4,12},{6,14},{8,16},{10,18},{12,20},{14,22},{16,24},... | collective-permute-start | bytes 331784 | tf_op jit(solution)/shard_map/ppermute | solution.py:82
  58.9 8.6 %collective-permute-start.16 = (bf16[432,128]{1,0:T(8,128)(2,1)S(1)}, bf16[432,128]{1,0:T(8,128)(2,1)S(1)}, u32[]{:S(2)}, u32[]{:S(2)}) collective-permute-start(bf16[432,128]{1,0:T(8,128)(2,1)S(1)} %get-tuple-element.90.refs_0_), channel_id=1, source_target_pairs={{0,16},{2,18},{4,20},{6,22},{8,24},{10,26},{12,28},{14,30},{16,0},... | collective-permute-start | bytes 331784 | tf_op jit(solution)/shard_map/ppermute | solution.py:82
  60.9 6.7 %collective-permute-start.15 = (bf16[432,128]{1,0:T(8,128)(2,1)S(1)}, bf16[432,128]{1,0:T(8,128)(2,1)S(1)}, u32[]{:S(2)}, u32[]{:S(2)}) collective-permute-start(bf16[432,128]{1,0:T(8,128)(2,1)S(1)} %get-tuple-element.90.refs_0_), channel_id=1, source_target_pairs={{0,24},{2,26},{4,28},{6,30},{8,0},{10,2},{12,4},{14,6},{16,8},{18,... | collective-permute-start | bytes 331784 | tf_op jit(solution)/shard_map/ppermute | solution.py:82
  67.7 12.2 %collective-permute-start.21 = (bf16[4,432,128]{2,1,0:T(8,128)(2,1)S(1)}, bf16[4,432,128]{2,1,0:T(8,128)(2,1)S(1)}, u32[]{:S(2)}, u32[]{:S(2)}) collective-permute-start(bf16[4,432,128]{2,1,0:T(8,128)(2,1)S(1)} %get-tuple-element.94.m_ref), channel_id=1, source_target_pairs={{0,4},{2,6},{4,0},{6,2},{8,12},{10,14},{12,8},{14,10},{16,20},{18,... | collective-permute-start | bytes 1327112 | tf_op jit(solution)/shard_map/ppermute | solution.py:82
  69.3 10.7 %collective-permute-start.20 = (bf16[4,432,128]{2,1,0:T(8,128)(2,1)S(1)}, bf16[4,432,128]{2,1,0:T(8,128)(2,1)S(1)}, u32[]{:S(2)}, u32[]{:S(2)}) collective-permute-start(bf16[4,432,128]{2,1,0:T(8,128)(2,1)S(1)} %get-tuple-element.94.m_ref), channel_id=1, source_target_pairs={{0,2},{2,0},{4,6},{6,4},{8,10},{10,8},{12,14},{14,12},{16,18},{18,... | collective-permute-start | bytes 1327112 | tf_op jit(solution)/shard_map/ppermute | solution.py:82
  70.2 6.6 %collective-permute-start.22 = (bf16[432,128]{1,0:T(8,128)(2,1)S(1)}, bf16[432,128]{1,0:T(8,128)(2,1)S(1)}, u32[]{:S(2)}, u32[]{:S(2)}) collective-permute-start(bf16[432,128]{1,0:T(8,128)(2,1)S(1)} %get-tuple-element.96), channel_id=1, source_target_pairs={{0,8},{2,10},{4,12},{6,14},{8,16},{10,18},{12,20},{14,22},{16,24},... | collective-permute-start | bytes 331784 | tf_op jit(solution)/shard_map/ppermute | solution.py:82
  72.0 7.9 %collective-permute-start.23 = (bf16[432,128]{1,0:T(8,128)(2,1)S(1)}, bf16[432,128]{1,0:T(8,128)(2,1)S(1)}, u32[]{:S(2)}, u32[]{:S(2)}) collective-permute-start(bf16[432,128]{1,0:T(8,128)(2,1)S(1)} %get-tuple-element.97), channel_id=1, source_target_pairs={{0,16},{2,18},{4,20},{6,22},{8,24},{10,26},{12,28},{14,30},{16,0},... | collective-permute-start | bytes 331784 | tf_op jit(solution)/shard_map/ppermute | solution.py:82
  73.5 6.5 %collective-permute-start.24 = (bf16[432,128]{1,0:T(8,128)(2,1)S(1)}, bf16[432,128]{1,0:T(8,128)(2,1)S(1)}, u32[]{:S(2)}, u32[]{:S(2)}) collective-permute-start(bf16[432,128]{1,0:T(8,128)(2,1)S(1)} %get-tuple-element.98), channel_id=1, source_target_pairs={{0,24},{2,26},{4,28},{6,30},{8,0},{10,2},{12,4},{14,6},{16,8},{18,... | collective-permute-start | bytes 331784 | tf_op jit(solution)/shard_map/ppermute | solution.py:82
  80.0 11.5 %collective-permute-start.28 = (bf16[4,224,128]{2,1,0:T(8,128)(2,1)S(1)}, bf16[4,224,128]{2,1,0:T(8,128)(2,1)S(1)}, u32[]{:S(2)}, u32[]{:S(2)}) collective-permute-start(bf16[4,224,128]{2,1,0:T(8,128)(2,1)S(1)} %get-tuple-element.100), channel_id=1, source_target_pairs={{0,4},{2,6},{4,0},{6,2},{8,12},{10,14},{12,8},{14,10},{16,20},{18,... | collective-permute-start | bytes 688136 | tf_op jit(solution)/shard_map/ppermute | solution.py:82
  81.3 10.2 %collective-permute-start.29 = (bf16[4,208,128]{2,1,0:T(8,128)(2,1)S(1)}, bf16[4,208,128]{2,1,0:T(8,128)(2,1)S(1)}, u32[]{:S(2)}, u32[]{:S(2)}) collective-permute-start(bf16[4,208,128]{2,1,0:T(8,128)(2,1)S(1)} %get-tuple-element.101), channel_id=1, source_target_pairs={{0,2},{2,0},{4,6},{6,4},{8,10},{10,8},{12,14},{14,12},{16,18},{18,... | collective-permute-start | bytes 638984 | tf_op jit(solution)/shard_map/ppermute | solution.py:82
  81.8 6.6 %collective-permute-start.27 = (bf16[432,128]{1,0:T(8,128)(2,1)S(1)}, bf16[432,128]{1,0:T(8,128)(2,1)S(1)}, u32[]{:S(2)}, u32[]{:S(2)}) collective-permute-start(bf16[432,128]{1,0:T(8,128)(2,1)S(1)} %get-tuple-element.99.refs_0_), channel_id=1, source_target_pairs={{0,8},{2,10},{4,12},{6,14},{8,16},{10,18},{12,20},{14,22},{16,24},... | collective-permute-start | bytes 331784 | tf_op jit(solution)/shard_map/ppermute | solution.py:82
  84.2 7.2 %collective-permute-start.26 = (bf16[432,128]{1,0:T(8,128)(2,1)S(1)}, bf16[432,128]{1,0:T(8,128)(2,1)S(1)}, u32[]{:S(2)}, u32[]{:S(2)}) collective-permute-start(bf16[432,128]{1,0:T(8,128)(2,1)S(1)} %get-tuple-element.99.refs_0_), channel_id=1, source_target_pairs={{0,16},{2,18},{4,20},{6,22},{8,24},{10,26},{12,28},{14,30},{16,0},... | collective-permute-start | bytes 331784 | tf_op jit(solution)/shard_map/ppermute | solution.py:82
  85.0 6.5 %collective-permute-start.25 = (bf16[432,128]{1,0:T(8,128)(2,1)S(1)}, bf16[432,128]{1,0:T(8,128)(2,1)S(1)}, u32[]{:S(2)}, u32[]{:S(2)}) collective-permute-start(bf16[432,128]{1,0:T(8,128)(2,1)S(1)} %get-tuple-element.99.refs_0_), channel_id=1, source_target_pairs={{0,24},{2,26},{4,28},{6,30},{8,0},{10,2},{12,4},{14,6},{16,8},{18,... | collective-permute-start | bytes 331784 | tf_op jit(solution)/shard_map/ppermute | solution.py:82
  91.5 9.9 %collective-permute-start.31 = (bf16[4,432,128]{2,1,0:T(8,128)(2,1)S(1)}, bf16[4,432,128]{2,1,0:T(8,128)(2,1)S(1)}, u32[]{:S(2)}, u32[]{:S(2)}) collective-permute-start(bf16[4,432,128]{2,1,0:T(8,128)(2,1)S(1)} %shard_map.80.after.m_ref), channel_id=1, source_target_pairs={{0,2},{2,0},{4,6},{6,4},{8,10},{10,8},{12,14},{14,12},{16,18},{18,... | collective-permute-start | bytes 1327112 | tf_op jit(solution)/shard_map/ppermute | solution.py:82
  93.3 10.8 %collective-permute-start.30 = (bf16[4,432,128]{2,1,0:T(8,128)(2,1)S(1)}, bf16[4,432,128]{2,1,0:T(8,128)(2,1)S(1)}, u32[]{:S(2)}, u32[]{:S(2)}) collective-permute-start(bf16[4,432,128]{2,1,0:T(8,128)(2,1)S(1)} %shard_map.80.after.m_ref), channel_id=1, source_target_pairs={{0,4},{2,6},{4,0},{6,2},{8,12},{10,14},{12,8},{14,10},{16,20},{18,... | collective-permute-start | bytes 1327112 | tf_op jit(solution)/shard_map/ppermute | solution.py:82
  104.1 6.4 %collective-permute-start.32 = (bf16[4,224,128]{2,1,0:T(8,128)(2,1)S(1)}, bf16[4,224,128]{2,1,0:T(8,128)(2,1)S(1)}, u32[]{:S(2)}, u32[]{:S(2)}) collective-permute-start(bf16[4,224,128]{2,1,0:T(8,128)(2,1)S(1)} %get-tuple-element.104), channel_id=1, source_target_pairs={{0,4},{2,6},{4,0},{6,2},{8,12},{10,14},{12,8},{14,10},{16,20},{18,... | collective-permute-start | bytes 688136 | tf_op jit(solution)/shard_map/ppermute | solution.py:82
  104.7 5.8 %collective-permute-start.33 = (bf16[4,208,128]{2,1,0:T(8,128)(2,1)S(1)}, bf16[4,208,128]{2,1,0:T(8,128)(2,1)S(1)}, u32[]{:S(2)}, u32[]{:S(2)}) collective-permute-start(bf16[4,208,128]{2,1,0:T(8,128)(2,1)S(1)} %get-tuple-element.105), channel_id=1, source_target_pairs={{0,2},{2,0},{4,6},{6,4},{8,10},{10,8},{12,14},{14,12},{16,18},{18,... | collective-permute-start | bytes 638984 | tf_op jit(solution)/shard_map/ppermute | solution.py:82
